TPU v7x, 32 devices: a whole 2x2x4 slice. The times are simulated.
32 devices in a mesh: grp: 2 (over y), loc: 2 (over x), dp: 8 (over z, core).
Axes of the slice: x: 2, y: 2, z: 4, core: 2. Of those that a mesh axis runs over, the one named last changes fastest.
Arguments:
- out_grad: bfloat16 [8, 256, 7168], P('dp', ('grp', 'loc')), may hold values from -6 to 6
- slot_token: int32 [8, 4, 2, 5], P('dp', ('grp', 'loc')), may hold values from 0 to 63, as said below
- slot_count: int32 [8, 4, 2], P('dp', ('grp', 'loc')), may hold values from 1 to 5, as said below
- slot_weight: bfloat16 [8, 4, 2, 5], P('dp', ('grp', 'loc')), may hold values from 0.049804688 to 0.59765625
- up_weight: bfloat16 [2, 7168, 512], P('grp', None, 'loc'), may hold values from -0.0625 to 0.0625
- down_weight: bfloat16 [2, 512, 7168], P('grp', 'loc'), may hold values from -0.25 to 0.25
- hidden_saved: bfloat16 [8, 2, 20, 512], P('dp', 'grp', None, 'loc'), may hold values from -6 to 6
- gate_saved: bfloat16 [8, 2, 20, 512], P('dp', 'grp', None, 'loc'), may hold values from -6 to 6
Outputs:
- input_grad: bfloat16 [8, 256, 7168], P('dp', ('grp', 'loc'))
- down_grad: float32 [2, 512, 7168], P('grp', ('loc', 'dp'))
Inputs may be any that keep to these rules, and one draw needn't show every extreme that they name: `slot_token`: within one replica, source device and expert the first slot_count slots name different tokens; later entries are arbitrary tokens of the range. `slot_count`: every source device fills all 5 slots of some expert, and in every replica some expert has all 5 slots filled from every source device.
All inputs are finite; a program needn't handle non-finite values.
Results may differ from a plain program's by a relative error of at most 0.012.
Values may be sent and summed in bfloat16 or wider, within the bound.
No kernel may reach another device: no remote copies, remote signals or barrier semaphores. Data moves between devices by JAX's collectives and lax.ppermute only.
A program may use at most 64 MiB of HBM per device.

v0:
```python
import jax
import jax.numpy as jnp
from jax import lax
from jax.sharding import PartitionSpec as P


def local(
    out_grad, slot_token, slot_count, slot_weight, up_weight, down_weight, hidden_saved, gate_saved
):
    group_count = lax.axis_size("grp")
    local_count = lax.axis_size("loc")
    replicas = lax.axis_size("dp")
    grad_rows = out_grad[0]
    tok_dev = grad_rows.shape[0]
    model_dim = grad_rows.shape[1]
    tokens = slot_token[0, 0]
    capacity = tokens.shape[1]
    live_mask = jnp.arange(capacity, dtype=jnp.int32)[None, :] < slot_count[0, 0][:, None]
    picked = jnp.take(grad_rows, tokens.reshape(-1), axis=0).reshape(
        group_count, capacity, model_dim
    )
    outgoing = jnp.where(live_mask[:, :, None], picked, jnp.zeros((), jnp.bfloat16))
    weights = slot_weight[0, 0]
    arrived, arrived_weights = (
        lax.all_to_all(outgoing, "grp", split_axis=0, concat_axis=0, tiled=True),
        lax.all_to_all(weights, "grp", split_axis=0, concat_axis=0, tiled=True),
    )
    rows_all, weights_all = (
        lax.all_gather(arrived[:, None], "loc", axis=1, tiled=True),
        lax.all_gather(arrived_weights[:, None], "loc", axis=1, tiled=True),
    )
    slot_total = group_count * local_count * capacity
    slot_rows = rows_all.reshape(slot_total, model_dim)
    slot_scale = weights_all.reshape(slot_total).astype(jnp.float32)[:, None]
    hidden = hidden_saved[0, 0]
    gate_act = gate_saved[0, 0]
    w_down = down_weight[0]
    w_up = up_weight[0]
    grad_act = lax.dot_general(
        slot_rows, w_down, (((1,), (1,)), ((), ())), preferred_element_type=jnp.float32
    )
    grad_up = (slot_scale * grad_act * gate_act.astype(jnp.float32)).astype(jnp.bfloat16)
    partial_value = lax.dot_general(
        grad_up, w_up, (((1,), (1,)), ((), ())), preferred_element_type=jnp.float32
    )
    partial_value = partial_value.astype(jnp.bfloat16)
    weighted = (slot_scale * hidden.astype(jnp.float32)).astype(jnp.bfloat16)
    product = lax.dot_general(
        weighted, slot_rows, (((0,), (0,)), ((), ())), preferred_element_type=jnp.float32
    )
    rounded = lax.optimization_barrier(product.astype(jnp.bfloat16))
    summed = lax.psum_scatter(
        rounded.astype(jnp.float32).astype(jnp.bfloat16), "dp", scatter_dimension=0, tiled=True
    ).astype(jnp.float32)
    down_grad = (summed / replicas)[None]
    term_rows = lax.optimization_barrier(partial_value).astype(jnp.float32)
    term_rows = term_rows.reshape(group_count, local_count, capacity, model_dim)
    summed_rows = lax.psum_scatter(
        term_rows.astype(jnp.bfloat16), "loc", scatter_dimension=1, tiled=True
    )
    returned = lax.all_to_all(summed_rows, "grp", split_axis=0, concat_axis=0, tiled=True)
    contribs = returned.reshape(group_count * capacity, model_dim)
    matches = jnp.arange(tok_dev, dtype=jnp.int32)[:, None] == tokens.reshape(-1)[None, :]
    onehot = (matches & live_mask.reshape(-1)[None, :]).astype(jnp.bfloat16)
    input_grad = jnp.dot(onehot, contribs, preferred_element_type=jnp.float32).astype(jnp.bfloat16)[
        None
    ]
    return (input_grad, down_grad)


def solution(mesh):
    return jax.shard_map(
        local,
        mesh=mesh,
        in_specs=(
            P("dp", ("grp", "loc"), None),
            P("dp", ("grp", "loc"), None, None),
            P("dp", ("grp", "loc"), None),
            P("dp", ("grp", "loc"), None, None),
            P("grp", None, "loc"),
            P("grp", "loc", None),
            P("dp", "grp", None, "loc"),
            P("dp", "grp", None, "loc"),
        ),
        out_specs=(P("dp", ("grp", "loc"), None), P("grp", ("loc", "dp"), None)),
        check_vma=False,
    )
```

profile of v0, /device:TPU:0, one launch (start us, length us, event | category | flops | bytes accessed | tf_op | source)
XLA Modules:
  0.0 99.1 jit_solution(3321650456488516974)
XLA Ops:
  8.0 0.0 copy-start
  8.0 0.0 copy-start.1
  8.0 1.3 %copy.19 = bf16[2,1,5]{2,1,0:T(2,128)(2,1)} copy(bf16[2,1,5]{2,0,1:T(2,128)(2,1)} %bitcast.40) | data formatting | bytes 40 | tf_op jit(solution)/shard_map/all_to_all | solution.py:26
  9.3 4.2 %all-to-all-start = ((bf16[2,1,5]{2,1,0:T(2,128)(2,1)}), bf16[2,1,5]{2,1,0:T(2,128)(2,1)S(1)}, u32[]{:S(2)}, u32[]{:S(2)}) async-start(bf16[2,1,5]{2,1,0:T(2,128)(2,1)} %copy.19), calls=%async_computation | async-start | bytes 2048 | tf_op jit(solution)/shard_map/all_to_all | solution.py:26
  13.6 0.8 reshape_squeeze.3
  14.3 0.8 compare_and_fusion
  15.1 0.0 copy-done
  15.1 0.6 gather_fusion
  15.7 0.1 gather.7
  15.8 0.8 select_select_fusion
  16.6 0.6 all-to-all-done
  17.2 3.4 %all-to-all-start.1 = ((bf16[2,5,7168]{2,1,0:T(8,128)(2,1)}), bf16[2,5,7168]{2,1,0:T(8,128)(2,1)S(1)}, u32[]{:S(2)}, u32[]{:S(2)}) async-start(bf16[2,5,7168]{2,1,0:T(8,128)(2,1)} %select_select_fusion), calls=%async_computation.1 | async-start | bytes 458752 | tf_op jit(solution)/shard_map/all_to_all | solution.py:25
  20.7 0.0 all-reduce.3.cloned.1.call-start
  20.7 4.2 %all_gather.6 = bf16[2,2,5]{2,0,1:T(2,128)(2,1)S(1)} all-gather(bf16[2,1,5]{2,0,1:T(2,128)(2,1)S(1)} %copy.20), channel_id=1, replica_groups=mesh['grp'=2,'loc'=2,'dp'=8] {'loc'}, dimensions={1}, use_global_device_ids=true | all-gather | bytes 60 | tf_op jit(solution)/shard_map/all_gather | solution.py:30
  25.0 0.1 reshape.116
  25.0 0.6 all-to-all-done.1
  25.7 0.2 copy.22
  25.8 5.8 %all-gather = bf16[2,10,7168]{2,0,1:T(2,128)(2,1)S(1)} all-gather(bf16[2,5,7168]{2,0,1:T(2,128)(2,1)S(1)} %copy.22), channel_id=2, replica_groups=mesh['grp'=2,'loc'=2,'dp'=8] {'loc'}, dimensions={1}, use_global_device_ids=true | all-gather | bytes 430080 | tf_op jit(solution)/shard_map/all_gather | solution.py:29
  31.6 0.1 copy.23
  31.7 0.1 reshape.114
  31.8 0.0 copy-done.1
  31.8 0.0 copy-start.2
  31.8 7.1 %convolution_convert_fusion.2 = bf16[20,7168]{1,0:T(8,128)(2,1)S(1)} fusion(bf16[1,7168,256]{2,1,0:T(8,128)(2,1)} %param.12, bf16[20,7168]{1,0:T(8,128)(2,1)S(1)} %reshape.114, bf16[1,256,7168]{2,1,0:T(8,128)(2,1)} %param.13, bf16[1,1,20,256]{3,2,1,0:T(8,128)(2,1)S(1)} %copy-done.1, f32[20]{0:T(128)S(1)} %reshape.116), kind=kOutput, calls=%fused_computation.4 | convolution fusion | flops 146964480 | bytes 7923792 | tf_op jit(solution)/shard_map/dot_general | solution.py:43
  38.9 0.1 convert_element_type.55
  39.1 1.0 %copy.24 = bf16[2,2,5,7168]{3,0,2,1:T(2,128)(2,1)} copy(bf16[2,2,5,7168]{3,2,1,0:T(8,128)(2,1)S(1)} %convert_element_type.55) | data formatting | bytes 573440 | tf_op jit(solution)/shard_map/convert_element_type | solution.py:59
  40.1 0.0 all-reduce.3.cloned.1.call-update
  40.1 0.0 copy-start.4
  40.1 0.0 copy-start.3
  40.1 0.0 reduce-scatter.2.cloned.1.call-start
  40.2 0.0 copy-done.2
  40.2 3.0 %convolution_convert_fusion = bf16[256,7168]{1,0:T(8,128)(2,1)} fusion(bf16[20,7168]{1,0:T(8,128)(2,1)S(1)} %reshape.114, bf16[1,1,20,256]{3,2,1,0:T(8,128)(2,1)S(1)} %copy-done.2, f32[20]{0:T(128)S(1)} %reshape.116), kind=kOutput, calls=%fused_computation.1 | convolution fusion | flops 75250688 | bytes 3967056 | tf_op jit(solution)/shard_map/dot_general | solution.py:48
  43.2 0.0 reduce-scatter.2.cloned.1.call-update
  43.2 0.0 copy-done.4
  43.3 0.6 dynamic-slice
  43.8 21.5 %all-reduce.3.cloned.1.call-done = bf16[2,2,5,7168]{3,0,2,1:T(2,128)(2,1)} async-done(((bf16[2,2,5,7168]{3,0,2,1:T(2,128)(2,1)}), bf16[2,2,5,7168]{3,0,2,1:T(2,128)(2,1)}) %all-reduce.3.cloned.1.call-update) | async-done | bytes 286736
  65.3 1.7 %constant_dynamic-slice_fusion = bf16[2,1,5,7168]{3,0,2,1:T(2,128)(2,1)S(1)} fusion(bf16[2,2,5,7168]{3,0,2,1:T(2,128)(2,1)} %all-reduce.3.cloned.1.call-done, u32[]{:T(128)} %bitcast.12), kind=kLoop, calls=%fused_computation.29 | loop fusion | bytes 286724
  67.0 0.7 copy.25
  67.7 3.4 %all-to-all-start.2 = ((bf16[2,1,5,7168]{3,2,1,0:T(8,128)(2,1)}), bf16[2,1,5,7168]{3,2,1,0:T(8,128)(2,1)S(1)}, u32[]{:S(2)}, u32[]{:S(2)}) async-start(bf16[2,1,5,7168]{3,2,1,0:T(8,128)(2,1)} %copy.25), calls=%async_computation.2 | async-start | bytes 458752 | tf_op jit(solution)/shard_map/all_to_all | solution.py:61
  71.1 0.0 copy-done.3
  71.1 0.1 eq.18
  71.2 0.1 lt.46
  71.3 4.8 %all-to-all-done.2 = bf16[2,1,5,7168]{3,2,1,0:T(8,128)(2,1)S(1)} async-done(((bf16[2,1,5,7168]{3,2,1,0:T(8,128)(2,1)}), bf16[2,1,5,7168]{3,2,1,0:T(8,128)(2,1)S(1)}, u32[]{:S(2)}, u32[]{:S(2)}) %all-to-all-start.2) | async-done | bytes 143392 | tf_op jit(solution)/shard_map/all_to_all | solution.py:61
  76.1 0.1 reshape.115
  76.2 1.3 %fusion = bf16[1,64,7168]{2,1,0:T(8,128)(2,1)} fusion(bf16[10,7168]{1,0:T(8,128)(2,1)S(1)} %reshape.115, s32[10]{0:T(128)S(1)} %eq.18, pred[10]{0:T(512)(128)(4,1)S(1)} %lt.46), kind=kOutput, calls=%fused_computation.3 | convolution fusion | flops 9635072 | bytes 1060914 | tf_op jit(solution)/shard_map/dot_general | solution.py:65
  77.5 12.2 %reduce-scatter.2.cloned.1.call-done = bf16[32,7168]{1,0:T(8,128)(2,1)} async-done(((bf16[256,7168]{1,0:T(8,128)(2,1)}), bf16[32,7168]{1,0:T(8,128)(2,1)}) %reduce-scatter.2.cloned.1.call-update) | async-done | bytes 458768 | tf_op jit(solution)/shard_map/reduce_scatter | solution.py:52
  89.7 2.0 %multiply_bitcast_fusion = f32[1,32,7168]{2,1,0:T(8,128)} fusion(bf16[32,7168]{1,0:T(8,128)(2,1)} %reduce-scatter.2.cloned.1.call-done), kind=kLoop, calls=%fused_computation.11 | loop fusion | flops 458752 | bytes 1376256 | tf_op jit(solution)/shard_map/broadcast_in_dim | solution.py:55
  (4 shorter events, 0.0 us)
Async XLA Ops:
  8.0 7.1 %copy-start = (bf16[1,64,7168]{2,1,0:T(8,128)(2,1)S(1)}, bf16[1,64,7168]{2,1,0:T(8,128)(2,1)}, u32[]{:S(2)}) copy-start(bf16[1,64,7168]{2,1,0:T(8,128)(2,1)} %param.8) | copy-start | bytes 2752516
  8.0 23.8 %copy-start.1 = (bf16[1,1,20,256]{3,2,1,0:T(8,128)(2,1)S(1)}, bf16[1,1,20,256]{3,2,1,0:T(8,128)(2,1)}, u32[]{:S(2)}) copy-start(bf16[1,1,20,256]{3,2,1,0:T(8,128)(2,1)} %param.15) | copy-start | bytes 30724
  9.3 7.9 %all-to-all-start = ((bf16[2,1,5]{2,1,0:T(2,128)(2,1)}), bf16[2,1,5]{2,1,0:T(2,128)(2,1)S(1)}, u32[]{:S(2)}, u32[]{:S(2)}) async-start(bf16[2,1,5]{2,1,0:T(2,128)(2,1)} %copy.19), calls=%async_computation | async-start | bytes 2048 | tf_op jit(solution)/shard_map/all_to_all | solution.py:26
  17.2 8.4 %all-to-all-start.1 = ((bf16[2,5,7168]{2,1,0:T(8,128)(2,1)}), bf16[2,5,7168]{2,1,0:T(8,128)(2,1)S(1)}, u32[]{:S(2)}, u32[]{:S(2)}) async-start(bf16[2,5,7168]{2,1,0:T(8,128)(2,1)} %select_select_fusion), calls=%async_computation.1 | async-start | bytes 458752 | tf_op jit(solution)/shard_map/all_to_all | solution.py:25
  20.7 44.6 %all-reduce.3.cloned.1.call-start = ((), (), s32[]{:S(2)}) async-start(), calls=%async_computation.5 | async-start | bytes 573440
  31.8 8.4 %copy-start.2 = (bf16[1,1,20,256]{3,2,1,0:T(8,128)(2,1)S(1)}, bf16[1,1,20,256]{3,2,1,0:T(8,128)(2,1)}, u32[]{:S(2)}) copy-start(bf16[1,1,20,256]{3,2,1,0:T(8,128)(2,1)} %param.14) | copy-start | bytes 30724
  40.1 3.1 %copy-start.4 = (u32[32]{0:T(128)S(1)}, u32[32]{0:T(128)}, u32[]{:S(2)}) copy-start(u32[32]{0:T(128)} %constant.31) | copy-start | bytes 388
  40.1 31.0 %copy-start.3 = (s32[1,1,2,5]{3,2,1,0:T(2,128)S(1)}, s32[1,1,2,5]{3,2,1,0:T(2,128)}, u32[]{:S(2)}) copy-start(s32[1,1,2,5]{3,2,1,0:T(2,128)} %param.9) | copy-start | bytes 124
  40.1 49.5 %reduce-scatter.2.cloned.1.call-start = ((), (), s32[]{:S(2)}) async-start(), calls=%async_computation.4 | async-start | bytes 4128768 | tf_op jit(solution)/shard_map/reduce_scatter | solution.py:52
  67.7 8.4 %all-to-all-start.2 = ((bf16[2,1,5,7168]{3,2,1,0:T(8,128)(2,1)}), bf16[2,1,5,7168]{3,2,1,0:T(8,128)(2,1)S(1)}, u32[]{:S(2)}, u32[]{:S(2)}) async-start(bf16[2,1,5,7168]{3,2,1,0:T(8,128)(2,1)} %copy.25), calls=%async_computation.2 | async-start | bytes 458752 | tf_op jit(solution)/shard_map/all_to_all | solution.py:61
Sparse Core Ops, SparseCore 0:
  40.2 25.0 all-reduce.2
Sparse Core Ops, SparseCore 1:
  43.3 46.3 reduce-scatter.1
where the time goes:
time: 99.5 us; the launch traced here: 99.1 us
  waiting for transfers between devices  39.7 us (40%)
  between operations  15.6 us (16%)
  matrix products  11.4 us (11%)
  starting transfers between devices  11.2 us (11%)
  blocking collectives  9.99 us (10%)
  local copies, waits for them, and re-layouts  7.58 us (8%)
  other arithmetic  3.55 us (4%)
    unnamed x3, waiting for transfers between devices  21.5 us
    reduce_scatter x1, waiting for transfers between devices, local(): lax.psum_scatter(rounded.astype(jnp.float32).astype(jnp.bfloat16), 'dp',...  12.2 us
    dot_general x1, matrix products, local(): lax.dot_general(grad_up, w_up, (((1,), (1,)), ((), ())), preferred_elemen...  7.11 us
    all_gather x1, blocking collectives, local(): lax.all_gather(arrived[:, None], 'loc', axis=1, tiled=True)  5.78 us
    all_to_all x1, waiting for transfers between devices, local(): lax.all_to_all(summed_rows, 'grp', split_axis=0, concat_axis=0, tiled=True)  4.81 us
    all_to_all x1, starting transfers between devices, local(): lax.all_to_all(weights, 'grp', split_axis=0, concat_axis=0, tiled=True)  4.23 us
    all_gather x1, blocking collectives, local(): lax.all_gather(arrived_weights[:, None], 'loc', axis=1, tiled=True)  4.22 us
    all_to_all x1, starting transfers between devices, local(): lax.all_to_all(summed_rows, 'grp', split_axis=0, concat_axis=0, tiled=True)  3.44 us
  transfers between devices with their start and end apart: 5, of which 5 were waited for; matrix products, arithmetic and copies ran while one was open for 11% of the time, Pallas kernels for 0%

commit v1 on v0

--- a/solution.py
+++ b/solution.py
@@ -1,10 +1,19 @@
+import functools
+
 import jax
 import jax.numpy as jnp
 from jax import lax
+from jax.experimental import pallas as pl
+from jax.experimental.pallas import tpu as pltpu
 from jax.sharding import PartitionSpec as P
 
-
-def local(
+AXES = ("grp", "loc", "dp")
+PIECES = 8
+F32 = jnp.float32
+BF16 = jnp.bfloat16
+
+
+def local_collectives(
     out_grad, slot_token, slot_count, slot_weight, up_weight, down_weight, hidden_saved, gate_saved
 ):
     group_count = lax.axis_size("grp")
@@ -66,6 +75,310 @@
         None
     ]
     return (input_grad, down_grad)
+
+
+def iota(shape, dim):
+    return lax.broadcasted_iota(jnp.int32, shape, dim)
+
+
+def quotient(value, cap, most):
+    shift = 16
+    factor = (1 << shift) // cap + 1
+    assert all((v * factor) >> shift == v // cap for v in range(most))
+    return lax.shift_right_logical(value * factor, shift)
+
+
+def dot(a, b):
+    return jnp.dot(a, b, preferred_element_type=F32)
+
+
+def dot_nt(a, b):
+    return lax.dot_general(a, b, (((1,), (1,)), ((), ())), preferred_element_type=F32)
+
+
+def hot(condition):
+    return jnp.where(condition, 1.0, 0.0).astype(BF16)
+
+
+def place():
+    group, loc, dp = (lax.axis_index(axis) for axis in AXES)
+    z = dp // 2
+    return group, loc, z % 2, z // 2, dp % 2
+
+
+def select_kernel(tok, cnt, weight, rows, hidden, near, far):
+    cap = tok.shape[3]
+    group, _, _, _, _ = place()
+    tokens, model = rows.shape[1], rows.shape[2]
+    piece_cols = model // PIECES
+    count = PIECES * cap
+    scale = weight[0, 0].astype(F32)
+    row, token = iota((count, tokens), 0), iota((count, tokens), 1)
+    piece = quotient(row, cap, count)
+    slot = row - cap * piece
+    for other, out in ((0, near), (1, far)):
+        expert = jnp.where(group == other, 0, 1)
+        live = cnt[0, 0, expert]
+        value = jnp.zeros((count, tokens), F32)
+        for s in range(cap):
+            name = jnp.where(s < live, tok[0, 0, expert, s], -1)
+            factor = jnp.where(
+                expert == 0, scale[0:1, s : s + 1], scale[1:2, s : s + 1]
+            )
+            value = jnp.where((slot == s) & (token == name), factor, value)
+        total = jnp.zeros((count, piece_cols), F32)
+        for j in range(PIECES):
+            chosen = jnp.where(piece == j, value, 0.0).astype(BF16)
+            total += dot(chosen, rows[0, :, j * piece_cols : (j + 1) * piece_cols])
+        out[:, :piece_cols] = total.astype(BF16)
+    half = hidden.shape[3] // 2
+    slots = hidden.shape[2]
+    r, c = iota((count, slots), 0), iota((count, slots), 1)
+    folded = dot(hot(r == c), hidden[0, 0, :, :half]) + dot(
+        hot(r == c + slots), hidden[0, 0, :, half:]
+    )
+    near[:, piece_cols:] = folded.astype(BF16)
+
+
+def spread_kernel(own, from_x, from_y, from_xy, keep, to_1, to_2, to_3):
+    count, piece_cols = from_y.shape
+    cap = count // PIECES
+    slots = 4 * cap
+    group, loc, zb, pair, _ = place()
+    source = 2 * group + loc
+    m, n = iota((2 * count, count), 0), iota((2 * count, count), 1)
+    mq, nq = quotient(m, cap, 2 * count), quotient(n, cap, count)
+    m_slot, n_slot = m - cap * mq, n - cap * nq
+    m_flip, m_source, m_part = mq >> 3, (mq >> 1) & 3, mq & 1
+    wanted = 4 * loc + 2 * (zb ^ m_flip) + m_part
+    rows_ok = (m_slot == n_slot) & (nq == wanted)
+    total = jnp.zeros((2 * count, piece_cols), F32)
+    for k, ref in enumerate((own, from_x, from_y, from_xy)):
+        total += dot(hot(rows_ok & (m_source == (source ^ k))), ref[:, :piece_cols])
+    m_loc, m_row = (mq >> 2) & 1, m - slots * (mq >> 2)
+    n_half, n_row = nq >> 2, n - slots * (nq >> 2)
+    hidden_ok = (m_row == n_row) & (n_half == (pair ^ m_flip))
+    hidden = dot(hot(hidden_ok & (m_loc == loc)), own[:, piece_cols:]) + dot(
+        hot(hidden_ok & (m_loc != loc)), from_x[:, piece_cols:]
+    )
+    total, hidden = total.astype(BF16), hidden.astype(BF16)
+    for ref, flip_zb, flip_pair in ((keep, 0, 0), (to_1, 1, 0), (to_2, 0, 1), (to_3, 1, 1)):
+        ref[:, :piece_cols] = total[flip_zb * count : (flip_zb + 1) * count]
+        ref[:, piece_cols:] = hidden[flip_pair * count : (flip_pair + 1) * count]
+
+
+def expert_kernel(
+    own, from_x, from_y, from_xy, down, gate, up, ret_own, ret_x, ret_y, ret_xy, stack
+):
+    count, piece_cols = from_y.shape
+    cap = count // PIECES
+    pad = stack.shape[0] // PIECES
+    slots = gate.shape[2]
+    group, loc, _, _, _ = place()
+    source = 2 * group + loc
+    m, n = iota((PIECES * pad, count), 0), iota((PIECES * pad, count), 1)
+    nq = quotient(n, cap, count)
+    n_slot = n - cap * nq
+    m_piece, m_slot = m // pad, m % pad
+    total = jnp.zeros((PIECES * pad, piece_cols), F32)
+    for k, ref in enumerate((own, from_x, from_y, from_xy)):
+        match = (m_piece == nq) & (m_slot == (source ^ k) * cap + n_slot)
+        total += dot(hot(match), ref[:, :piece_cols])
+    slot_rows = total.astype(BF16)
+    grad_act = jnp.zeros((pad, down.shape[1]), F32)
+    for j in range(PIECES):
+        grad_act += dot_nt(
+            slot_rows[j * pad : (j + 1) * pad], down[0, :, j * piece_cols : (j + 1) * piece_cols]
+        )
+    gate_pad = dot(hot(iota((pad, slots), 0) == iota((pad, slots), 1)), gate[0, 0])
+    grad_up = (grad_act * gate_pad).astype(BF16)
+    for j in range(PIECES):
+        part = dot_nt(grad_up, up[0, j * piece_cols : (j + 1) * piece_cols, :])
+        stack[j * pad : (j + 1) * pad, :] = part.astype(BF16)
+    n, m = iota((count, PIECES * pad), 0), iota((count, PIECES * pad), 1)
+    nq = quotient(n, cap, count)
+    n_slot = n - cap * nq
+    m_piece, m_slot = m // pad, m % pad
+    for k, ref in enumerate((ret_own, ret_x, ret_y, ret_xy)):
+        match = (m_piece == nq) & (m_slot == (source ^ k) * cap + n_slot)
+        ref[...] = dot(hot(match), stack[...]).astype(BF16)
+
+
+def combine_kernel(tok, cnt, own, from_x, from_y, from_xy, out):
+    count, piece_cols = own.shape
+    cap = tok.shape[3]
+    tokens = out.shape[1]
+    group, _, _, _, _ = place()
+    m, n = iota((tokens, count), 0), iota((tokens, count), 1)
+    nq = quotient(n, cap, count)
+    n_slot = n - cap * nq
+    pairs = []
+    for other, (a, b) in enumerate(((own, from_x), (from_y, from_xy))):
+        contrib = (a[...].astype(F32) + b[...].astype(F32)).astype(BF16)
+        expert = jnp.where(group == other, 0, 1)
+        live = cnt[0, 0, expert]
+        match = jnp.zeros((tokens, count), F32)
+        for s in range(cap):
+            name = jnp.where(s < live, tok[0, 0, expert, s], -1)
+            match = jnp.where((n_slot == s) & (m == name), 1.0, match)
+        pairs.append((match, contrib))
+    for j in range(PIECES):
+        total = jnp.zeros((tokens, piece_cols), F32)
+        for match, contrib in pairs:
+            total += dot(jnp.where(nq == j, match, 0.0).astype(BF16), contrib)
+        out[0, :, j * piece_cols : (j + 1) * piece_cols] = total.astype(BF16)
+
+
+def product_kernel(scale, own, from_1, from_2, from_3, keep, send):
+    count = own.shape[0]
+    cap = count // PIECES
+    slots = 4 * cap
+    half = own.shape[1] - keep.shape[1] // 2
+    piece_cols = own.shape[1] - half
+    _, _, _, _, core = place()
+    refs = (own, from_1, from_2, from_3)
+    rows = jnp.concatenate([ref[:, :piece_cols].astype(F32) for ref in refs], 0).astype(BF16)
+    m, n = iota((4 * count, count), 0), iota((4 * count, count), 1)
+    mq = quotient(m, cap, 4 * count)
+    m_slot = m - cap * mq
+    m_part, m_loc, m_source, m_has = mq >> 4, (mq >> 3) & 1, (mq >> 1) & 3, mq & 1
+    nq = quotient(n, cap, count)
+    n_loc, n_row = nq >> 2, n - slots * (nq >> 2)
+    ok = (m_has == m_part) & (m_loc == n_loc) & (m_source * cap + m_slot == n_row)
+    place_rows = jnp.where(ok, scale, 0.0).astype(BF16)
+    spread = [dot(place_rows, ref[:, piece_cols:]) for ref in refs]
+    rows_dev = half // 4
+    for part in range(2):
+        for loc in range(2):
+            at = (2 * part + loc) * count
+            hidden = jnp.concatenate([value[at : at + count] for value in spread], 0)
+            product = dot(hidden.T.astype(BF16), rows)
+            for zb in range(2):
+                base = zb * 2 * rows_dev
+                first = product[base : base + rows_dev]
+                second = product[base + rows_dev : base + 2 * rows_dev]
+                block = slice((2 * loc + zb) * rows_dev, (2 * loc + zb + 1) * rows_dev)
+                cols = slice(part * piece_cols, (part + 1) * piece_cols)
+                keep[block, cols] = jnp.where(core == 0, first, second).astype(BF16)
+                send[block, cols] = jnp.where(core == 0, second, first).astype(BF16)
+
+
+def add_kernel(mine, other, own, to_x, to_z, to_xz):
+    rows_dev = own.shape[0]
+    _, loc, zb, _, _ = place()
+    for k, out in enumerate((own, to_z, to_x, to_xz)):
+        at = pl.ds(pl.multiple_of(((2 * loc + zb) ^ k) * rows_dev, rows_dev), rows_dev)
+        out[...] = (mine[at, :].astype(F32) + other[at, :].astype(F32)).astype(BF16)
+
+
+def join_kernel(own, from_x, from_z, from_xz, out):
+    cols = own.shape[1]
+    _, loc, zb, _, _ = place()
+    for k, ref in enumerate((own, from_z, from_x, from_xz)):
+        at = pl.ds(pl.multiple_of(((2 * loc + zb) ^ k) * cols, cols), cols)
+        out[0, :, at] = ref[...].astype(F32)
+
+
+VM = pl.BlockSpec(memory_space=pltpu.VMEM)
+SM = pl.BlockSpec(memory_space=pltpu.SMEM)
+
+
+def call(kernel, outs, args, specs=None, scratch=(), flops=0, nbytes=0):
+    out_shape = tuple(jax.ShapeDtypeStruct(shape, dtype) for shape, dtype in outs)
+    result = pl.pallas_call(
+        kernel,
+        out_shape=out_shape,
+        in_specs=specs or [VM] * len(args),
+        out_specs=tuple([VM] * len(outs)),
+        scratch_shapes=list(scratch),
+        compiler_params=pltpu.CompilerParams(vmem_limit_bytes=40 * 1024 * 1024),
+        cost_estimate=pl.CostEstimate(flops=flops, bytes_accessed=nbytes, transcendentals=0),
+    )(*args)
+    return result
+
+
+def swap(value, group_flip=0, loc_flip=0, dp_flip=0):
+    sizes = [lax.axis_size(axis) for axis in AXES]
+    pairs = []
+    for g in range(sizes[0]):
+        for l in range(sizes[1]):
+            for d in range(sizes[2]):
+                here = (g * sizes[1] + l) * sizes[2] + d
+                there = ((g ^ group_flip) * sizes[1] + (l ^ loc_flip)) * sizes[2] + (d ^ dp_flip)
+                pairs.append((here, there))
+    return lax.ppermute(value, AXES, pairs)
+
+
+def local_messages(
+    out_grad, slot_token, slot_count, slot_weight, up_weight, down_weight, hidden_saved, gate_saved
+):
+    model = out_grad.shape[2]
+    tokens = out_grad.shape[1]
+    cap = slot_token.shape[3]
+    hidden_dev = hidden_saved.shape[3]
+    replicas = lax.axis_size("dp")
+    piece_cols, half, count = model // PIECES, hidden_dev // 2, PIECES * cap
+    rows_dev = hidden_dev // replicas
+    near, far = call(
+        select_kernel,
+        [((count, piece_cols + half), BF16), ((count, piece_cols), BF16)],
+        (slot_token, slot_count, slot_weight, out_grad, hidden_saved),
+        [SM, SM, VM, VM, VM],
+        nbytes=tokens * model * 2,
+    )
+    from_x = swap(near, loc_flip=1)
+    from_y = swap(far, group_flip=1)
+    from_xy = swap(far, group_flip=1, loc_flip=1)
+    arrived = (near, from_x, from_y, from_xy)
+    message = ((count, piece_cols + half), BF16)
+    mine, to_1, to_2, to_3 = call(spread_kernel, [message] * 4, arrived, nbytes=count * model)
+    from_1 = swap(to_1, dp_flip=2)
+    from_2 = swap(to_2, dp_flip=4)
+    from_3 = swap(to_3, dp_flip=6)
+    pad = -(-4 * cap // 16) * 16
+    ret_own, ret_x, ret_y, ret_xy = call(
+        expert_kernel,
+        [((count, piece_cols), BF16)] * 4,
+        arrived + (down_weight, gate_saved, up_weight),
+        scratch=[pltpu.VMEM((PIECES * pad, piece_cols), BF16)],
+        flops=4 * pad * model * hidden_dev,
+        nbytes=4 * model * hidden_dev,
+    )
+    back_x = swap(ret_x, loc_flip=1)
+    back_y = swap(ret_y, group_flip=1)
+    back_xy = swap(ret_xy, group_flip=1, loc_flip=1)
+    (input_grad,) = call(
+        combine_kernel,
+        [((1, tokens, model), BF16)],
+        (slot_token, slot_count, ret_own, back_x, back_y, back_xy),
+        [SM, SM, VM, VM, VM, VM],
+        nbytes=2 * tokens * model,
+    )
+    block = ((4 * rows_dev, 2 * piece_cols), BF16)
+    keep, send = call(
+        functools.partial(product_kernel, 1.0 / replicas),
+        [block] * 2,
+        (mine, from_1, from_2, from_3),
+        nbytes=16 * rows_dev * piece_cols,
+    )
+    other = swap(send, dp_flip=1)
+    block = ((rows_dev, 2 * piece_cols), BF16)
+    own, to_x, to_z, to_xz = call(add_kernel, [block] * 4, (keep, other), nbytes=1 << 20)
+    got_x = swap(to_x, loc_flip=1)
+    got_z = swap(to_z, dp_flip=2)
+    got_xz = swap(to_xz, loc_flip=1, dp_flip=2)
+    (down_grad,) = call(
+        join_kernel, [((1, rows_dev, model), F32)], (own, got_x, got_z, got_xz), nbytes=1 << 20
+    )
+    return (input_grad, down_grad)
+
+
+def local(*args):
+    sizes = tuple(lax.axis_size(axis) for axis in AXES)
+    model, cap, hidden_dev = args[0].shape[2], args[1].shape[3], args[6].shape[3]
+    fits = sizes == (2, 2, 8) and model % (PIECES * 128) == 0
+    fits = fits and hidden_dev % 256 == 0 and args[0].shape[1] % 16 == 0 and 4 * cap <= 32
+    return (local_messages if fits else local_collectives)(*args)
 
 
 def solution(mesh):

time: 99.5 us -> 51.4 us (0.52)
  waiting for transfers between devices: 39.7 us -> 15.3 us
  between operations: 15.6 us -> 0.71 us
  matrix products: 11.4 us -> 0 us
  Pallas kernels: 0 us -> 10.2 us
  blocking collectives: 9.99 us -> 0 us
  starting transfers between devices: 11.2 us -> 16.2 us
  other arithmetic: 3.55 us -> 0 us
  local copies, waits for them, and re-layouts: 7.58 us -> 8.65 us
    unnamed x3 -> x0, waiting for transfers between devices: 21.5 us -> none
    ppermute x0 -> x13, starting transfers between devices: none -> 16.2 us  [swap(): return lax.ppermute(value, AXES, pairs)]
    ppermute x0 -> x13, waiting for transfers between devices: none -> 15.3 us  [swap(): return lax.ppermute(value, AXES, pairs)]
    reduce_scatter x1 -> x0, waiting for transfers between devices: 12.2 us -> none  [local(): lax.psum_scatter(rounded.astype(jnp.float32).astype(jnp.bfloat16), 'dp',...]
    dot_general x3 -> x0, matrix products: 11.4 us -> none  [the longest x1 7.11 us: local(): lax.dot_general(grad_up, w_up, (((1,), (1,)), ((), ())), preferred_elemen...]
    all_to_all x3 -> x0, starting transfers between devices: 11.1 us -> none  [the longest x1 4.23 us: local(): lax.all_to_all(weights, 'grp', split_axis=0, concat_axis=0, tiled=True)]
    pallas_call x0 -> x7, Pallas kernels: none -> 10.2 us  [call(): pl.pallas_call(kernel, out_shape=out_shape, in_specs=specs or [VM] * len(...]
    all_gather x2 -> x0, blocking collectives: 9.99 us -> none  [the longest x1 5.78 us: local(): lax.all_gather(arrived[:, None], 'loc', axis=1, tiled=True)]
  transfers between devices with their start and end apart: 5 -> 13, of which waited for: 5 -> 7; matrix products, arithmetic and copies ran while one was open for 11% -> 0% of each run, Pallas kernels for 0% -> 14%
where the time goes in v1:
time: 51.4 us; the launch traced here: 51.1 us
  starting transfers between devices  16.2 us (32%)
  waiting for transfers between devices  15.3 us (30%)
  Pallas kernels  10.2 us (20%)
  local copies, waits for them, and re-layouts  8.65 us (17%)
  between operations  0.71 us (1%)
    ppermute x13, starting transfers between devices, swap(): return lax.ppermute(value, AXES, pairs)  16.2 us
    ppermute x13, waiting for transfers between devices, swap(): return lax.ppermute(value, AXES, pairs)  15.3 us
    pallas_call x7, Pallas kernels, call(): pl.pallas_call(kernel, out_shape=out_shape, in_specs=specs or [VM] * len(...  10.2 us
    unnamed x20, local copies, waits for them, and re-layouts  8.65 us
  transfers between devices with their start and end apart: 13, of which 7 were waited for; matrix products, arithmetic and copies ran while one was open for 0% of the time, Pallas kernels for 14%

profile of v1, /device:TPU:0, one launch (start us, length us, event | category | flops | bytes accessed | tf_op | source)
XLA Modules:
  0.0 51.1 jit_solution(15136738646907009392)
XLA Ops:
  0.6 0.0 copy-start.2
  0.6 1.2 %copy-done.2 = bf16[1,64,7168]{2,1,0:T(8,128)(2,1)S(1)} copy-done((bf16[1,64,7168]{2,1,0:T(8,128)(2,1)S(1)}, bf16[1,64,7168]{2,1,0:T(8,128)(2,1)}, u32[]{:S(2)}) %copy-start.2) | copy-done | bytes 917528
  1.8 0.0 copy-start.3
  1.8 0.7 %copy-done.3 = bf16[1,1,20,256]{3,2,1,0:T(8,128)(2,1)S(1)} copy-done((bf16[1,1,20,256]{3,2,1,0:T(8,128)(2,1)S(1)}, bf16[1,1,20,256]{3,2,1,0:T(8,128)(2,1)}, u32[]{:S(2)}) %copy-start.3) | copy-done | bytes 10264
  2.5 0.0 copy-start.5
  2.5 0.7 %copy-done.5 = s32[1,1,2,5]{3,2,1,0:T(2,128)S(1)} copy-done((s32[1,1,2,5]{3,2,1,0:T(2,128)S(1)}, s32[1,1,2,5]{3,2,1,0:T(2,128)}, u32[]{:S(2)}) %copy-start.5) | copy-done | bytes 64
  3.2 0.0 copy-start.7
  3.2 0.7 %copy-done.7 = s32[1,1,2]{2,1,0:T(1,128)S(1)} copy-done((s32[1,1,2]{2,1,0:T(1,128)S(1)}, s32[1,1,2]{2,1,0:T(1,128)}, u32[]{:S(2)}) %copy-start.7) | copy-done | bytes 32
  3.9 0.0 copy-start.9
  3.9 0.7 %copy-done.9 = bf16[1,1,2,5]{3,2,1,0:T(2,128)(2,1)S(1)} copy-done((bf16[1,1,2,5]{3,2,1,0:T(2,128)(2,1)S(1)}, bf16[1,1,2,5]{3,2,1,0:T(2,128)(2,1)}, u32[]{:S(2)}) %copy-start.9) | copy-done | bytes 44
  4.5 1.2 %shard_map.95 = (bf16[40,1024]{1,0:T(8,128)(2,1)S(1)}, bf16[40,896]{1,0:T(8,128)(2,1)S(1)}) custom-call(s32[1,1,2,5]{3,2,1,0:T(2,128)S(1)} %copy-done.5, s32[1,1,2]{2,1,0:T(1,128)S(1)} %copy-done.7, bf16[1,1,2,5]{3,2,1,0:T(2,128)(2,1)S(1)} %copy-done.9, bf16[1,64,7168]{2,1,0:T(8,128)(2,1)S(1)} %copy-done.2, bf16[1,1,20,256]{3,2,1,0:T(8,128)(2,1)S(1)} %copy-done.3), custom_call_target="tpu_custom_call" | custom-call | bytes 917504 | tf_op jit(solution)/shard_map/pallas_call | solution.py:288
  5.8 3.0 %collective-permute-start = (bf16[40,1024]{1,0:T(8,128)(2,1)S(1)}, bf16[40,1024]{1,0:T(8,128)(2,1)S(1)}, u32[]{:S(2)}, u32[]{:S(2)}) collective-permute-start(bf16[40,1024]{1,0:T(8,128)(2,1)S(1)} %get-tuple-element.18.own), channel_id=1, source_target_pairs={{0,8},{1,9},{2,10},{3,11},{4,12},{5,13},{6,14},{7,15},{8,0},{9,1},... | collective-permute-start | bytes 245768 | tf_op jit(solution)/shard_map/ppermute | solution.py:309
  8.8 1.5 %collective-permute-start.2 = (bf16[40,896]{1,0:T(8,128)(2,1)S(1)}, bf16[40,896]{1,0:T(8,128)(2,1)S(1)}, u32[]{:S(2)}, u32[]{:S(2)}) collective-permute-start(bf16[40,896]{1,0:T(8,128)(2,1)S(1)} %get-tuple-element.19), channel_id=1, source_target_pairs={{0,24},{1,25},{2,26},{3,27},{4,28},{5,29},{6,30},{7,31},{8,16},{9,... | collective-permute-start | bytes 215048 | tf_op jit(solution)/shard_map/ppermute | solution.py:309
  10.3 0.0 collective-permute-start.1
  10.3 4.0 %collective-permute-done.2.from_xy = bf16[40,896]{1,0:T(8,128)(2,1)S(1)} collective-permute-done((bf16[40,896]{1,0:T(8,128)(2,1)S(1)}, bf16[40,896]{1,0:T(8,128)(2,1)S(1)}, u32[]{:S(2)}, u32[]{:S(2)}) %collective-permute-start.2) | collective-permute-done | bytes 71712 | tf_op jit(solution)/shard_map/ppermute | solution.py:309
  14.3 0.7 %collective-permute-done.1.from_y = bf16[40,896]{1,0:T(8,128)(2,1)S(1)} collective-permute-done((bf16[40,896]{1,0:T(8,128)(2,1)S(1)}, bf16[40,896]{1,0:T(8,128)(2,1)S(1)}, u32[]{:S(2)}, u32[]{:S(2)}) %collective-permute-start.1) | collective-permute-done | bytes 71712 | tf_op jit(solution)/shard_map/ppermute | solution.py:309
  15.0 0.0 collective-permute-done.from_x
  15.0 0.3 shard_map.98
  15.4 1.6 %collective-permute-start.6 = (bf16[40,1024]{1,0:T(8,128)(2,1)S(1)}, bf16[40,1024]{1,0:T(8,128)(2,1)S(1)}, u32[]{:S(2)}, u32[]{:S(2)}) collective-permute-start(bf16[40,1024]{1,0:T(8,128)(2,1)S(1)} %get-tuple-element.25), channel_id=1, source_target_pairs={{0,2},{1,3},{2,0},{3,1},{4,6},{5,7},{6,4},{7,5},{8,10},{9,11},{10,... | collective-permute-start | bytes 245768 | tf_op jit(solution)/shard_map/ppermute | solution.py:309
  17.0 2.6 %collective-permute-start.7 = (bf16[40,1024]{1,0:T(8,128)(2,1)S(1)}, bf16[40,1024]{1,0:T(8,128)(2,1)S(1)}, u32[]{:S(2)}, u32[]{:S(2)}) collective-permute-start(bf16[40,1024]{1,0:T(8,128)(2,1)S(1)} %get-tuple-element.26), channel_id=1, source_target_pairs={{0,4},{1,5},{2,6},{3,7},{4,0},{5,1},{6,2},{7,3},{8,12},{9,13},{10,... | collective-permute-start | bytes 245768 | tf_op jit(solution)/shard_map/ppermute | solution.py:309
  19.6 0.2 collective-permute-start.8
  19.8 0.7 %collective-permute-done.6.from_1 = bf16[40,1024]{1,0:T(8,128)(2,1)S(1)} collective-permute-done((bf16[40,1024]{1,0:T(8,128)(2,1)S(1)}, bf16[40,1024]{1,0:T(8,128)(2,1)S(1)}, u32[]{:S(2)}, u32[]{:S(2)}) %collective-permute-start.6) | collective-permute-done | bytes 81952 | tf_op jit(solution)/shard_map/ppermute | solution.py:309
  20.5 3.6 %collective-permute-done.7.from_2 = bf16[40,1024]{1,0:T(8,128)(2,1)S(1)} collective-permute-done((bf16[40,1024]{1,0:T(8,128)(2,1)S(1)}, bf16[40,1024]{1,0:T(8,128)(2,1)S(1)}, u32[]{:S(2)}, u32[]{:S(2)}) %collective-permute-start.7) | collective-permute-done | bytes 81952 | tf_op jit(solution)/shard_map/ppermute | solution.py:309
  24.1 1.8 %collective-permute-done.8.from_3 = bf16[40,1024]{1,0:T(8,128)(2,1)S(1)} collective-permute-done((bf16[40,1024]{1,0:T(8,128)(2,1)S(1)}, bf16[40,1024]{1,0:T(8,128)(2,1)S(1)}, u32[]{:S(2)}, u32[]{:S(2)}) %collective-permute-start.8) | collective-permute-done | bytes 81952 | tf_op jit(solution)/shard_map/ppermute | solution.py:309
  25.9 0.7 %shard_map.99 = (bf16[128,1792]{1,0:T(8,128)(2,1)S(1)}, bf16[128,1792]{1,0:T(8,128)(2,1)S(1)}) custom-call(bf16[40,1024]{1,0:T(8,128)(2,1)S(1)} %get-tuple-element.24.own, bf16[40,1024]{1,0:T(8,128)(2,1)S(1)} %collective-permute-done.6.from_1, bf16[40,1024]{1,0:T(8,128)(2,1)S(1)} %collective-permute-done.7.from_2, ...), custom_call_target="tpu_custom_call" | custom-call | bytes 458752 | tf_op jit(solution)/shard_map/pallas_call | solution.py:288
  26.6 0.1 collective-permute-start.9
  26.6 0.0 copy-start
  26.7 2.0 %copy-done = bf16[1,256,7168]{2,1,0:T(8,128)(2,1)S(1)} copy-done((bf16[1,256,7168]{2,1,0:T(8,128)(2,1)S(1)}, bf16[1,256,7168]{2,1,0:T(8,128)(2,1)}, u32[]{:S(2)}) %copy-start) | copy-done | bytes 3670040
  28.7 0.0 copy-start.1
  28.7 2.0 %copy-done.1 = bf16[1,7168,256]{2,1,0:T(8,128)(2,1)S(1)} copy-done((bf16[1,7168,256]{2,1,0:T(8,128)(2,1)S(1)}, bf16[1,7168,256]{2,1,0:T(8,128)(2,1)}, u32[]{:S(2)}) %copy-start.1) | copy-done | bytes 3670040
  30.7 0.0 copy-start.4
  30.7 0.7 %copy-done.4 = bf16[1,1,20,256]{3,2,1,0:T(8,128)(2,1)S(1)} copy-done((bf16[1,1,20,256]{3,2,1,0:T(8,128)(2,1)S(1)}, bf16[1,1,20,256]{3,2,1,0:T(8,128)(2,1)}, u32[]{:S(2)}) %copy-start.4) | copy-done | bytes 10264
  31.4 0.0 copy-start.6
  31.4 0.0 copy-start.8
  31.4 4.8 %shard_map.96 = (bf16[40,896]{1,0:T(8,128)(2,1)S(1)}, bf16[40,896]{1,0:T(8,128)(2,1)S(1)}, bf16[40,896]{1,0:T(8,128)(2,1)S(1)}, bf16[40,896]{1,0:T(8,128)(2,1)S(1)}) custom-call(bf16[40,1024]{1,0:T(8,128)(2,1)S(1)} %get-tuple-element.18.own, bf16[40,1024]{1,0:T(8,128)(2,1)S(1)} %collective-permute-done.from_x, ...), custom_call_target="tpu_custom_call" | custom-call | flops 234881024 | bytes 7340032 | tf_op jit(solution)/shard_map/pallas_call | solution.py:288
  36.2 1.3 %collective-permute-start.3 = (bf16[40,896]{1,0:T(8,128)(2,1)S(1)}, bf16[40,896]{1,0:T(8,128)(2,1)S(1)}, u32[]{:S(2)}, u32[]{:S(2)}) collective-permute-start(bf16[40,896]{1,0:T(8,128)(2,1)S(1)} %get-tuple-element.21), channel_id=1, source_target_pairs={{0,8},{1,9},{2,10},{3,11},{4,12},{5,13},{6,14},{7,15},{8,0},{9,1},... | collective-permute-start | bytes 215048 | tf_op jit(solution)/shard_map/ppermute | solution.py:309
  37.5 0.0 collective-permute-done.9.other
  37.5 0.1 shard_map.100
  37.6 0.9 %collective-permute-start.10 = (bf16[32,1792]{1,0:T(8,128)(2,1)S(1)}, bf16[32,1792]{1,0:T(8,128)(2,1)S(1)}, u32[]{:S(2)}, u32[]{:S(2)}) collective-permute-start(bf16[32,1792]{1,0:T(8,128)(2,1)S(1)} %get-tuple-element.31), channel_id=1, source_target_pairs={{0,8},{1,9},{2,10},{3,11},{4,12},{5,13},{6,14},{7,15},{8,0},{9,1},... | collective-permute-start | bytes 344072 | tf_op jit(solution)/shard_map/ppermute | solution.py:309
  38.5 0.0 collective-permute-start.11
  38.5 2.7 %collective-permute-start.12 = (bf16[32,1792]{1,0:T(8,128)(2,1)S(1)}, bf16[32,1792]{1,0:T(8,128)(2,1)S(1)}, u32[]{:S(2)}, u32[]{:S(2)}) collective-permute-start(bf16[32,1792]{1,0:T(8,128)(2,1)S(1)} %get-tuple-element.33), channel_id=1, source_target_pairs={{0,10},{1,11},{2,8},{3,9},{4,14},{5,15},{6,12},{7,13},{8,2},{9,3},... | collective-permute-start | bytes 344072 | tf_op jit(solution)/shard_map/ppermute | solution.py:309
  41.1 0.8 %collective-permute-start.4 = (bf16[40,896]{1,0:T(8,128)(2,1)S(1)}, bf16[40,896]{1,0:T(8,128)(2,1)S(1)}, u32[]{:S(2)}, u32[]{:S(2)}) collective-permute-start(bf16[40,896]{1,0:T(8,128)(2,1)S(1)} %get-tuple-element.22), channel_id=1, source_target_pairs={{0,16},{1,17},{2,18},{3,19},{4,20},{5,21},{6,22},{7,23},{8,24},{9,... | collective-permute-start | bytes 215048 | tf_op jit(solution)/shard_map/ppermute | solution.py:309
  42.0 0.0 collective-permute-done.3.from_x
  42.0 1.5 %collective-permute-start.5 = (bf16[40,896]{1,0:T(8,128)(2,1)S(1)}, bf16[40,896]{1,0:T(8,128)(2,1)S(1)}, u32[]{:S(2)}, u32[]{:S(2)}) collective-permute-start(bf16[40,896]{1,0:T(8,128)(2,1)S(1)} %get-tuple-element.23), channel_id=1, source_target_pairs={{0,24},{1,25},{2,26},{3,27},{4,28},{5,29},{6,30},{7,31},{8,16},{9,... | collective-permute-start | bytes 215048 | tf_op jit(solution)/shard_map/ppermute | solution.py:309
  43.4 2.5 %collective-permute-done.4.from_y = bf16[40,896]{1,0:T(8,128)(2,1)S(1)} collective-permute-done((bf16[40,896]{1,0:T(8,128)(2,1)S(1)}, bf16[40,896]{1,0:T(8,128)(2,1)S(1)}, u32[]{:S(2)}, u32[]{:S(2)}) %collective-permute-start.4) | collective-permute-done | bytes 71712 | tf_op jit(solution)/shard_map/ppermute | solution.py:309
  45.9 2.0 %collective-permute-done.5.from_xy = bf16[40,896]{1,0:T(8,128)(2,1)S(1)} collective-permute-done((bf16[40,896]{1,0:T(8,128)(2,1)S(1)}, bf16[40,896]{1,0:T(8,128)(2,1)S(1)}, u32[]{:S(2)}, u32[]{:S(2)}) %collective-permute-start.5) | collective-permute-done | bytes 71712 | tf_op jit(solution)/shard_map/ppermute | solution.py:309
  47.9 0.0 copy-done.6
  47.9 0.0 copy-done.8
  47.9 2.1 %shard_map.97 = bf16[1,64,7168]{2,1,0:T(8,128)(2,1)} custom-call(s32[1,1,2,5]{3,2,1,0:T(2,128)S(1)} %copy-done.6, s32[1,1,2]{2,1,0:T(1,128)S(1)} %copy-done.8, bf16[40,896]{1,0:T(8,128)(2,1)S(1)} %get-tuple-element.20.own, bf16[40,896]{1,0:T(8,128)(2,1)S(1)} %collective-permute-done.3.from_x, bf16[40,896]{1,0:T(8,128)(2,1)S(1)} %collective-permute-done.4.from_y, ...), custom_call_target="tpu_custom_call" | custom-call | bytes 917504 | tf_op jit(solution)/shard_map/pallas_call | solution.py:288
  50.0 0.0 collective-permute-done.10.from_x
  50.0 0.0 collective-permute-done.11.from_z
  50.1 0.0 collective-permute-done.12.from_xz
  50.1 1.0 %shard_map.101 = f32[1,32,7168]{2,1,0:T(8,128)} custom-call(bf16[32,1792]{1,0:T(8,128)(2,1)S(1)} %get-tuple-element.30.own, bf16[32,1792]{1,0:T(8,128)(2,1)S(1)} %collective-permute-done.10.from_x, bf16[32,1792]{1,0:T(8,128)(2,1)S(1)} %collective-permute-done.11.from_z, bf16[32,1792]{1,0:T(8,128)(2,1)S(1)} %collective-permute-done.12.from_xz), custom_call_target="tpu_custom_call" | custom-call | bytes 1048576 | tf_op jit(solution)/shard_map/pallas_call | solution.py:288
Async XLA Ops:
  0.6 1.2 %copy-start.2 = (bf16[1,64,7168]{2,1,0:T(8,128)(2,1)S(1)}, bf16[1,64,7168]{2,1,0:T(8,128)(2,1)}, u32[]{:S(2)}) copy-start(bf16[1,64,7168]{2,1,0:T(8,128)(2,1)} %rows.1) | copy-start | bytes 2752516
  1.8 0.7 %copy-start.3 = (bf16[1,1,20,256]{3,2,1,0:T(8,128)(2,1)S(1)}, bf16[1,1,20,256]{3,2,1,0:T(8,128)(2,1)}, u32[]{:S(2)}) copy-start(bf16[1,1,20,256]{3,2,1,0:T(8,128)(2,1)} %hidden.1) | copy-start | bytes 30724
  2.5 0.7 %copy-start.5 = (s32[1,1,2,5]{3,2,1,0:T(2,128)S(1)}, s32[1,1,2,5]{3,2,1,0:T(2,128)}, u32[]{:S(2)}) copy-start(s32[1,1,2,5]{3,2,1,0:T(2,128)} %tok.3) | copy-start | bytes 124
  3.2 0.7 %copy-start.7 = (s32[1,1,2]{2,1,0:T(1,128)S(1)}, s32[1,1,2]{2,1,0:T(1,128)}, u32[]{:S(2)}) copy-start(s32[1,1,2]{2,1,0:T(1,128)} %cnt.3) | copy-start | bytes 28
  3.9 0.7 %copy-start.9 = (bf16[1,1,2,5]{3,2,1,0:T(2,128)(2,1)S(1)}, bf16[1,1,2,5]{3,2,1,0:T(2,128)(2,1)}, u32[]{:S(2)}) copy-start(bf16[1,1,2,5]{3,2,1,0:T(2,128)(2,1)} %weight.1) | copy-start | bytes 64
  5.8 9.3 %collective-permute-start = (bf16[40,1024]{1,0:T(8,128)(2,1)S(1)}, bf16[40,1024]{1,0:T(8,128)(2,1)S(1)}, u32[]{:S(2)}, u32[]{:S(2)}) collective-permute-start(bf16[40,1024]{1,0:T(8,128)(2,1)S(1)} %get-tuple-element.18.own), channel_id=1, source_target_pairs={{0,8},{1,9},{2,10},{3,11},{4,12},{5,13},{6,14},{7,15},{8,0},{9,1},... | collective-permute-start | bytes 245768 | tf_op jit(solution)/shard_map/ppermute | solution.py:309
  8.8 5.5 %collective-permute-start.2 = (bf16[40,896]{1,0:T(8,128)(2,1)S(1)}, bf16[40,896]{1,0:T(8,128)(2,1)S(1)}, u32[]{:S(2)}, u32[]{:S(2)}) collective-permute-start(bf16[40,896]{1,0:T(8,128)(2,1)S(1)} %get-tuple-element.19), channel_id=1, source_target_pairs={{0,24},{1,25},{2,26},{3,27},{4,28},{5,29},{6,30},{7,31},{8,16},{9,... | collective-permute-start | bytes 215048 | tf_op jit(solution)/shard_map/ppermute | solution.py:309
  10.3 4.8 %collective-permute-start.1 = (bf16[40,896]{1,0:T(8,128)(2,1)S(1)}, bf16[40,896]{1,0:T(8,128)(2,1)S(1)}, u32[]{:S(2)}, u32[]{:S(2)}) collective-permute-start(bf16[40,896]{1,0:T(8,128)(2,1)S(1)} %get-tuple-element.19), channel_id=1, source_target_pairs={{0,16},{1,17},{2,18},{3,19},{4,20},{5,21},{6,22},{7,23},{8,24},{9,... | collective-permute-start | bytes 215048 | tf_op jit(solution)/shard_map/ppermute | solution.py:309
  15.4 5.1 %collective-permute-start.6 = (bf16[40,1024]{1,0:T(8,128)(2,1)S(1)}, bf16[40,1024]{1,0:T(8,128)(2,1)S(1)}, u32[]{:S(2)}, u32[]{:S(2)}) collective-permute-start(bf16[40,1024]{1,0:T(8,128)(2,1)S(1)} %get-tuple-element.25), channel_id=1, source_target_pairs={{0,2},{1,3},{2,0},{3,1},{4,6},{5,7},{6,4},{7,5},{8,10},{9,11},{10,... | collective-permute-start | bytes 245768 | tf_op jit(solution)/shard_map/ppermute | solution.py:309
  17.0 7.1 %collective-permute-start.7 = (bf16[40,1024]{1,0:T(8,128)(2,1)S(1)}, bf16[40,1024]{1,0:T(8,128)(2,1)S(1)}, u32[]{:S(2)}, u32[]{:S(2)}) collective-permute-start(bf16[40,1024]{1,0:T(8,128)(2,1)S(1)} %get-tuple-element.26), channel_id=1, source_target_pairs={{0,4},{1,5},{2,6},{3,7},{4,0},{5,1},{6,2},{7,3},{8,12},{9,13},{10,... | collective-permute-start | bytes 245768 | tf_op jit(solution)/shard_map/ppermute | solution.py:309
  19.6 6.3 %collective-permute-start.8 = (bf16[40,1024]{1,0:T(8,128)(2,1)S(1)}, bf16[40,1024]{1,0:T(8,128)(2,1)S(1)}, u32[]{:S(2)}, u32[]{:S(2)}) collective-permute-start(bf16[40,1024]{1,0:T(8,128)(2,1)S(1)} %get-tuple-element.27), channel_id=1, source_target_pairs={{0,6},{1,7},{2,4},{3,5},{4,2},{5,3},{6,0},{7,1},{8,14},{9,15},{10,... | collective-permute-start | bytes 245768 | tf_op jit(solution)/shard_map/ppermute | solution.py:309
  26.6 10.9 %collective-permute-start.9 = (bf16[128,1792]{1,0:T(8,128)(2,1)S(1)}, bf16[128,1792]{1,0:T(8,128)(2,1)S(1)}, u32[]{:S(2)}, u32[]{:S(2)}) collective-permute-start(bf16[128,1792]{1,0:T(8,128)(2,1)S(1)} %get-tuple-element.29), channel_id=1, source_target_pairs={{0,1},{1,0},{2,3},{3,2},{4,5},{5,4},{6,7},{7,6},{8,9},{9,8},{10,11... | collective-permute-start | bytes 1376264 | tf_op jit(solution)/shard_map/ppermute | solution.py:309
  26.6 2.0 %copy-start = (bf16[1,256,7168]{2,1,0:T(8,128)(2,1)S(1)}, bf16[1,256,7168]{2,1,0:T(8,128)(2,1)}, u32[]{:S(2)}) copy-start(bf16[1,256,7168]{2,1,0:T(8,128)(2,1)} %down.1) | copy-start | bytes 11010052
  28.7 2.0 %copy-start.1 = (bf16[1,7168,256]{2,1,0:T(8,128)(2,1)S(1)}, bf16[1,7168,256]{2,1,0:T(8,128)(2,1)}, u32[]{:S(2)}) copy-start(bf16[1,7168,256]{2,1,0:T(8,128)(2,1)} %up.1) | copy-start | bytes 11010052
  30.7 0.7 %copy-start.4 = (bf16[1,1,20,256]{3,2,1,0:T(8,128)(2,1)S(1)}, bf16[1,1,20,256]{3,2,1,0:T(8,128)(2,1)}, u32[]{:S(2)}) copy-start(bf16[1,1,20,256]{3,2,1,0:T(8,128)(2,1)} %gate.1) | copy-start | bytes 30724
  31.4 16.5 %copy-start.6 = (s32[1,1,2,5]{3,2,1,0:T(2,128)S(1)}, s32[1,1,2,5]{3,2,1,0:T(2,128)}, u32[]{:S(2)}) copy-start(s32[1,1,2,5]{3,2,1,0:T(2,128)} %tok.3) | copy-start | bytes 124
  31.4 16.5 %copy-start.8 = (s32[1,1,2]{2,1,0:T(1,128)S(1)}, s32[1,1,2]{2,1,0:T(1,128)}, u32[]{:S(2)}) copy-start(s32[1,1,2]{2,1,0:T(1,128)} %cnt.3) | copy-start | bytes 28
  36.2 5.8 %collective-permute-start.3 = (bf16[40,896]{1,0:T(8,128)(2,1)S(1)}, bf16[40,896]{1,0:T(8,128)(2,1)S(1)}, u32[]{:S(2)}, u32[]{:S(2)}) collective-permute-start(bf16[40,896]{1,0:T(8,128)(2,1)S(1)} %get-tuple-element.21), channel_id=1, source_target_pairs={{0,8},{1,9},{2,10},{3,11},{4,12},{5,13},{6,14},{7,15},{8,0},{9,1},... | collective-permute-start | bytes 215048 | tf_op jit(solution)/shard_map/ppermute | solution.py:309
  37.6 12.5 %collective-permute-start.10 = (bf16[32,1792]{1,0:T(8,128)(2,1)S(1)}, bf16[32,1792]{1,0:T(8,128)(2,1)S(1)}, u32[]{:S(2)}, u32[]{:S(2)}) collective-permute-start(bf16[32,1792]{1,0:T(8,128)(2,1)S(1)} %get-tuple-element.31), channel_id=1, source_target_pairs={{0,8},{1,9},{2,10},{3,11},{4,12},{5,13},{6,14},{7,15},{8,0},{9,1},... | collective-permute-start | bytes 344072 | tf_op jit(solution)/shard_map/ppermute | solution.py:309
  38.5 11.6 %collective-permute-start.11 = (bf16[32,1792]{1,0:T(8,128)(2,1)S(1)}, bf16[32,1792]{1,0:T(8,128)(2,1)S(1)}, u32[]{:S(2)}, u32[]{:S(2)}) collective-permute-start(bf16[32,1792]{1,0:T(8,128)(2,1)S(1)} %get-tuple-element.32), channel_id=1, source_target_pairs={{0,2},{1,3},{2,0},{3,1},{4,6},{5,7},{6,4},{7,5},{8,10},{9,11},{10,... | collective-permute-start | bytes 344072 | tf_op jit(solution)/shard_map/ppermute | solution.py:309
  38.5 11.6 %collective-permute-start.12 = (bf16[32,1792]{1,0:T(8,128)(2,1)S(1)}, bf16[32,1792]{1,0:T(8,128)(2,1)S(1)}, u32[]{:S(2)}, u32[]{:S(2)}) collective-permute-start(bf16[32,1792]{1,0:T(8,128)(2,1)S(1)} %get-tuple-element.33), channel_id=1, source_target_pairs={{0,10},{1,11},{2,8},{3,9},{4,14},{5,15},{6,12},{7,13},{8,2},{9,3},... | collective-permute-start | bytes 344072 | tf_op jit(solution)/shard_map/ppermute | solution.py:309
  41.1 4.8 %collective-permute-start.4 = (bf16[40,896]{1,0:T(8,128)(2,1)S(1)}, bf16[40,896]{1,0:T(8,128)(2,1)S(1)}, u32[]{:S(2)}, u32[]{:S(2)}) collective-permute-start(bf16[40,896]{1,0:T(8,128)(2,1)S(1)} %get-tuple-element.22), channel_id=1, source_target_pairs={{0,16},{1,17},{2,18},{3,19},{4,20},{5,21},{6,22},{7,23},{8,24},{9,... | collective-permute-start | bytes 215048 | tf_op jit(solution)/shard_map/ppermute | solution.py:309
  42.0 6.0 %collective-permute-start.5 = (bf16[40,896]{1,0:T(8,128)(2,1)S(1)}, bf16[40,896]{1,0:T(8,128)(2,1)S(1)}, u32[]{:S(2)}, u32[]{:S(2)}) collective-permute-start(bf16[40,896]{1,0:T(8,128)(2,1)S(1)} %get-tuple-element.23), channel_id=1, source_target_pairs={{0,24},{1,25},{2,26},{3,27},{4,28},{5,29},{6,30},{7,31},{8,16},{9,... | collective-permute-start | bytes 215048 | tf_op jit(solution)/shard_map/ppermute | solution.py:309

commit v2 on v1

--- a/solution.py
+++ b/solution.py
@@ -106,17 +106,32 @@
     return group, loc, z % 2, z // 2, dp % 2
 
 
-def select_kernel(tok, cnt, weight, rows, hidden, near, far):
+def select_kernel(
+    tok_hbm, cnt_hbm, weight_hbm, rows_hbm, hidden_hbm, near, far, names, tok, cnt, weight, rows,
+    hidden, sems
+):
+    pairs = (
+        (tok_hbm, tok), (cnt_hbm, cnt), (weight_hbm, weight), (rows_hbm, rows), (hidden_hbm, hidden)
+    )
+    copies = [pltpu.make_async_copy(a, b, sems.at[i]) for i, (a, b) in enumerate(pairs)]
+    for copy in copies:
+        copy.start()
     cap = tok.shape[3]
     group, _, _, _, _ = place()
     tokens, model = rows.shape[1], rows.shape[2]
     piece_cols = model // PIECES
     count = PIECES * cap
-    scale = weight[0, 0].astype(F32)
     row, token = iota((count, tokens), 0), iota((count, tokens), 1)
     piece = quotient(row, cap, count)
     slot = row - cap * piece
-    for other, out in ((0, near), (1, far)):
+    line, lane = iota(names.shape, 0), iota(names.shape, 1)
+    lane_slot = lane - cap * quotient(lane, cap, names.shape[1])
+    for copy in copies[:3]:
+        copy.wait()
+    scale = weight[0, 0].astype(F32)
+    named = jnp.full(names.shape, -1, jnp.int32)
+    values = []
+    for other in range(2):
         expert = jnp.where(group == other, 0, 1)
         live = cnt[0, 0, expert]
         value = jnp.zeros((count, tokens), F32)
@@ -126,6 +141,12 @@
                 expert == 0, scale[0:1, s : s + 1], scale[1:2, s : s + 1]
             )
             value = jnp.where((slot == s) & (token == name), factor, value)
+            named = jnp.where((line == other) & (lane_slot == s), name, named)
+        values.append(value)
+    names[...] = named
+    for copy in copies[3:]:
+        copy.wait()
+    for value, out in zip(values, (near, far)):
         total = jnp.zeros((count, piece_cols), F32)
         for j in range(PIECES):
             chosen = jnp.where(piece == j, value, 0.0).astype(BF16)
@@ -140,7 +161,16 @@
     near[:, piece_cols:] = folded.astype(BF16)
 
 
-def spread_kernel(own, from_x, from_y, from_xy, keep, to_1, to_2, to_3):
+def load_kernel(down_hbm, up_hbm, gate_hbm, after, down, up, gate, sems):
+    pairs = ((down_hbm, down), (up_hbm, up), (gate_hbm, gate))
+    copies = [pltpu.make_async_copy(a, b, sems.at[i]) for i, (a, b) in enumerate(pairs)]
+    for copy in copies:
+        copy.start()
+    for copy in copies:
+        copy.wait()
+
+
+def spread_kernel(own, from_x, from_y, from_xy, after, keep, to_1, to_2, to_3):
     count, piece_cols = from_y.shape
     cap = count // PIECES
     slots = 4 * cap
@@ -204,32 +234,21 @@
         ref[...] = dot(hot(match), stack[...]).astype(BF16)
 
 
-def combine_kernel(tok, cnt, own, from_x, from_y, from_xy, out):
+def combine_kernel(names, own, from_x, from_y, from_xy, out):
     count, piece_cols = own.shape
-    cap = tok.shape[3]
+    cap = count // PIECES
     tokens = out.shape[1]
-    group, _, _, _, _ = place()
-    m, n = iota((tokens, count), 0), iota((tokens, count), 1)
-    nq = quotient(n, cap, count)
-    n_slot = n - cap * nq
-    pairs = []
-    for other, (a, b) in enumerate(((own, from_x), (from_y, from_xy))):
-        contrib = (a[...].astype(F32) + b[...].astype(F32)).astype(BF16)
-        expert = jnp.where(group == other, 0, 1)
-        live = cnt[0, 0, expert]
-        match = jnp.zeros((tokens, count), F32)
-        for s in range(cap):
-            name = jnp.where(s < live, tok[0, 0, expert, s], -1)
-            match = jnp.where((n_slot == s) & (m == name), 1.0, match)
-        pairs.append((match, contrib))
+    near = (own[...].astype(F32) + from_x[...].astype(F32)).astype(BF16)
+    far = (from_y[...].astype(F32) + from_xy[...].astype(F32)).astype(BF16)
+    token, lane = iota((tokens, count), 0), iota((tokens, count), 1)
+    piece = quotient(lane, cap, count)
+    match = [token == names[other : other + 1, :count] for other in range(2)]
     for j in range(PIECES):
-        total = jnp.zeros((tokens, piece_cols), F32)
-        for match, contrib in pairs:
-            total += dot(jnp.where(nq == j, match, 0.0).astype(BF16), contrib)
+        total = dot(hot(match[0] & (piece == j)), near) + dot(hot(match[1] & (piece == j)), far)
         out[0, :, j * piece_cols : (j + 1) * piece_cols] = total.astype(BF16)
 
 
-def product_kernel(scale, own, from_1, from_2, from_3, keep, send):
+def product_kernel(scale, own, from_1, from_2, from_3, after, keep, send):
     count = own.shape[0]
     cap = count // PIECES
     slots = 4 * cap
@@ -280,7 +299,7 @@
 
 
 VM = pl.BlockSpec(memory_space=pltpu.VMEM)
-SM = pl.BlockSpec(memory_space=pltpu.SMEM)
+ANY = pl.BlockSpec(memory_space=pl.ANY)
 
 
 def call(kernel, outs, args, specs=None, scratch=(), flops=0, nbytes=0):
@@ -291,10 +310,14 @@
         in_specs=specs or [VM] * len(args),
         out_specs=tuple([VM] * len(outs)),
         scratch_shapes=list(scratch),
-        compiler_params=pltpu.CompilerParams(vmem_limit_bytes=40 * 1024 * 1024),
+        compiler_params=pltpu.CompilerParams(vmem_limit_bytes=16 * 1024 * 1024),
         cost_estimate=pl.CostEstimate(flops=flops, bytes_accessed=nbytes, transcendentals=0),
     )(*args)
     return result
+
+
+def hbm(value):
+    return pltpu.with_memory_space_constraint(value, pltpu.HBM)
 
 
 def swap(value, group_flip=0, loc_flip=0, dp_flip=0):
@@ -319,19 +342,38 @@
     replicas = lax.axis_size("dp")
     piece_cols, half, count = model // PIECES, hidden_dev // 2, PIECES * cap
     rows_dev = hidden_dev // replicas
-    near, far = call(
+    inputs = (slot_token, slot_count, slot_weight, out_grad, hidden_saved)
+    spaces = (pltpu.SMEM, pltpu.SMEM, pltpu.VMEM, pltpu.VMEM, pltpu.VMEM)
+    near, far, names = call(
         select_kernel,
-        [((count, piece_cols + half), BF16), ((count, piece_cols), BF16)],
-        (slot_token, slot_count, slot_weight, out_grad, hidden_saved),
-        [SM, SM, VM, VM, VM],
+        [
+            ((count, piece_cols + half), BF16),
+            ((count, piece_cols), BF16),
+            ((8, 128), jnp.int32),
+        ],
+        [hbm(x) for x in inputs],
+        [ANY] * 5,
+        scratch=[space(x.shape, x.dtype) for space, x in zip(spaces, inputs)]
+        + [pltpu.SemaphoreType.DMA((5,))],
         nbytes=tokens * model * 2,
     )
     from_x = swap(near, loc_flip=1)
     from_y = swap(far, group_flip=1)
     from_xy = swap(far, group_flip=1, loc_flip=1)
     arrived = (near, from_x, from_y, from_xy)
+    held = (down_weight, up_weight, gate_saved)
+    down, up, gate = call(
+        load_kernel,
+        [(x.shape, x.dtype) for x in held],
+        [hbm(x) for x in held] + [far],
+        [ANY] * 4,
+        scratch=[pltpu.SemaphoreType.DMA((3,))],
+        nbytes=8 * model * hidden_dev,
+    )
     message = ((count, piece_cols + half), BF16)
-    mine, to_1, to_2, to_3 = call(spread_kernel, [message] * 4, arrived, nbytes=count * model)
+    mine, to_1, to_2, to_3 = call(
+        spread_kernel, [message] * 4, arrived + (gate,), [VM] * 4 + [ANY], nbytes=count * model
+    )
     from_1 = swap(to_1, dp_flip=2)
     from_2 = swap(to_2, dp_flip=4)
     from_3 = swap(to_3, dp_flip=6)
@@ -339,7 +381,7 @@
     ret_own, ret_x, ret_y, ret_xy = call(
         expert_kernel,
         [((count, piece_cols), BF16)] * 4,
-        arrived + (down_weight, gate_saved, up_weight),
+        arrived + (down, gate, up),
         scratch=[pltpu.VMEM((PIECES * pad, piece_cols), BF16)],
         flops=4 * pad * model * hidden_dev,
         nbytes=4 * model * hidden_dev,
@@ -350,15 +392,15 @@
     (input_grad,) = call(
         combine_kernel,
         [((1, tokens, model), BF16)],
-        (slot_token, slot_count, ret_own, back_x, back_y, back_xy),
-        [SM, SM, VM, VM, VM, VM],
+        (names, ret_own, back_x, back_y, back_xy),
         nbytes=2 * tokens * model,
     )
     block = ((4 * rows_dev, 2 * piece_cols), BF16)
     keep, send = call(
         functools.partial(product_kernel, 1.0 / replicas),
         [block] * 2,
-        (mine, from_1, from_2, from_3),
+        (mine, from_1, from_2, from_3, ret_own),
+        [VM] * 4 + [ANY],
         nbytes=16 * rows_dev * piece_cols,
     )
     other = swap(send, dp_flip=1)

time: 51.4 us -> 38.2 us (0.74)
  local copies, waits for them, and re-layouts: 8.65 us -> 0 us
  waiting for transfers between devices: 15.3 us -> 7.34 us
  Pallas kernels: 10.2 us -> 13.4 us
    unnamed x20 -> x0, local copies, waits for them, and re-layouts: 8.65 us -> none
    ppermute x13, waiting for transfers between devices: 15.3 us -> 7.34 us  [swap(): return lax.ppermute(value, AXES, pairs)]
    pallas_call x7 -> x8, Pallas kernels: 10.2 us -> 13.4 us  [call(): pl.pallas_call(kernel, out_shape=out_shape, in_specs=specs or [VM] * len(...]
  transfers between devices with their start and end apart: 13 -> 13, of which waited for: 7 -> 6; matrix products, arithmetic and copies ran while one was open for 0% -> 0% of each run, Pallas kernels for 14% -> 25%
where the time goes in v2:
time: 38.2 us; the launch traced here: 38 us
  starting transfers between devices  16.6 us (43%)
  Pallas kernels  13.4 us (35%)
  waiting for transfers between devices  7.34 us (19%)
  between operations  0.71 us (2%)
    ppermute x13, starting transfers between devices, swap(): return lax.ppermute(value, AXES, pairs)  16.6 us
    pallas_call x8, Pallas kernels, call(): pl.pallas_call(kernel, out_shape=out_shape, in_specs=specs or [VM] * len(...  13.4 us
    ppermute x13, waiting for transfers between devices, swap(): return lax.ppermute(value, AXES, pairs)  7.34 us
  transfers between devices with their start and end apart: 13, of which 6 were waited for; matrix products, arithmetic and copies ran while one was open for 0% of the time, Pallas kernels for 25%

profile of v2, /device:TPU:0, one launch (start us, length us, event | category | flops | bytes accessed | tf_op | source)
XLA Modules:
  0.0 38.0 jit_solution(17435700359603475041)
XLA Ops:
  0.6 1.8 %shard_map.95 = (bf16[40,1024]{1,0:T(8,128)(2,1)S(1)}, bf16[40,896]{1,0:T(8,128)(2,1)S(1)}, s32[8,128]{1,0:T(8,128)S(1)}) custom-call(s32[1,1,2,5]{3,2,1,0:T(2,128)} %tok_hbm.1, s32[1,1,2]{2,1,0:T(1,128)} %cnt_hbm.1, bf16[1,1,2,5]{3,2,1,0:T(2,128)(2,1)} %weight_hbm.1, bf16[1,64,7168]{2,1,0:T(8,128)(2,1)} %rows_hbm.1, bf16[1,1,20,256]{3,2,1,0:T(8,128)(2,1)} %hidden_hbm.1), custom_call_target="tpu_custom_call" | custom-call | bytes 917504 | tf_op jit(solution)/shard_map/pallas_call | solution.py:307
  2.4 3.0 %collective-permute-start = (bf16[40,1024]{1,0:T(8,128)(2,1)S(1)}, bf16[40,1024]{1,0:T(8,128)(2,1)S(1)}, u32[]{:S(2)}, u32[]{:S(2)}) collective-permute-start(bf16[40,1024]{1,0:T(8,128)(2,1)S(1)} %get-tuple-element.23.own), channel_id=1, source_target_pairs={{0,8},{1,9},{2,10},{3,11},{4,12},{5,13},{6,14},{7,15},{8,0},{9,1},... | collective-permute-start | bytes 245768 | tf_op jit(solution)/shard_map/ppermute | solution.py:332
  5.4 1.5 %collective-permute-start.2 = (bf16[40,896]{1,0:T(8,128)(2,1)S(1)}, bf16[40,896]{1,0:T(8,128)(2,1)S(1)}, u32[]{:S(2)}, u32[]{:S(2)}) collective-permute-start(bf16[40,896]{1,0:T(8,128)(2,1)S(1)} %get-tuple-element.24.after), channel_id=1, source_target_pairs={{0,24},{1,25},{2,26},{3,27},{4,28},{5,29},{6,30},{7,31},{8,16},{9,... | collective-permute-start | bytes 215048 | tf_op jit(solution)/shard_map/ppermute | solution.py:332
  6.9 0.1 collective-permute-start.1
  7.0 3.2 %shard_map.96 = (bf16[1,256,7168]{2,1,0:T(8,128)(2,1)S(1)}, bf16[1,7168,256]{2,1,0:T(8,128)(2,1)S(1)}, bf16[1,1,20,256]{3,2,1,0:T(8,128)(2,1)S(1)}) custom-call(bf16[1,256,7168]{2,1,0:T(8,128)(2,1)} %down_hbm.1, bf16[1,7168,256]{2,1,0:T(8,128)(2,1)} %up_hbm.1, bf16[1,1,20,256]{3,2,1,0:T(8,128)(2,1)} %gate_hbm.1, bf16[40,896]{1,0:T(8,128)(2,1)S(1)} %get-tuple-element.24.after), custom_call_target="tpu_custom_call" | custom-call | bytes 14680064 | tf_op jit(solution)/shard_map/pallas_call | solution.py:307
  10.2 0.8 %collective-permute-done.2.from_xy = bf16[40,896]{1,0:T(8,128)(2,1)S(1)} collective-permute-done((bf16[40,896]{1,0:T(8,128)(2,1)S(1)}, bf16[40,896]{1,0:T(8,128)(2,1)S(1)}, u32[]{:S(2)}, u32[]{:S(2)}) %collective-permute-start.2) | collective-permute-done | bytes 71712 | tf_op jit(solution)/shard_map/ppermute | solution.py:332
  11.0 0.7 %collective-permute-done.1.from_y = bf16[40,896]{1,0:T(8,128)(2,1)S(1)} collective-permute-done((bf16[40,896]{1,0:T(8,128)(2,1)S(1)}, bf16[40,896]{1,0:T(8,128)(2,1)S(1)}, u32[]{:S(2)}, u32[]{:S(2)}) %collective-permute-start.1) | collective-permute-done | bytes 71712 | tf_op jit(solution)/shard_map/ppermute | solution.py:332
  11.7 0.0 collective-permute-done.from_x
  11.7 0.3 shard_map.99
  12.1 1.6 %collective-permute-start.6 = (bf16[40,1024]{1,0:T(8,128)(2,1)S(1)}, bf16[40,1024]{1,0:T(8,128)(2,1)S(1)}, u32[]{:S(2)}, u32[]{:S(2)}) collective-permute-start(bf16[40,1024]{1,0:T(8,128)(2,1)S(1)} %get-tuple-element.33), channel_id=1, source_target_pairs={{0,2},{1,3},{2,0},{3,1},{4,6},{5,7},{6,4},{7,5},{8,10},{9,11},{10,... | collective-permute-start | bytes 245768 | tf_op jit(solution)/shard_map/ppermute | solution.py:332
  13.7 2.6 %collective-permute-start.7 = (bf16[40,1024]{1,0:T(8,128)(2,1)S(1)}, bf16[40,1024]{1,0:T(8,128)(2,1)S(1)}, u32[]{:S(2)}, u32[]{:S(2)}) collective-permute-start(bf16[40,1024]{1,0:T(8,128)(2,1)S(1)} %get-tuple-element.34), channel_id=1, source_target_pairs={{0,4},{1,5},{2,6},{3,7},{4,0},{5,1},{6,2},{7,3},{8,12},{9,13},{10,... | collective-permute-start | bytes 245768 | tf_op jit(solution)/shard_map/ppermute | solution.py:332
  16.3 0.2 collective-permute-start.8
  16.5 4.8 %shard_map.97 = (bf16[40,896]{1,0:T(8,128)(2,1)S(1)}, bf16[40,896]{1,0:T(8,128)(2,1)S(1)}, bf16[40,896]{1,0:T(8,128)(2,1)S(1)}, bf16[40,896]{1,0:T(8,128)(2,1)S(1)}) custom-call(bf16[40,1024]{1,0:T(8,128)(2,1)S(1)} %get-tuple-element.23.own, bf16[40,1024]{1,0:T(8,128)(2,1)S(1)} %collective-permute-done.from_x, ...), custom_call_target="tpu_custom_call" | custom-call | flops 234881024 | bytes 7340032 | tf_op jit(solution)/shard_map/pallas_call | solution.py:307
  21.3 0.0 collective-permute-done.6.from_1
  21.3 0.0 collective-permute-done.7.from_2
  21.3 1.3 %collective-permute-done.8.from_3 = bf16[40,1024]{1,0:T(8,128)(2,1)S(1)} collective-permute-done((bf16[40,1024]{1,0:T(8,128)(2,1)S(1)}, bf16[40,1024]{1,0:T(8,128)(2,1)S(1)}, u32[]{:S(2)}, u32[]{:S(2)}) %collective-permute-start.8) | collective-permute-done | bytes 81952 | tf_op jit(solution)/shard_map/ppermute | solution.py:332
  22.6 0.7 %shard_map.100 = (bf16[128,1792]{1,0:T(8,128)(2,1)S(1)}, bf16[128,1792]{1,0:T(8,128)(2,1)S(1)}) custom-call(bf16[40,1024]{1,0:T(8,128)(2,1)S(1)} %get-tuple-element.32.own, bf16[40,1024]{1,0:T(8,128)(2,1)S(1)} %collective-permute-done.6.from_1, bf16[40,1024]{1,0:T(8,128)(2,1)S(1)} %collective-permute-done.7.from_2, ...), custom_call_target="tpu_custom_call" | custom-call | bytes 458752 | tf_op jit(solution)/shard_map/pallas_call | solution.py:307
  23.2 0.1 collective-permute-start.9
  23.3 1.3 %collective-permute-start.3 = (bf16[40,896]{1,0:T(8,128)(2,1)S(1)}, bf16[40,896]{1,0:T(8,128)(2,1)S(1)}, u32[]{:S(2)}, u32[]{:S(2)}) collective-permute-start(bf16[40,896]{1,0:T(8,128)(2,1)S(1)} %get-tuple-element.29), channel_id=1, source_target_pairs={{0,8},{1,9},{2,10},{3,11},{4,12},{5,13},{6,14},{7,15},{8,0},{9,1},... | collective-permute-start | bytes 215048 | tf_op jit(solution)/shard_map/ppermute | solution.py:332
  24.6 0.5 %collective-permute-done.9.other = bf16[128,1792]{1,0:T(8,128)(2,1)S(1)} collective-permute-done((bf16[128,1792]{1,0:T(8,128)(2,1)S(1)}, bf16[128,1792]{1,0:T(8,128)(2,1)S(1)}, u32[]{:S(2)}, u32[]{:S(2)}) %collective-permute-start.9) | collective-permute-done | bytes 458784 | tf_op jit(solution)/shard_map/ppermute | solution.py:332
  25.1 0.1 shard_map.101
  25.2 1.3 %collective-permute-start.10 = (bf16[32,1792]{1,0:T(8,128)(2,1)S(1)}, bf16[32,1792]{1,0:T(8,128)(2,1)S(1)}, u32[]{:S(2)}, u32[]{:S(2)}) collective-permute-start(bf16[32,1792]{1,0:T(8,128)(2,1)S(1)} %get-tuple-element.39), channel_id=1, source_target_pairs={{0,8},{1,9},{2,10},{3,11},{4,12},{5,13},{6,14},{7,15},{8,0},{9,1},... | collective-permute-start | bytes 344072 | tf_op jit(solution)/shard_map/ppermute | solution.py:332
  26.5 0.0 collective-permute-start.11
  26.5 2.3 %collective-permute-start.12 = (bf16[32,1792]{1,0:T(8,128)(2,1)S(1)}, bf16[32,1792]{1,0:T(8,128)(2,1)S(1)}, u32[]{:S(2)}, u32[]{:S(2)}) collective-permute-start(bf16[32,1792]{1,0:T(8,128)(2,1)S(1)} %get-tuple-element.41), channel_id=1, source_target_pairs={{0,10},{1,11},{2,8},{3,9},{4,14},{5,15},{6,12},{7,13},{8,2},{9,3},... | collective-permute-start | bytes 344072 | tf_op jit(solution)/shard_map/ppermute | solution.py:332
  28.8 0.8 %collective-permute-start.4 = (bf16[40,896]{1,0:T(8,128)(2,1)S(1)}, bf16[40,896]{1,0:T(8,128)(2,1)S(1)}, u32[]{:S(2)}, u32[]{:S(2)}) collective-permute-start(bf16[40,896]{1,0:T(8,128)(2,1)S(1)} %get-tuple-element.30), channel_id=1, source_target_pairs={{0,16},{1,17},{2,18},{3,19},{4,20},{5,21},{6,22},{7,23},{8,24},{9,... | collective-permute-start | bytes 215048 | tf_op jit(solution)/shard_map/ppermute | solution.py:332
  29.6 0.0 collective-permute-done.3.from_x
  29.6 1.8 %collective-permute-start.5 = (bf16[40,896]{1,0:T(8,128)(2,1)S(1)}, bf16[40,896]{1,0:T(8,128)(2,1)S(1)}, u32[]{:S(2)}, u32[]{:S(2)}) collective-permute-start(bf16[40,896]{1,0:T(8,128)(2,1)S(1)} %get-tuple-element.31), channel_id=1, source_target_pairs={{0,24},{1,25},{2,26},{3,27},{4,28},{5,29},{6,30},{7,31},{8,16},{9,... | collective-permute-start | bytes 215048 | tf_op jit(solution)/shard_map/ppermute | solution.py:332
  31.5 2.1 %collective-permute-done.4.from_y = bf16[40,896]{1,0:T(8,128)(2,1)S(1)} collective-permute-done((bf16[40,896]{1,0:T(8,128)(2,1)S(1)}, bf16[40,896]{1,0:T(8,128)(2,1)S(1)}, u32[]{:S(2)}, u32[]{:S(2)}) %collective-permute-start.4) | collective-permute-done | bytes 71712 | tf_op jit(solution)/shard_map/ppermute | solution.py:332
  33.6 1.9 %collective-permute-done.5.from_xy = bf16[40,896]{1,0:T(8,128)(2,1)S(1)} collective-permute-done((bf16[40,896]{1,0:T(8,128)(2,1)S(1)}, bf16[40,896]{1,0:T(8,128)(2,1)S(1)}, u32[]{:S(2)}, u32[]{:S(2)}) %collective-permute-start.5) | collective-permute-done | bytes 71712 | tf_op jit(solution)/shard_map/ppermute | solution.py:332
  35.5 1.5 %shard_map.98 = bf16[1,64,7168]{2,1,0:T(8,128)(2,1)} custom-call(s32[8,128]{1,0:T(8,128)S(1)} %get-tuple-element.22.names, bf16[40,896]{1,0:T(8,128)(2,1)S(1)} %get-tuple-element.28.own.after, bf16[40,896]{1,0:T(8,128)(2,1)S(1)} %collective-permute-done.3.from_x, bf16[40,896]{1,0:T(8,128)(2,1)S(1)} %collective-permute-done.4.from_y, ...), custom_call_target="tpu_custom_call" | custom-call | bytes 917504 | tf_op jit(solution)/shard_map/pallas_call | solution.py:307
  37.0 0.0 collective-permute-done.10.from_x
  37.0 0.0 collective-permute-done.11.from_z
  37.0 0.0 collective-permute-done.12.from_xz
  37.0 1.0 %shard_map.102 = f32[1,32,7168]{2,1,0:T(8,128)} custom-call(bf16[32,1792]{1,0:T(8,128)(2,1)S(1)} %get-tuple-element.38.own, bf16[32,1792]{1,0:T(8,128)(2,1)S(1)} %collective-permute-done.10.from_x, bf16[32,1792]{1,0:T(8,128)(2,1)S(1)} %collective-permute-done.11.from_z, bf16[32,1792]{1,0:T(8,128)(2,1)S(1)} %collective-permute-done.12.from_xz), custom_call_target="tpu_custom_call" | custom-call | bytes 1048576 | tf_op jit(solution)/shard_map/pallas_call | solution.py:307
Async XLA Ops:
  2.4 9.3 %collective-permute-start = (bf16[40,1024]{1,0:T(8,128)(2,1)S(1)}, bf16[40,1024]{1,0:T(8,128)(2,1)S(1)}, u32[]{:S(2)}, u32[]{:S(2)}) collective-permute-start(bf16[40,1024]{1,0:T(8,128)(2,1)S(1)} %get-tuple-element.23.own), channel_id=1, source_target_pairs={{0,8},{1,9},{2,10},{3,11},{4,12},{5,13},{6,14},{7,15},{8,0},{9,1},... | collective-permute-start | bytes 245768 | tf_op jit(solution)/shard_map/ppermute | solution.py:332
  5.4 5.5 %collective-permute-start.2 = (bf16[40,896]{1,0:T(8,128)(2,1)S(1)}, bf16[40,896]{1,0:T(8,128)(2,1)S(1)}, u32[]{:S(2)}, u32[]{:S(2)}) collective-permute-start(bf16[40,896]{1,0:T(8,128)(2,1)S(1)} %get-tuple-element.24.after), channel_id=1, source_target_pairs={{0,24},{1,25},{2,26},{3,27},{4,28},{5,29},{6,30},{7,31},{8,16},{9,... | collective-permute-start | bytes 215048 | tf_op jit(solution)/shard_map/ppermute | solution.py:332
  6.9 4.8 %collective-permute-start.1 = (bf16[40,896]{1,0:T(8,128)(2,1)S(1)}, bf16[40,896]{1,0:T(8,128)(2,1)S(1)}, u32[]{:S(2)}, u32[]{:S(2)}) collective-permute-start(bf16[40,896]{1,0:T(8,128)(2,1)S(1)} %get-tuple-element.24.after), channel_id=1, source_target_pairs={{0,16},{1,17},{2,18},{3,19},{4,20},{5,21},{6,22},{7,23},{8,24},{9,... | collective-permute-start | bytes 215048 | tf_op jit(solution)/shard_map/ppermute | solution.py:332
  12.1 9.2 %collective-permute-start.6 = (bf16[40,1024]{1,0:T(8,128)(2,1)S(1)}, bf16[40,1024]{1,0:T(8,128)(2,1)S(1)}, u32[]{:S(2)}, u32[]{:S(2)}) collective-permute-start(bf16[40,1024]{1,0:T(8,128)(2,1)S(1)} %get-tuple-element.33), channel_id=1, source_target_pairs={{0,2},{1,3},{2,0},{3,1},{4,6},{5,7},{6,4},{7,5},{8,10},{9,11},{10,... | collective-permute-start | bytes 245768 | tf_op jit(solution)/shard_map/ppermute | solution.py:332
  13.7 7.6 %collective-permute-start.7 = (bf16[40,1024]{1,0:T(8,128)(2,1)S(1)}, bf16[40,1024]{1,0:T(8,128)(2,1)S(1)}, u32[]{:S(2)}, u32[]{:S(2)}) collective-permute-start(bf16[40,1024]{1,0:T(8,128)(2,1)S(1)} %get-tuple-element.34), channel_id=1, source_target_pairs={{0,4},{1,5},{2,6},{3,7},{4,0},{5,1},{6,2},{7,3},{8,12},{9,13},{10,... | collective-permute-start | bytes 245768 | tf_op jit(solution)/shard_map/ppermute | solution.py:332
  16.3 6.3 %collective-permute-start.8 = (bf16[40,1024]{1,0:T(8,128)(2,1)S(1)}, bf16[40,1024]{1,0:T(8,128)(2,1)S(1)}, u32[]{:S(2)}, u32[]{:S(2)}) collective-permute-start(bf16[40,1024]{1,0:T(8,128)(2,1)S(1)} %get-tuple-element.35), channel_id=1, source_target_pairs={{0,6},{1,7},{2,4},{3,5},{4,2},{5,3},{6,0},{7,1},{8,14},{9,15},{10,... | collective-permute-start | bytes 245768 | tf_op jit(solution)/shard_map/ppermute | solution.py:332
  23.2 1.9 %collective-permute-start.9 = (bf16[128,1792]{1,0:T(8,128)(2,1)S(1)}, bf16[128,1792]{1,0:T(8,128)(2,1)S(1)}, u32[]{:S(2)}, u32[]{:S(2)}) collective-permute-start(bf16[128,1792]{1,0:T(8,128)(2,1)S(1)} %get-tuple-element.37), channel_id=1, source_target_pairs={{0,1},{1,0},{2,3},{3,2},{4,5},{5,4},{6,7},{7,6},{8,9},{9,8},{10,11... | collective-permute-start | bytes 1376264 | tf_op jit(solution)/shard_map/ppermute | solution.py:332
  23.3 6.3 %collective-permute-start.3 = (bf16[40,896]{1,0:T(8,128)(2,1)S(1)}, bf16[40,896]{1,0:T(8,128)(2,1)S(1)}, u32[]{:S(2)}, u32[]{:S(2)}) collective-permute-start(bf16[40,896]{1,0:T(8,128)(2,1)S(1)} %get-tuple-element.29), channel_id=1, source_target_pairs={{0,8},{1,9},{2,10},{3,11},{4,12},{5,13},{6,14},{7,15},{8,0},{9,1},... | collective-permute-start | bytes 215048 | tf_op jit(solution)/shard_map/ppermute | solution.py:332
  25.2 11.8 %collective-permute-start.10 = (bf16[32,1792]{1,0:T(8,128)(2,1)S(1)}, bf16[32,1792]{1,0:T(8,128)(2,1)S(1)}, u32[]{:S(2)}, u32[]{:S(2)}) collective-permute-start(bf16[32,1792]{1,0:T(8,128)(2,1)S(1)} %get-tuple-element.39), channel_id=1, source_target_pairs={{0,8},{1,9},{2,10},{3,11},{4,12},{5,13},{6,14},{7,15},{8,0},{9,1},... | collective-permute-start | bytes 344072 | tf_op jit(solution)/shard_map/ppermute | solution.py:332
  26.5 10.5 %collective-permute-start.11 = (bf16[32,1792]{1,0:T(8,128)(2,1)S(1)}, bf16[32,1792]{1,0:T(8,128)(2,1)S(1)}, u32[]{:S(2)}, u32[]{:S(2)}) collective-permute-start(bf16[32,1792]{1,0:T(8,128)(2,1)S(1)} %get-tuple-element.40), channel_id=1, source_target_pairs={{0,2},{1,3},{2,0},{3,1},{4,6},{5,7},{6,4},{7,5},{8,10},{9,11},{10,... | collective-permute-start | bytes 344072 | tf_op jit(solution)/shard_map/ppermute | solution.py:332
  26.5 10.5 %collective-permute-start.12 = (bf16[32,1792]{1,0:T(8,128)(2,1)S(1)}, bf16[32,1792]{1,0:T(8,128)(2,1)S(1)}, u32[]{:S(2)}, u32[]{:S(2)}) collective-permute-start(bf16[32,1792]{1,0:T(8,128)(2,1)S(1)} %get-tuple-element.41), channel_id=1, source_target_pairs={{0,10},{1,11},{2,8},{3,9},{4,14},{5,15},{6,12},{7,13},{8,2},{9,3},... | collective-permute-start | bytes 344072 | tf_op jit(solution)/shard_map/ppermute | solution.py:332
  28.8 4.8 %collective-permute-start.4 = (bf16[40,896]{1,0:T(8,128)(2,1)S(1)}, bf16[40,896]{1,0:T(8,128)(2,1)S(1)}, u32[]{:S(2)}, u32[]{:S(2)}) collective-permute-start(bf16[40,896]{1,0:T(8,128)(2,1)S(1)} %get-tuple-element.30), channel_id=1, source_target_pairs={{0,16},{1,17},{2,18},{3,19},{4,20},{5,21},{6,22},{7,23},{8,24},{9,... | collective-permute-start | bytes 215048 | tf_op jit(solution)/shard_map/ppermute | solution.py:332
  29.6 5.8 %collective-permute-start.5 = (bf16[40,896]{1,0:T(8,128)(2,1)S(1)}, bf16[40,896]{1,0:T(8,128)(2,1)S(1)}, u32[]{:S(2)}, u32[]{:S(2)}) collective-permute-start(bf16[40,896]{1,0:T(8,128)(2,1)S(1)} %get-tuple-element.31), channel_id=1, source_target_pairs={{0,24},{1,25},{2,26},{3,27},{4,28},{5,29},{6,30},{7,31},{8,16},{9,... | collective-permute-start | bytes 215048 | tf_op jit(solution)/shard_map/ppermute | solution.py:332

commit v3 on v2

--- a/solution.py
+++ b/solution.py
@@ -198,7 +198,7 @@
 
 
 def expert_kernel(
-    own, from_x, from_y, from_xy, down, gate, up, ret_own, ret_x, ret_y, ret_xy, stack
+    own, from_x, from_y, from_xy, down, gate, up, ret_own, ret_y, ret_x, stack
 ):
     count, piece_cols = from_y.shape
     cap = count // PIECES
@@ -229,26 +229,23 @@
     nq = quotient(n, cap, count)
     n_slot = n - cap * nq
     m_piece, m_slot = m // pad, m % pad
-    for k, ref in enumerate((ret_own, ret_x, ret_y, ret_xy)):
+    back = []
+    for k in range(4):
         match = (m_piece == nq) & (m_slot == (source ^ k) * cap + n_slot)
-        ref[...] = dot(hot(match), stack[...]).astype(BF16)
-
-
-def combine_kernel(names, own, from_x, from_y, from_xy, out):
-    count, piece_cols = own.shape
-    cap = count // PIECES
-    tokens = out.shape[1]
-    near = (own[...].astype(F32) + from_x[...].astype(F32)).astype(BF16)
-    far = (from_y[...].astype(F32) + from_xy[...].astype(F32)).astype(BF16)
-    token, lane = iota((tokens, count), 0), iota((tokens, count), 1)
-    piece = quotient(lane, cap, count)
-    match = [token == names[other : other + 1, :count] for other in range(2)]
-    for j in range(PIECES):
-        total = dot(hot(match[0] & (piece == j)), near) + dot(hot(match[1] & (piece == j)), far)
-        out[0, :, j * piece_cols : (j + 1) * piece_cols] = total.astype(BF16)
-
-
-def product_kernel(scale, own, from_1, from_2, from_3, after, keep, send):
+        back.append(dot(hot(match), stack[...]))
+    ret_own[...] = back[0].astype(BF16)
+    ret_y[...] = back[2].astype(BF16)
+    ret_x[...] = jnp.concatenate([back[1], back[3]], 0).astype(BF16)
+
+
+def merge_kernel(ret_own, ret_y, from_x, near, far):
+    other = from_x[...].astype(F32)
+    count = near.shape[0]
+    near[...] = (ret_own[...].astype(F32) + other[:count]).astype(BF16)
+    far[...] = (ret_y[...].astype(F32) + other[count:]).astype(BF16)
+
+
+def product_kernel(scale, own, from_2, from_3, from_1, after, keep, send):
     count = own.shape[0]
     cap = count // PIECES
     slots = 4 * cap
@@ -290,25 +287,49 @@
         out[...] = (mine[at, :].astype(F32) + other[at, :].astype(F32)).astype(BF16)
 
 
-def join_kernel(own, from_x, from_z, from_xz, out):
+def finish_kernel(
+    own, from_x, from_z, from_xz, names, near, far, tokens_hbm, down_hbm, tokens_out, down_out, sems
+):
     cols = own.shape[1]
+    count, piece_cols = near.shape
+    cap = count // PIECES
+    tokens = tokens_out.shape[1]
     _, loc, zb, _, _ = place()
+    copies = []
+
+    def send(source, target):
+        copy = pltpu.make_async_copy(source, target, sems.at[len(copies)])
+        copy.start()
+        copies.append(copy)
+
     for k, ref in enumerate((own, from_z, from_x, from_xz)):
-        at = pl.ds(pl.multiple_of(((2 * loc + zb) ^ k) * cols, cols), cols)
-        out[0, :, at] = ref[...].astype(F32)
+        start = pl.multiple_of(((2 * loc + zb) ^ k) * cols, cols)
+        down_out[k] = ref[...].astype(F32)
+        send(down_out.at[k], down_hbm.at[0, :, pl.ds(start, cols)])
+    token, lane = iota((tokens, count), 0), iota((tokens, count), 1)
+    piece = quotient(lane, cap, count)
+    match = [token == names[other : other + 1, :count] for other in range(2)]
+    for j in range(PIECES):
+        total = dot(hot(match[0] & (piece == j)), near[...]) + dot(
+            hot(match[1] & (piece == j)), far[...]
+        )
+        tokens_out[j] = total.astype(BF16)
+        send(tokens_out.at[j], tokens_hbm.at[0, :, pl.ds(j * piece_cols, piece_cols)])
+    for copy in copies:
+        copy.wait()
 
 
 VM = pl.BlockSpec(memory_space=pltpu.VMEM)
 ANY = pl.BlockSpec(memory_space=pl.ANY)
 
 
-def call(kernel, outs, args, specs=None, scratch=(), flops=0, nbytes=0):
+def call(kernel, outs, args, specs=None, outs_specs=None, scratch=(), flops=0, nbytes=0):
     out_shape = tuple(jax.ShapeDtypeStruct(shape, dtype) for shape, dtype in outs)
     result = pl.pallas_call(
         kernel,
         out_shape=out_shape,
         in_specs=specs or [VM] * len(args),
-        out_specs=tuple([VM] * len(outs)),
+        out_specs=tuple(outs_specs or [VM] * len(outs)),
         scratch_shapes=list(scratch),
         compiler_params=pltpu.CompilerParams(vmem_limit_bytes=16 * 1024 * 1024),
         cost_estimate=pl.CostEstimate(flops=flops, bytes_accessed=nbytes, transcendentals=0),
@@ -357,9 +378,9 @@
         + [pltpu.SemaphoreType.DMA((5,))],
         nbytes=tokens * model * 2,
     )
+    from_xy = swap(far, group_flip=1, loc_flip=1)
+    from_y = swap(far, group_flip=1)
     from_x = swap(near, loc_flip=1)
-    from_y = swap(far, group_flip=1)
-    from_xy = swap(far, group_flip=1, loc_flip=1)
     arrived = (near, from_x, from_y, from_xy)
     held = (down_weight, up_weight, gate_saved)
     down, up, gate = call(
@@ -374,43 +395,47 @@
     mine, to_1, to_2, to_3 = call(
         spread_kernel, [message] * 4, arrived + (gate,), [VM] * 4 + [ANY], nbytes=count * model
     )
-    from_1 = swap(to_1, dp_flip=2)
     from_2 = swap(to_2, dp_flip=4)
     from_3 = swap(to_3, dp_flip=6)
+    from_1 = swap(to_1, dp_flip=2)
     pad = -(-4 * cap // 16) * 16
-    ret_own, ret_x, ret_y, ret_xy = call(
+    part = ((count, piece_cols), BF16)
+    ret_own, ret_y, ret_x = call(
         expert_kernel,
-        [((count, piece_cols), BF16)] * 4,
+        [part, part, ((2 * count, piece_cols), BF16)],
         arrived + (down, gate, up),
         scratch=[pltpu.VMEM((PIECES * pad, piece_cols), BF16)],
         flops=4 * pad * model * hidden_dev,
         nbytes=4 * model * hidden_dev,
     )
     back_x = swap(ret_x, loc_flip=1)
-    back_y = swap(ret_y, group_flip=1)
-    back_xy = swap(ret_xy, group_flip=1, loc_flip=1)
-    (input_grad,) = call(
-        combine_kernel,
-        [((1, tokens, model), BF16)],
-        (names, ret_own, back_x, back_y, back_xy),
-        nbytes=2 * tokens * model,
-    )
+    near_sum, far_sum = call(merge_kernel, [part] * 2, (ret_own, ret_y, back_x), nbytes=1 << 18)
+    back_y = swap(far_sum, group_flip=1)
     block = ((4 * rows_dev, 2 * piece_cols), BF16)
     keep, send = call(
         functools.partial(product_kernel, 1.0 / replicas),
         [block] * 2,
-        (mine, from_1, from_2, from_3, ret_own),
+        (mine, from_2, from_3, from_1, ret_own),
         [VM] * 4 + [ANY],
         nbytes=16 * rows_dev * piece_cols,
     )
     other = swap(send, dp_flip=1)
     block = ((rows_dev, 2 * piece_cols), BF16)
     own, to_x, to_z, to_xz = call(add_kernel, [block] * 4, (keep, other), nbytes=1 << 20)
+    got_xz = swap(to_xz, loc_flip=1, dp_flip=2)
+    got_z = swap(to_z, dp_flip=2)
     got_x = swap(to_x, loc_flip=1)
-    got_z = swap(to_z, dp_flip=2)
-    got_xz = swap(to_xz, loc_flip=1, dp_flip=2)
-    (down_grad,) = call(
-        join_kernel, [((1, rows_dev, model), F32)], (own, got_x, got_z, got_xz), nbytes=1 << 20
+    input_grad, down_grad = call(
+        finish_kernel,
+        [((1, tokens, model), BF16), ((1, rows_dev, model), F32)],
+        (own, got_x, got_z, got_xz, names, near_sum, back_y),
+        outs_specs=[ANY] * 2,
+        scratch=[
+            pltpu.VMEM((PIECES, tokens, piece_cols), BF16),
+            pltpu.VMEM((4, rows_dev, 2 * piece_cols), F32),
+            pltpu.SemaphoreType.DMA((4 + PIECES,)),
+        ],
+        nbytes=4 << 20,
     )
     return (input_grad, down_grad)
 

time: 38.2 us -> 35.1 us (0.919)
  starting transfers between devices: 16.6 us -> 14.4 us
  Pallas kernels: 13.4 us -> 12.4 us
    ppermute x13 -> x12, starting transfers between devices: 16.6 us -> 14.4 us  [swap(): return lax.ppermute(value, AXES, pairs)]
    pallas_call x8, Pallas kernels: 13.4 us -> 12.4 us  [call(): pl.pallas_call(kernel, out_shape=out_shape, in_specs=specs or [VM] * len(...]
    ppermute x13 -> x12, waiting for transfers between devices: 7.34 us -> 7.5 us  [swap(): return lax.ppermute(value, AXES, pairs)]
  transfers between devices with their start and end apart: 13 -> 12, of which waited for: 6 -> 7; matrix products, arithmetic and copies ran while one was open for 0% -> 0% of each run, Pallas kernels for 25% -> 23%
where the time goes in v3:
time: 35.1 us; the launch traced here: 34.9 us
  starting transfers between devices  14.4 us (41%)
  Pallas kernels  12.4 us (35%)
  waiting for transfers between devices  7.5 us (21%)
  between operations  0.7 us (2%)
    ppermute x12, starting transfers between devices, swap(): return lax.ppermute(value, AXES, pairs)  14.4 us
    pallas_call x8, Pallas kernels, call(): pl.pallas_call(kernel, out_shape=out_shape, in_specs=specs or [VM] * len(...  12.4 us
    ppermute x12, waiting for transfers between devices, swap(): return lax.ppermute(value, AXES, pairs)  7.5 us
  transfers between devices with their start and end apart: 12, of which 7 were waited for; matrix products, arithmetic and copies ran while one was open for 0% of the time, Pallas kernels for 23%

profile of v3, /device:TPU:0, one launch (start us, length us, event | category | flops | bytes accessed | tf_op | source)
XLA Modules:
  0.0 34.9 jit_solution(16418609811076052618)
XLA Ops:
  0.6 1.8 %shard_map.95 = (bf16[40,1024]{1,0:T(8,128)(2,1)S(1)}, bf16[40,896]{1,0:T(8,128)(2,1)S(1)}, s32[8,128]{1,0:T(8,128)S(1)}) custom-call(s32[1,1,2,5]{3,2,1,0:T(2,128)} %tok_hbm.1, s32[1,1,2]{2,1,0:T(1,128)} %cnt_hbm.1, bf16[1,1,2,5]{3,2,1,0:T(2,128)(2,1)} %weight_hbm.1, bf16[1,64,7168]{2,1,0:T(8,128)(2,1)} %rows_hbm.1, bf16[1,1,20,256]{3,2,1,0:T(8,128)(2,1)} %hidden_hbm.1), custom_call_target="tpu_custom_call" | custom-call | bytes 917504 | tf_op jit(solution)/shard_map/pallas_call | solution.py:328
  2.4 3.0 %collective-permute-start = (bf16[40,1024]{1,0:T(8,128)(2,1)S(1)}, bf16[40,1024]{1,0:T(8,128)(2,1)S(1)}, u32[]{:S(2)}, u32[]{:S(2)}) collective-permute-start(bf16[40,1024]{1,0:T(8,128)(2,1)S(1)} %get-tuple-element.23.own), channel_id=1, source_target_pairs={{0,8},{1,9},{2,10},{3,11},{4,12},{5,13},{6,14},{7,15},{8,0},{9,1},... | collective-permute-start | bytes 245768 | tf_op jit(solution)/shard_map/ppermute | solution.py:353
  5.4 1.5 %collective-permute-start.2 = (bf16[40,896]{1,0:T(8,128)(2,1)S(1)}, bf16[40,896]{1,0:T(8,128)(2,1)S(1)}, u32[]{:S(2)}, u32[]{:S(2)}) collective-permute-start(bf16[40,896]{1,0:T(8,128)(2,1)S(1)} %get-tuple-element.24.after), channel_id=1, source_target_pairs={{0,24},{1,25},{2,26},{3,27},{4,28},{5,29},{6,30},{7,31},{8,16},{9,... | collective-permute-start | bytes 215048 | tf_op jit(solution)/shard_map/ppermute | solution.py:353
  6.9 0.1 collective-permute-start.1
  7.0 3.2 %shard_map.96 = (bf16[1,256,7168]{2,1,0:T(8,128)(2,1)S(1)}, bf16[1,7168,256]{2,1,0:T(8,128)(2,1)S(1)}, bf16[1,1,20,256]{3,2,1,0:T(8,128)(2,1)S(1)}) custom-call(bf16[1,256,7168]{2,1,0:T(8,128)(2,1)} %down_hbm.1, bf16[1,7168,256]{2,1,0:T(8,128)(2,1)} %up_hbm.1, bf16[1,1,20,256]{3,2,1,0:T(8,128)(2,1)} %gate_hbm.1, bf16[40,896]{1,0:T(8,128)(2,1)S(1)} %get-tuple-element.24.after), custom_call_target="tpu_custom_call" | custom-call | bytes 14680064 | tf_op jit(solution)/shard_map/pallas_call | solution.py:328
  10.2 0.8 %collective-permute-done.2.from_xy = bf16[40,896]{1,0:T(8,128)(2,1)S(1)} collective-permute-done((bf16[40,896]{1,0:T(8,128)(2,1)S(1)}, bf16[40,896]{1,0:T(8,128)(2,1)S(1)}, u32[]{:S(2)}, u32[]{:S(2)}) %collective-permute-start.2) | collective-permute-done | bytes 71712 | tf_op jit(solution)/shard_map/ppermute | solution.py:353
  11.0 0.7 %collective-permute-done.1.from_y = bf16[40,896]{1,0:T(8,128)(2,1)S(1)} collective-permute-done((bf16[40,896]{1,0:T(8,128)(2,1)S(1)}, bf16[40,896]{1,0:T(8,128)(2,1)S(1)}, u32[]{:S(2)}, u32[]{:S(2)}) %collective-permute-start.1) | collective-permute-done | bytes 71712 | tf_op jit(solution)/shard_map/ppermute | solution.py:353
  11.7 0.0 collective-permute-done.from_x
  11.7 0.3 shard_map.97
  12.1 2.7 %collective-permute-start.3 = (bf16[40,1024]{1,0:T(8,128)(2,1)S(1)}, bf16[40,1024]{1,0:T(8,128)(2,1)S(1)}, u32[]{:S(2)}, u32[]{:S(2)}) collective-permute-start(bf16[40,1024]{1,0:T(8,128)(2,1)S(1)} %get-tuple-element.27), channel_id=1, source_target_pairs={{0,4},{1,5},{2,6},{3,7},{4,0},{5,1},{6,2},{7,3},{8,12},{9,13},{10,... | collective-permute-start | bytes 245768 | tf_op jit(solution)/shard_map/ppermute | solution.py:353
  14.7 1.3 %collective-permute-start.4 = (bf16[40,1024]{1,0:T(8,128)(2,1)S(1)}, bf16[40,1024]{1,0:T(8,128)(2,1)S(1)}, u32[]{:S(2)}, u32[]{:S(2)}) collective-permute-start(bf16[40,1024]{1,0:T(8,128)(2,1)S(1)} %get-tuple-element.28), channel_id=1, source_target_pairs={{0,6},{1,7},{2,4},{3,5},{4,2},{5,3},{6,0},{7,1},{8,14},{9,15},{10,... | collective-permute-start | bytes 245768 | tf_op jit(solution)/shard_map/ppermute | solution.py:353
  16.1 0.2 collective-permute-start.5
  16.3 4.8 %shard_map.98 = (bf16[40,896]{1,0:T(8,128)(2,1)S(1)}, bf16[40,896]{1,0:T(8,128)(2,1)S(1)}, bf16[80,896]{1,0:T(8,128)(2,1)S(1)}) custom-call(bf16[40,1024]{1,0:T(8,128)(2,1)S(1)} %get-tuple-element.23.own, bf16[40,1024]{1,0:T(8,128)(2,1)S(1)} %collective-permute-done.from_x, bf16[40,896]{1,0:T(8,128)(2,1)S(1)} %collective-permute-done.1.from_y, ...), custom_call_target="tpu_custom_call" | custom-call | flops 234881024 | bytes 7340032 | tf_op jit(solution)/shard_map/pallas_call | solution.py:328
  21.1 0.0 collective-permute-done.3.from_2
  21.1 0.1 collective-permute-done.4.from_3
  21.1 0.5 %collective-permute-done.5.from_1 = bf16[40,1024]{1,0:T(8,128)(2,1)S(1)} collective-permute-done((bf16[40,1024]{1,0:T(8,128)(2,1)S(1)}, bf16[40,1024]{1,0:T(8,128)(2,1)S(1)}, u32[]{:S(2)}, u32[]{:S(2)}) %collective-permute-start.5) | collective-permute-done | bytes 81952 | tf_op jit(solution)/shard_map/ppermute | solution.py:353
  21.6 0.7 %shard_map.99 = (bf16[128,1792]{1,0:T(8,128)(2,1)S(1)}, bf16[128,1792]{1,0:T(8,128)(2,1)S(1)}) custom-call(bf16[40,1024]{1,0:T(8,128)(2,1)S(1)} %get-tuple-element.26.own, bf16[40,1024]{1,0:T(8,128)(2,1)S(1)} %collective-permute-done.3.from_2, bf16[40,1024]{1,0:T(8,128)(2,1)S(1)} %collective-permute-done.4.from_3, ...), custom_call_target="tpu_custom_call" | custom-call | bytes 458752 | tf_op jit(solution)/shard_map/pallas_call | solution.py:328
  22.3 0.1 collective-permute-start.6
  22.4 1.3 %collective-permute-start.10 = (bf16[80,896]{1,0:T(8,128)(2,1)S(1)}, bf16[80,896]{1,0:T(8,128)(2,1)S(1)}, u32[]{:S(2)}, u32[]{:S(2)}) collective-permute-start(bf16[80,896]{1,0:T(8,128)(2,1)S(1)} %get-tuple-element.41), channel_id=1, source_target_pairs={{0,8},{1,9},{2,10},{3,11},{4,12},{5,13},{6,14},{7,15},{8,0},{9,1},... | collective-permute-start | bytes 430088 | tf_op jit(solution)/shard_map/ppermute | solution.py:353
  23.6 0.5 %collective-permute-done.6.other = bf16[128,1792]{1,0:T(8,128)(2,1)S(1)} collective-permute-done((bf16[128,1792]{1,0:T(8,128)(2,1)S(1)}, bf16[128,1792]{1,0:T(8,128)(2,1)S(1)}, u32[]{:S(2)}, u32[]{:S(2)}) %collective-permute-start.6) | collective-permute-done | bytes 458784 | tf_op jit(solution)/shard_map/ppermute | solution.py:353
  24.2 0.1 shard_map.100
  24.3 1.3 %collective-permute-start.7 = (bf16[32,1792]{1,0:T(8,128)(2,1)S(1)}, bf16[32,1792]{1,0:T(8,128)(2,1)S(1)}, u32[]{:S(2)}, u32[]{:S(2)}) collective-permute-start(bf16[32,1792]{1,0:T(8,128)(2,1)S(1)} %get-tuple-element.36), channel_id=1, source_target_pairs={{0,8},{1,9},{2,10},{3,11},{4,12},{5,13},{6,14},{7,15},{8,0},{9,1},... | collective-permute-start | bytes 344072 | tf_op jit(solution)/shard_map/ppermute | solution.py:353
  25.6 1.3 %collective-permute-start.8 = (bf16[32,1792]{1,0:T(8,128)(2,1)S(1)}, bf16[32,1792]{1,0:T(8,128)(2,1)S(1)}, u32[]{:S(2)}, u32[]{:S(2)}) collective-permute-start(bf16[32,1792]{1,0:T(8,128)(2,1)S(1)} %get-tuple-element.37), channel_id=1, source_target_pairs={{0,2},{1,3},{2,0},{3,1},{4,6},{5,7},{6,4},{7,5},{8,10},{9,11},{10,... | collective-permute-start | bytes 344072 | tf_op jit(solution)/shard_map/ppermute | solution.py:353
  26.8 1.0 %collective-permute-start.9 = (bf16[32,1792]{1,0:T(8,128)(2,1)S(1)}, bf16[32,1792]{1,0:T(8,128)(2,1)S(1)}, u32[]{:S(2)}, u32[]{:S(2)}) collective-permute-start(bf16[32,1792]{1,0:T(8,128)(2,1)S(1)} %get-tuple-element.38), channel_id=1, source_target_pairs={{0,10},{1,11},{2,8},{3,9},{4,14},{5,15},{6,12},{7,13},{8,2},{9,3},... | collective-permute-start | bytes 344072 | tf_op jit(solution)/shard_map/ppermute | solution.py:353
  27.8 1.2 %collective-permute-done.10.from_x = bf16[80,896]{1,0:T(8,128)(2,1)S(1)} collective-permute-done((bf16[80,896]{1,0:T(8,128)(2,1)S(1)}, bf16[80,896]{1,0:T(8,128)(2,1)S(1)}, u32[]{:S(2)}, u32[]{:S(2)}) %collective-permute-start.10) | collective-permute-done | bytes 143392 | tf_op jit(solution)/shard_map/ppermute | solution.py:353
  29.0 0.7 %collective-permute-start.11 = (bf16[40,896]{1,0:T(8,128)(2,1)S(1)}, bf16[40,896]{1,0:T(8,128)(2,1)S(1)}, u32[]{:S(2)}, u32[]{:S(2)}) collective-permute-start(bf16[40,896]{1,0:T(8,128)(2,1)S(1)} %get-tuple-element.43), channel_id=1, source_target_pairs={{0,16},{1,17},{2,18},{3,19},{4,20},{5,21},{6,22},{7,23},{8,24},{9,... | collective-permute-start | bytes 215048 | tf_op jit(solution)/shard_map/ppermute | solution.py:353
  29.7 3.7 %collective-permute-done.11.far = bf16[40,896]{1,0:T(8,128)(2,1)S(1)} collective-permute-done((bf16[40,896]{1,0:T(8,128)(2,1)S(1)}, bf16[40,896]{1,0:T(8,128)(2,1)S(1)}, u32[]{:S(2)}, u32[]{:S(2)}) %collective-permute-start.11) | collective-permute-done | bytes 71712 | tf_op jit(solution)/shard_map/ppermute | solution.py:353
  33.4 0.0 collective-permute-done.7.from_x
  33.5 0.0 collective-permute-done.8.from_z
  33.5 0.0 collective-permute-done.9.from_xz
  33.5 1.5 %shard_map.102 = (bf16[1,64,7168]{2,1,0:T(8,128)(2,1)}, f32[1,32,7168]{2,1,0:T(8,128)}) custom-call(bf16[32,1792]{1,0:T(8,128)(2,1)S(1)} %get-tuple-element.35.own, bf16[32,1792]{1,0:T(8,128)(2,1)S(1)} %collective-permute-done.7.from_x, bf16[32,1792]{1,0:T(8,128)(2,1)S(1)} %collective-permute-done.8.from_z, ...), custom_call_target="tpu_custom_call" | custom-call | bytes 4194304 | tf_op jit(solution)/shard_map/pallas_call | solution.py:328
  (1 shorter events, 0.0 us)
Async XLA Ops:
  2.4 9.3 %collective-permute-start = (bf16[40,1024]{1,0:T(8,128)(2,1)S(1)}, bf16[40,1024]{1,0:T(8,128)(2,1)S(1)}, u32[]{:S(2)}, u32[]{:S(2)}) collective-permute-start(bf16[40,1024]{1,0:T(8,128)(2,1)S(1)} %get-tuple-element.23.own), channel_id=1, source_target_pairs={{0,8},{1,9},{2,10},{3,11},{4,12},{5,13},{6,14},{7,15},{8,0},{9,1},... | collective-permute-start | bytes 245768 | tf_op jit(solution)/shard_map/ppermute | solution.py:353
  5.4 5.5 %collective-permute-start.2 = (bf16[40,896]{1,0:T(8,128)(2,1)S(1)}, bf16[40,896]{1,0:T(8,128)(2,1)S(1)}, u32[]{:S(2)}, u32[]{:S(2)}) collective-permute-start(bf16[40,896]{1,0:T(8,128)(2,1)S(1)} %get-tuple-element.24.after), channel_id=1, source_target_pairs={{0,24},{1,25},{2,26},{3,27},{4,28},{5,29},{6,30},{7,31},{8,16},{9,... | collective-permute-start | bytes 215048 | tf_op jit(solution)/shard_map/ppermute | solution.py:353
  6.9 4.8 %collective-permute-start.1 = (bf16[40,896]{1,0:T(8,128)(2,1)S(1)}, bf16[40,896]{1,0:T(8,128)(2,1)S(1)}, u32[]{:S(2)}, u32[]{:S(2)}) collective-permute-start(bf16[40,896]{1,0:T(8,128)(2,1)S(1)} %get-tuple-element.24.after), channel_id=1, source_target_pairs={{0,16},{1,17},{2,18},{3,19},{4,20},{5,21},{6,22},{7,23},{8,24},{9,... | collective-permute-start | bytes 215048 | tf_op jit(solution)/shard_map/ppermute | solution.py:353
  12.1 9.0 %collective-permute-start.3 = (bf16[40,1024]{1,0:T(8,128)(2,1)S(1)}, bf16[40,1024]{1,0:T(8,128)(2,1)S(1)}, u32[]{:S(2)}, u32[]{:S(2)}) collective-permute-start(bf16[40,1024]{1,0:T(8,128)(2,1)S(1)} %get-tuple-element.27), channel_id=1, source_target_pairs={{0,4},{1,5},{2,6},{3,7},{4,0},{5,1},{6,2},{7,3},{8,12},{9,13},{10,... | collective-permute-start | bytes 245768 | tf_op jit(solution)/shard_map/ppermute | solution.py:353
  14.7 6.4 %collective-permute-start.4 = (bf16[40,1024]{1,0:T(8,128)(2,1)S(1)}, bf16[40,1024]{1,0:T(8,128)(2,1)S(1)}, u32[]{:S(2)}, u32[]{:S(2)}) collective-permute-start(bf16[40,1024]{1,0:T(8,128)(2,1)S(1)} %get-tuple-element.28), channel_id=1, source_target_pairs={{0,6},{1,7},{2,4},{3,5},{4,2},{5,3},{6,0},{7,1},{8,14},{9,15},{10,... | collective-permute-start | bytes 245768 | tf_op jit(solution)/shard_map/ppermute | solution.py:353
  16.1 5.5 %collective-permute-start.5 = (bf16[40,1024]{1,0:T(8,128)(2,1)S(1)}, bf16[40,1024]{1,0:T(8,128)(2,1)S(1)}, u32[]{:S(2)}, u32[]{:S(2)}) collective-permute-start(bf16[40,1024]{1,0:T(8,128)(2,1)S(1)} %get-tuple-element.29), channel_id=1, source_target_pairs={{0,2},{1,3},{2,0},{3,1},{4,6},{5,7},{6,4},{7,5},{8,10},{9,11},{10,... | collective-permute-start | bytes 245768 | tf_op jit(solution)/shard_map/ppermute | solution.py:353
  22.3 1.9 %collective-permute-start.6 = (bf16[128,1792]{1,0:T(8,128)(2,1)S(1)}, bf16[128,1792]{1,0:T(8,128)(2,1)S(1)}, u32[]{:S(2)}, u32[]{:S(2)}) collective-permute-start(bf16[128,1792]{1,0:T(8,128)(2,1)S(1)} %get-tuple-element.34), channel_id=1, source_target_pairs={{0,1},{1,0},{2,3},{3,2},{4,5},{5,4},{6,7},{7,6},{8,9},{9,8},{10,11... | collective-permute-start | bytes 1376264 | tf_op jit(solution)/shard_map/ppermute | solution.py:353
  22.4 6.6 %collective-permute-start.10 = (bf16[80,896]{1,0:T(8,128)(2,1)S(1)}, bf16[80,896]{1,0:T(8,128)(2,1)S(1)}, u32[]{:S(2)}, u32[]{:S(2)}) collective-permute-start(bf16[80,896]{1,0:T(8,128)(2,1)S(1)} %get-tuple-element.41), channel_id=1, source_target_pairs={{0,8},{1,9},{2,10},{3,11},{4,12},{5,13},{6,14},{7,15},{8,0},{9,1},... | collective-permute-start | bytes 430088 | tf_op jit(solution)/shard_map/ppermute | solution.py:353
  24.3 9.2 %collective-permute-start.7 = (bf16[32,1792]{1,0:T(8,128)(2,1)S(1)}, bf16[32,1792]{1,0:T(8,128)(2,1)S(1)}, u32[]{:S(2)}, u32[]{:S(2)}) collective-permute-start(bf16[32,1792]{1,0:T(8,128)(2,1)S(1)} %get-tuple-element.36), channel_id=1, source_target_pairs={{0,8},{1,9},{2,10},{3,11},{4,12},{5,13},{6,14},{7,15},{8,0},{9,1},... | collective-permute-start | bytes 344072 | tf_op jit(solution)/shard_map/ppermute | solution.py:353
  25.6 7.9 %collective-permute-start.8 = (bf16[32,1792]{1,0:T(8,128)(2,1)S(1)}, bf16[32,1792]{1,0:T(8,128)(2,1)S(1)}, u32[]{:S(2)}, u32[]{:S(2)}) collective-permute-start(bf16[32,1792]{1,0:T(8,128)(2,1)S(1)} %get-tuple-element.37), channel_id=1, source_target_pairs={{0,2},{1,3},{2,0},{3,1},{4,6},{5,7},{6,4},{7,5},{8,10},{9,11},{10,... | collective-permute-start | bytes 344072 | tf_op jit(solution)/shard_map/ppermute | solution.py:353
  26.8 6.6 %collective-permute-start.9 = (bf16[32,1792]{1,0:T(8,128)(2,1)S(1)}, bf16[32,1792]{1,0:T(8,128)(2,1)S(1)}, u32[]{:S(2)}, u32[]{:S(2)}) collective-permute-start(bf16[32,1792]{1,0:T(8,128)(2,1)S(1)} %get-tuple-element.38), channel_id=1, source_target_pairs={{0,10},{1,11},{2,8},{3,9},{4,14},{5,15},{6,12},{7,13},{8,2},{9,3},... | collective-permute-start | bytes 344072 | tf_op jit(solution)/shard_map/ppermute | solution.py:353
  29.0 4.4 %collective-permute-start.11 = (bf16[40,896]{1,0:T(8,128)(2,1)S(1)}, bf16[40,896]{1,0:T(8,128)(2,1)S(1)}, u32[]{:S(2)}, u32[]{:S(2)}) collective-permute-start(bf16[40,896]{1,0:T(8,128)(2,1)S(1)} %get-tuple-element.43), channel_id=1, source_target_pairs={{0,16},{1,17},{2,18},{3,19},{4,20},{5,21},{6,22},{7,23},{8,24},{9,... | collective-permute-start | bytes 215048 | tf_op jit(solution)/shard_map/ppermute | solution.py:353

commit v4 on v3

--- a/solution.py
+++ b/solution.py
@@ -146,12 +146,14 @@
     names[...] = named
     for copy in copies[3:]:
         copy.wait()
-    for value, out in zip(values, (near, far)):
-        total = jnp.zeros((count, piece_cols), F32)
-        for j in range(PIECES):
-            chosen = jnp.where(piece == j, value, 0.0).astype(BF16)
-            total += dot(chosen, rows[0, :, j * piece_cols : (j + 1) * piece_cols])
-        out[:, :piece_cols] = total.astype(BF16)
+    value = jnp.concatenate(values, 0)
+    piece = jnp.concatenate([piece, piece], 0)
+    total = jnp.zeros((2 * count, piece_cols), F32)
+    for j in range(PIECES):
+        chosen = jnp.where(piece == j, value, 0.0).astype(BF16)
+        total += dot(chosen, rows[0, :, j * piece_cols : (j + 1) * piece_cols])
+    near[:, :piece_cols] = total[:count].astype(BF16)
+    far[...] = total[count:].astype(BF16)
     half = hidden.shape[3] // 2
     slots = hidden.shape[2]
     r, c = iota((count, slots), 0), iota((count, slots), 1)
@@ -215,11 +217,12 @@
         match = (m_piece == nq) & (m_slot == (source ^ k) * cap + n_slot)
         total += dot(hot(match), ref[:, :piece_cols])
     slot_rows = total.astype(BF16)
-    grad_act = jnp.zeros((pad, down.shape[1]), F32)
+    turned = jnp.zeros((down.shape[1], pad), F32)
     for j in range(PIECES):
-        grad_act += dot_nt(
-            slot_rows[j * pad : (j + 1) * pad], down[0, :, j * piece_cols : (j + 1) * piece_cols]
+        turned += dot_nt(
+            down[0, :, j * piece_cols : (j + 1) * piece_cols], slot_rows[j * pad : (j + 1) * pad]
         )
+    grad_act = turned.T
     gate_pad = dot(hot(iota((pad, slots), 0) == iota((pad, slots), 1)), gate[0, 0])
     grad_up = (grad_act * gate_pad).astype(BF16)
     for j in range(PIECES):
@@ -245,14 +248,17 @@
     far[...] = (ret_y[...].astype(F32) + other[count:]).astype(BF16)
 
 
-def product_kernel(scale, own, from_2, from_3, from_1, after, keep, send):
+def product_kernel(
+    scale, own, from_2, from_3, from_1, swap_own, swap_2, swap_3, swap_1, after, keep, to_xz, to_x,
+    to_z, stage
+):
+    refs = (own, from_2, from_3, from_1, swap_own, swap_2, swap_3, swap_1)
     count = own.shape[0]
     cap = count // PIECES
     slots = 4 * cap
-    half = own.shape[1] - keep.shape[1] // 2
-    piece_cols = own.shape[1] - half
-    _, _, _, _, core = place()
-    refs = (own, from_1, from_2, from_3)
+    rows_dev = keep.shape[0]
+    piece_cols = keep.shape[1] // 2
+    _, loc, zb, _, core = place()
     rows = jnp.concatenate([ref[:, :piece_cols].astype(F32) for ref in refs], 0).astype(BF16)
     m, n = iota((4 * count, count), 0), iota((4 * count, count), 1)
     mq = quotient(m, cap, 4 * count)
@@ -263,32 +269,28 @@
     ok = (m_has == m_part) & (m_loc == n_loc) & (m_source * cap + m_slot == n_row)
     place_rows = jnp.where(ok, scale, 0.0).astype(BF16)
     spread = [dot(place_rows, ref[:, piece_cols:]) for ref in refs]
-    rows_dev = half // 4
     for part in range(2):
-        for loc in range(2):
-            at = (2 * part + loc) * count
-            hidden = jnp.concatenate([value[at : at + count] for value in spread], 0)
-            product = dot(hidden.T.astype(BF16), rows)
-            for zb in range(2):
-                base = zb * 2 * rows_dev
-                first = product[base : base + rows_dev]
-                second = product[base + rows_dev : base + 2 * rows_dev]
-                block = slice((2 * loc + zb) * rows_dev, (2 * loc + zb + 1) * rows_dev)
-                cols = slice(part * piece_cols, (part + 1) * piece_cols)
-                keep[block, cols] = jnp.where(core == 0, first, second).astype(BF16)
-                send[block, cols] = jnp.where(core == 0, second, first).astype(BF16)
-
-
-def add_kernel(mine, other, own, to_x, to_z, to_xz):
-    rows_dev = own.shape[0]
-    _, loc, zb, _, _ = place()
-    for k, out in enumerate((own, to_z, to_x, to_xz)):
-        at = pl.ds(pl.multiple_of(((2 * loc + zb) ^ k) * rows_dev, rows_dev), rows_dev)
-        out[...] = (mine[at, :].astype(F32) + other[at, :].astype(F32)).astype(BF16)
+        for side in range(2):
+            at = (2 * part + side) * count
+            hidden = jnp.concatenate([value[at : at + count] for value in spread], 0).T
+            pick = [
+                jnp.where(
+                    core == 0,
+                    hidden[2 * k * rows_dev : (2 * k + 1) * rows_dev],
+                    hidden[(2 * k + 1) * rows_dev : (2 * k + 2) * rows_dev],
+                )
+                for k in range(2)
+            ]
+            product = dot(jnp.concatenate(pick, 0).astype(BF16), rows).astype(BF16)
+            cols = slice(part * piece_cols, (part + 1) * piece_cols)
+            stage[2 * side, :, cols] = product[:rows_dev]
+            stage[2 * side + 1, :, cols] = product[rows_dev:]
+    for k, out in enumerate((keep, to_z, to_x, to_xz)):
+        out[...] = stage[(2 * loc + zb) ^ k]
 
 
 def finish_kernel(
-    own, from_x, from_z, from_xz, names, near, far, tokens_hbm, down_hbm, tokens_out, down_out, sems
+    own, from_xz, from_x, from_z, names, near, far, tokens_hbm, down_hbm, tokens_out, down_out, sems
 ):
     cols = own.shape[1]
     count, piece_cols = near.shape
@@ -411,24 +413,24 @@
     back_x = swap(ret_x, loc_flip=1)
     near_sum, far_sum = call(merge_kernel, [part] * 2, (ret_own, ret_y, back_x), nbytes=1 << 18)
     back_y = swap(far_sum, group_flip=1)
-    block = ((4 * rows_dev, 2 * piece_cols), BF16)
-    keep, send = call(
+    parts = (mine, from_2, from_3, from_1)
+    swapped = tuple(swap(x, dp_flip=1) for x in parts)
+    block = ((rows_dev, 2 * piece_cols), BF16)
+    own, to_xz, to_x, to_z = call(
         functools.partial(product_kernel, 1.0 / replicas),
-        [block] * 2,
-        (mine, from_2, from_3, from_1, ret_own),
-        [VM] * 4 + [ANY],
-        nbytes=16 * rows_dev * piece_cols,
-    )
-    other = swap(send, dp_flip=1)
-    block = ((rows_dev, 2 * piece_cols), BF16)
-    own, to_x, to_z, to_xz = call(add_kernel, [block] * 4, (keep, other), nbytes=1 << 20)
+        [block] * 4,
+        parts + swapped + (ret_own,),
+        [VM] * 8 + [ANY],
+        scratch=[pltpu.VMEM((4, rows_dev, 2 * piece_cols), BF16)],
+        nbytes=1 << 20,
+    )
     got_xz = swap(to_xz, loc_flip=1, dp_flip=2)
     got_z = swap(to_z, dp_flip=2)
     got_x = swap(to_x, loc_flip=1)
     input_grad, down_grad = call(
         finish_kernel,
         [((1, tokens, model), BF16), ((1, rows_dev, model), F32)],
-        (own, got_x, got_z, got_xz, names, near_sum, back_y),
+        (own, got_xz, got_x, got_z, names, near_sum, back_y),
         outs_specs=[ANY] * 2,
         scratch=[
             pltpu.VMEM((PIECES, tokens, piece_cols), BF16),

time: 35.1 us -> 34.1 us (0.972)
  Pallas kernels: 12.4 us -> 10.9 us
  starting transfers between devices: 14.4 us -> 15.1 us
    pallas_call x8 -> x7, Pallas kernels: 12.4 us -> 10.9 us  [call(): pl.pallas_call(kernel, out_shape=out_shape, in_specs=specs or [VM] * len(...]
    ppermute x12 -> x15, starting transfers between devices: 14.4 us -> 15.1 us  [swap(): return lax.ppermute(value, AXES, pairs)]
    ppermute x12 -> x15, waiting for transfers between devices: 7.5 us -> 7.18 us  [swap(): return lax.ppermute(value, AXES, pairs)]
  transfers between devices with their start and end apart: 12 -> 15, of which waited for: 7 -> 9; matrix products, arithmetic and copies ran while one was open for 0% -> 0% of each run, Pallas kernels for 23% -> 22%
where the time goes in v4:
time: 34.1 us; the launch traced here: 33.9 us
  starting transfers between devices  15.1 us (44%)
  Pallas kernels  10.9 us (32%)
  waiting for transfers between devices  7.18 us (21%)
  between operations  0.69 us (2%)
    ppermute x15, starting transfers between devices, swap(): return lax.ppermute(value, AXES, pairs)  15.1 us
    pallas_call x7, Pallas kernels, call(): pl.pallas_call(kernel, out_shape=out_shape, in_specs=specs or [VM] * len(...  10.9 us
    ppermute x15, waiting for transfers between devices, swap(): return lax.ppermute(value, AXES, pairs)  7.18 us
  transfers between devices with their start and end apart: 15, of which 9 were waited for; matrix products, arithmetic and copies ran while one was open for 0% of the time, Pallas kernels for 22%

profile of v4, /device:TPU:0, one launch (start us, length us, event | category | flops | bytes accessed | tf_op | source)
XLA Modules:
  0.0 33.9 jit_solution(14780078372186400844)
XLA Ops:
  0.6 1.7 %shard_map.95 = (bf16[40,1024]{1,0:T(8,128)(2,1)S(1)}, bf16[40,896]{1,0:T(8,128)(2,1)S(1)}, s32[8,128]{1,0:T(8,128)S(1)}) custom-call(s32[1,1,2,5]{3,2,1,0:T(2,128)} %tok_hbm.1, s32[1,1,2]{2,1,0:T(1,128)} %cnt_hbm.1, bf16[1,1,2,5]{3,2,1,0:T(2,128)(2,1)} %weight_hbm.1, bf16[1,64,7168]{2,1,0:T(8,128)(2,1)} %rows_hbm.1, bf16[1,1,20,256]{3,2,1,0:T(8,128)(2,1)} %hidden_hbm.1), custom_call_target="tpu_custom_call" | custom-call | bytes 917504 | tf_op jit(solution)/shard_map/pallas_call | solution.py:330
  2.4 3.0 %collective-permute-start = (bf16[40,1024]{1,0:T(8,128)(2,1)S(1)}, bf16[40,1024]{1,0:T(8,128)(2,1)S(1)}, u32[]{:S(2)}, u32[]{:S(2)}) collective-permute-start(bf16[40,1024]{1,0:T(8,128)(2,1)S(1)} %get-tuple-element.21.own), channel_id=1, source_target_pairs={{0,8},{1,9},{2,10},{3,11},{4,12},{5,13},{6,14},{7,15},{8,0},{9,1},... | collective-permute-start | bytes 245768 | tf_op jit(solution)/shard_map/ppermute | solution.py:355
  5.4 1.5 %collective-permute-start.2 = (bf16[40,896]{1,0:T(8,128)(2,1)S(1)}, bf16[40,896]{1,0:T(8,128)(2,1)S(1)}, u32[]{:S(2)}, u32[]{:S(2)}) collective-permute-start(bf16[40,896]{1,0:T(8,128)(2,1)S(1)} %get-tuple-element.22.after), channel_id=1, source_target_pairs={{0,24},{1,25},{2,26},{3,27},{4,28},{5,29},{6,30},{7,31},{8,16},{9,... | collective-permute-start | bytes 215048 | tf_op jit(solution)/shard_map/ppermute | solution.py:355
  6.9 0.0 collective-permute-start.1
  6.9 3.2 %shard_map.96 = (bf16[1,256,7168]{2,1,0:T(8,128)(2,1)S(1)}, bf16[1,7168,256]{2,1,0:T(8,128)(2,1)S(1)}, bf16[1,1,20,256]{3,2,1,0:T(8,128)(2,1)S(1)}) custom-call(bf16[1,256,7168]{2,1,0:T(8,128)(2,1)} %down_hbm.1, bf16[1,7168,256]{2,1,0:T(8,128)(2,1)} %up_hbm.1, bf16[1,1,20,256]{3,2,1,0:T(8,128)(2,1)} %gate_hbm.1, bf16[40,896]{1,0:T(8,128)(2,1)S(1)} %get-tuple-element.22.after), custom_call_target="tpu_custom_call" | custom-call | bytes 14680064 | tf_op jit(solution)/shard_map/pallas_call | solution.py:330
  10.1 0.8 %collective-permute-done.2.from_xy = bf16[40,896]{1,0:T(8,128)(2,1)S(1)} collective-permute-done((bf16[40,896]{1,0:T(8,128)(2,1)S(1)}, bf16[40,896]{1,0:T(8,128)(2,1)S(1)}, u32[]{:S(2)}, u32[]{:S(2)}) %collective-permute-start.2) | collective-permute-done | bytes 71712 | tf_op jit(solution)/shard_map/ppermute | solution.py:355
  10.9 0.7 %collective-permute-done.1.from_y = bf16[40,896]{1,0:T(8,128)(2,1)S(1)} collective-permute-done((bf16[40,896]{1,0:T(8,128)(2,1)S(1)}, bf16[40,896]{1,0:T(8,128)(2,1)S(1)}, u32[]{:S(2)}, u32[]{:S(2)}) %collective-permute-start.1) | collective-permute-done | bytes 71712 | tf_op jit(solution)/shard_map/ppermute | solution.py:355
  11.7 0.0 collective-permute-done.from_x
  11.7 0.3 %shard_map.97 = (bf16[40,1024]{1,0:T(8,128)(2,1)S(1)}, bf16[40,1024]{1,0:T(8,128)(2,1)S(1)}, bf16[40,1024]{1,0:T(8,128)(2,1)S(1)}, bf16[40,1024]{1,0:T(8,128)(2,1)S(1)}) custom-call(bf16[40,1024]{1,0:T(8,128)(2,1)S(1)} %get-tuple-element.21.own, bf16[40,1024]{1,0:T(8,128)(2,1)S(1)} %collective-permute-done.from_x, ...), custom_call_target="tpu_custom_call" | custom-call | bytes 286720 | tf_op jit(solution)/shard_map/pallas_call | solution.py:330
  12.0 2.6 %collective-permute-start.3 = (bf16[40,1024]{1,0:T(8,128)(2,1)S(1)}, bf16[40,1024]{1,0:T(8,128)(2,1)S(1)}, u32[]{:S(2)}, u32[]{:S(2)}) collective-permute-start(bf16[40,1024]{1,0:T(8,128)(2,1)S(1)} %get-tuple-element.25), channel_id=1, source_target_pairs={{0,4},{1,5},{2,6},{3,7},{4,0},{5,1},{6,2},{7,3},{8,12},{9,13},{10,... | collective-permute-start | bytes 245768 | tf_op jit(solution)/shard_map/ppermute | solution.py:355
  14.7 1.3 %collective-permute-start.4 = (bf16[40,1024]{1,0:T(8,128)(2,1)S(1)}, bf16[40,1024]{1,0:T(8,128)(2,1)S(1)}, u32[]{:S(2)}, u32[]{:S(2)}) collective-permute-start(bf16[40,1024]{1,0:T(8,128)(2,1)S(1)} %get-tuple-element.26), channel_id=1, source_target_pairs={{0,6},{1,7},{2,4},{3,5},{4,2},{5,3},{6,0},{7,1},{8,14},{9,15},{10,... | collective-permute-start | bytes 245768 | tf_op jit(solution)/shard_map/ppermute | solution.py:355
  16.0 0.2 collective-permute-start.5
  16.3 3.2 %shard_map.98 = (bf16[40,896]{1,0:T(8,128)(2,1)S(1)}, bf16[40,896]{1,0:T(8,128)(2,1)S(1)}, bf16[80,896]{1,0:T(8,128)(2,1)S(1)}) custom-call(bf16[40,1024]{1,0:T(8,128)(2,1)S(1)} %get-tuple-element.21.own, bf16[40,1024]{1,0:T(8,128)(2,1)S(1)} %collective-permute-done.from_x, bf16[40,896]{1,0:T(8,128)(2,1)S(1)} %collective-permute-done.1.from_y, ...), custom_call_target="tpu_custom_call" | custom-call | flops 234881024 | bytes 7340032 | tf_op jit(solution)/shard_map/pallas_call | solution.py:330
  19.5 1.3 %collective-permute-start.13 = (bf16[80,896]{1,0:T(8,128)(2,1)S(1)}, bf16[80,896]{1,0:T(8,128)(2,1)S(1)}, u32[]{:S(2)}, u32[]{:S(2)}) collective-permute-start(bf16[80,896]{1,0:T(8,128)(2,1)S(1)} %get-tuple-element.37), channel_id=1, source_target_pairs={{0,8},{1,9},{2,10},{3,11},{4,12},{5,13},{6,14},{7,15},{8,0},{9,1},... | collective-permute-start | bytes 430088 | tf_op jit(solution)/shard_map/ppermute | solution.py:355
  20.7 0.0 collective-permute-start.6
  20.8 0.0 collective-permute-done.3.from_2
  20.8 0.5 %collective-permute-start.7 = (bf16[40,1024]{1,0:T(8,128)(2,1)S(1)}, bf16[40,1024]{1,0:T(8,128)(2,1)S(1)}, u32[]{:S(2)}, u32[]{:S(2)}) collective-permute-start(bf16[40,1024]{1,0:T(8,128)(2,1)S(1)} %collective-permute-done.3.from_2), channel_id=1, source_target_pairs={{0,1},{1,0},{2,3},{3,2},{4,5},{5,4},{6,7},{7,6},{8,9},{9,8},{10,11... | collective-permute-start | bytes 245768 | tf_op jit(solution)/shard_map/ppermute | solution.py:355
  21.3 0.0 collective-permute-done.4.from_3
  21.3 0.1 collective-permute-start.8
  21.3 0.2 collective-permute-done.5.from_1
  21.6 0.2 collective-permute-start.9
  21.8 0.2 collective-permute-done.6.swap_own
  22.0 0.2 collective-permute-done.7.swap_2
  22.2 0.4 %collective-permute-done.8.swap_3 = bf16[40,1024]{1,0:T(8,128)(2,1)S(1)} collective-permute-done((bf16[40,1024]{1,0:T(8,128)(2,1)S(1)}, bf16[40,1024]{1,0:T(8,128)(2,1)S(1)}, u32[]{:S(2)}, u32[]{:S(2)}) %collective-permute-start.8) | collective-permute-done | bytes 81952 | tf_op jit(solution)/shard_map/ppermute | solution.py:355
  22.5 0.3 collective-permute-done.9.swap_1
  22.8 0.9 %shard_map.99 = (bf16[32,1792]{1,0:T(8,128)(2,1)S(1)}, bf16[32,1792]{1,0:T(8,128)(2,1)S(1)}, bf16[32,1792]{1,0:T(8,128)(2,1)S(1)}, bf16[32,1792]{1,0:T(8,128)(2,1)S(1)}) custom-call(bf16[40,1024]{1,0:T(8,128)(2,1)S(1)} %get-tuple-element.24.own, bf16[40,1024]{1,0:T(8,128)(2,1)S(1)} %collective-permute-done.3.from_2, ...), custom_call_target="tpu_custom_call" | custom-call | bytes 1048576 | tf_op jit(solution)/shard_map/pallas_call | solution.py:330
  23.7 2.0 %collective-permute-start.10 = (bf16[32,1792]{1,0:T(8,128)(2,1)S(1)}, bf16[32,1792]{1,0:T(8,128)(2,1)S(1)}, u32[]{:S(2)}, u32[]{:S(2)}) collective-permute-start(bf16[32,1792]{1,0:T(8,128)(2,1)S(1)} %get-tuple-element.32), channel_id=1, source_target_pairs={{0,10},{1,11},{2,8},{3,9},{4,14},{5,15},{6,12},{7,13},{8,2},{9,3},... | collective-permute-start | bytes 344072 | tf_op jit(solution)/shard_map/ppermute | solution.py:355
  25.7 1.2 %collective-permute-start.11 = (bf16[32,1792]{1,0:T(8,128)(2,1)S(1)}, bf16[32,1792]{1,0:T(8,128)(2,1)S(1)}, u32[]{:S(2)}, u32[]{:S(2)}) collective-permute-start(bf16[32,1792]{1,0:T(8,128)(2,1)S(1)} %get-tuple-element.33), channel_id=1, source_target_pairs={{0,8},{1,9},{2,10},{3,11},{4,12},{5,13},{6,14},{7,15},{8,0},{9,1},... | collective-permute-start | bytes 344072 | tf_op jit(solution)/shard_map/ppermute | solution.py:355
  26.9 0.4 %collective-permute-start.12 = (bf16[32,1792]{1,0:T(8,128)(2,1)S(1)}, bf16[32,1792]{1,0:T(8,128)(2,1)S(1)}, u32[]{:S(2)}, u32[]{:S(2)}) collective-permute-start(bf16[32,1792]{1,0:T(8,128)(2,1)S(1)} %get-tuple-element.34), channel_id=1, source_target_pairs={{0,2},{1,3},{2,0},{3,1},{4,6},{5,7},{6,4},{7,5},{8,10},{9,11},{10,... | collective-permute-start | bytes 344072 | tf_op jit(solution)/shard_map/ppermute | solution.py:355
  27.3 0.0 collective-permute-done.13.from_x
  27.3 0.7 %collective-permute-start.14 = (bf16[40,896]{1,0:T(8,128)(2,1)S(1)}, bf16[40,896]{1,0:T(8,128)(2,1)S(1)}, u32[]{:S(2)}, u32[]{:S(2)}) collective-permute-start(bf16[40,896]{1,0:T(8,128)(2,1)S(1)} %get-tuple-element.39), channel_id=1, source_target_pairs={{0,16},{1,17},{2,18},{3,19},{4,20},{5,21},{6,22},{7,23},{8,24},{9,... | collective-permute-start | bytes 215048 | tf_op jit(solution)/shard_map/ppermute | solution.py:355
  28.1 3.7 %collective-permute-done.14.far = bf16[40,896]{1,0:T(8,128)(2,1)S(1)} collective-permute-done((bf16[40,896]{1,0:T(8,128)(2,1)S(1)}, bf16[40,896]{1,0:T(8,128)(2,1)S(1)}, u32[]{:S(2)}, u32[]{:S(2)}) %collective-permute-start.14) | collective-permute-done | bytes 71712 | tf_op jit(solution)/shard_map/ppermute | solution.py:355
  31.7 0.0 collective-permute-done.10.from_xz
  31.7 0.7 %collective-permute-done.11.from_x = bf16[32,1792]{1,0:T(8,128)(2,1)S(1)} collective-permute-done((bf16[32,1792]{1,0:T(8,128)(2,1)S(1)}, bf16[32,1792]{1,0:T(8,128)(2,1)S(1)}, u32[]{:S(2)}, u32[]{:S(2)}) %collective-permute-start.11) | collective-permute-done | bytes 114720 | tf_op jit(solution)/shard_map/ppermute | solution.py:355
  32.4 0.0 collective-permute-done.12.from_z
  32.4 1.5 %shard_map.101 = (bf16[1,64,7168]{2,1,0:T(8,128)(2,1)}, f32[1,32,7168]{2,1,0:T(8,128)}) custom-call(bf16[32,1792]{1,0:T(8,128)(2,1)S(1)} %get-tuple-element.31.own, bf16[32,1792]{1,0:T(8,128)(2,1)S(1)} %collective-permute-done.10.from_xz, bf16[32,1792]{1,0:T(8,128)(2,1)S(1)} %collective-permute-done.11.from_x, ...), custom_call_target="tpu_custom_call" | custom-call | bytes 4194304 | tf_op jit(solution)/shard_map/pallas_call | solution.py:330
  (1 shorter events, 0.0 us)
Async XLA Ops:
  2.4 9.3 %collective-permute-start = (bf16[40,1024]{1,0:T(8,128)(2,1)S(1)}, bf16[40,1024]{1,0:T(8,128)(2,1)S(1)}, u32[]{:S(2)}, u32[]{:S(2)}) collective-permute-start(bf16[40,1024]{1,0:T(8,128)(2,1)S(1)} %get-tuple-element.21.own), channel_id=1, source_target_pairs={{0,8},{1,9},{2,10},{3,11},{4,12},{5,13},{6,14},{7,15},{8,0},{9,1},... | collective-permute-start | bytes 245768 | tf_op jit(solution)/shard_map/ppermute | solution.py:355
  5.4 5.5 %collective-permute-start.2 = (bf16[40,896]{1,0:T(8,128)(2,1)S(1)}, bf16[40,896]{1,0:T(8,128)(2,1)S(1)}, u32[]{:S(2)}, u32[]{:S(2)}) collective-permute-start(bf16[40,896]{1,0:T(8,128)(2,1)S(1)} %get-tuple-element.22.after), channel_id=1, source_target_pairs={{0,24},{1,25},{2,26},{3,27},{4,28},{5,29},{6,30},{7,31},{8,16},{9,... | collective-permute-start | bytes 215048 | tf_op jit(solution)/shard_map/ppermute | solution.py:355
  6.9 4.8 %collective-permute-start.1 = (bf16[40,896]{1,0:T(8,128)(2,1)S(1)}, bf16[40,896]{1,0:T(8,128)(2,1)S(1)}, u32[]{:S(2)}, u32[]{:S(2)}) collective-permute-start(bf16[40,896]{1,0:T(8,128)(2,1)S(1)} %get-tuple-element.22.after), channel_id=1, source_target_pairs={{0,16},{1,17},{2,18},{3,19},{4,20},{5,21},{6,22},{7,23},{8,24},{9,... | collective-permute-start | bytes 215048 | tf_op jit(solution)/shard_map/ppermute | solution.py:355
  12.0 8.7 %collective-permute-start.3 = (bf16[40,1024]{1,0:T(8,128)(2,1)S(1)}, bf16[40,1024]{1,0:T(8,128)(2,1)S(1)}, u32[]{:S(2)}, u32[]{:S(2)}) collective-permute-start(bf16[40,1024]{1,0:T(8,128)(2,1)S(1)} %get-tuple-element.25), channel_id=1, source_target_pairs={{0,4},{1,5},{2,6},{3,7},{4,0},{5,1},{6,2},{7,3},{8,12},{9,13},{10,... | collective-permute-start | bytes 245768 | tf_op jit(solution)/shard_map/ppermute | solution.py:355
  14.7 6.6 %collective-permute-start.4 = (bf16[40,1024]{1,0:T(8,128)(2,1)S(1)}, bf16[40,1024]{1,0:T(8,128)(2,1)S(1)}, u32[]{:S(2)}, u32[]{:S(2)}) collective-permute-start(bf16[40,1024]{1,0:T(8,128)(2,1)S(1)} %get-tuple-element.26), channel_id=1, source_target_pairs={{0,6},{1,7},{2,4},{3,5},{4,2},{5,3},{6,0},{7,1},{8,14},{9,15},{10,... | collective-permute-start | bytes 245768 | tf_op jit(solution)/shard_map/ppermute | solution.py:355
  16.0 5.5 %collective-permute-start.5 = (bf16[40,1024]{1,0:T(8,128)(2,1)S(1)}, bf16[40,1024]{1,0:T(8,128)(2,1)S(1)}, u32[]{:S(2)}, u32[]{:S(2)}) collective-permute-start(bf16[40,1024]{1,0:T(8,128)(2,1)S(1)} %get-tuple-element.27), channel_id=1, source_target_pairs={{0,2},{1,3},{2,0},{3,1},{4,6},{5,7},{6,4},{7,5},{8,10},{9,11},{10,... | collective-permute-start | bytes 245768 | tf_op jit(solution)/shard_map/ppermute | solution.py:355
  19.5 7.8 %collective-permute-start.13 = (bf16[80,896]{1,0:T(8,128)(2,1)S(1)}, bf16[80,896]{1,0:T(8,128)(2,1)S(1)}, u32[]{:S(2)}, u32[]{:S(2)}) collective-permute-start(bf16[80,896]{1,0:T(8,128)(2,1)S(1)} %get-tuple-element.37), channel_id=1, source_target_pairs={{0,8},{1,9},{2,10},{3,11},{4,12},{5,13},{6,14},{7,15},{8,0},{9,1},... | collective-permute-start | bytes 430088 | tf_op jit(solution)/shard_map/ppermute | solution.py:355
  20.7 1.3 %collective-permute-start.6 = (bf16[40,1024]{1,0:T(8,128)(2,1)S(1)}, bf16[40,1024]{1,0:T(8,128)(2,1)S(1)}, u32[]{:S(2)}, u32[]{:S(2)}) collective-permute-start(bf16[40,1024]{1,0:T(8,128)(2,1)S(1)} %get-tuple-element.24.own), channel_id=1, source_target_pairs={{0,1},{1,0},{2,3},{3,2},{4,5},{5,4},{6,7},{7,6},{8,9},{9,8},{10,11... | collective-permute-start | bytes 245768 | tf_op jit(solution)/shard_map/ppermute | solution.py:355
  20.8 1.4 %collective-permute-start.7 = (bf16[40,1024]{1,0:T(8,128)(2,1)S(1)}, bf16[40,1024]{1,0:T(8,128)(2,1)S(1)}, u32[]{:S(2)}, u32[]{:S(2)}) collective-permute-start(bf16[40,1024]{1,0:T(8,128)(2,1)S(1)} %collective-permute-done.3.from_2), channel_id=1, source_target_pairs={{0,1},{1,0},{2,3},{3,2},{4,5},{5,4},{6,7},{7,6},{8,9},{9,8},{10,11... | collective-permute-start | bytes 245768 | tf_op jit(solution)/shard_map/ppermute | solution.py:355
  21.3 1.3 %collective-permute-start.8 = (bf16[40,1024]{1,0:T(8,128)(2,1)S(1)}, bf16[40,1024]{1,0:T(8,128)(2,1)S(1)}, u32[]{:S(2)}, u32[]{:S(2)}) collective-permute-start(bf16[40,1024]{1,0:T(8,128)(2,1)S(1)} %collective-permute-done.4.from_3), channel_id=1, source_target_pairs={{0,1},{1,0},{2,3},{3,2},{4,5},{5,4},{6,7},{7,6},{8,9},{9,8},{10,11... | collective-permute-start | bytes 245768 | tf_op jit(solution)/shard_map/ppermute | solution.py:355
  21.6 1.3 %collective-permute-start.9 = (bf16[40,1024]{1,0:T(8,128)(2,1)S(1)}, bf16[40,1024]{1,0:T(8,128)(2,1)S(1)}, u32[]{:S(2)}, u32[]{:S(2)}) collective-permute-start(bf16[40,1024]{1,0:T(8,128)(2,1)S(1)} %collective-permute-done.5.from_1), channel_id=1, source_target_pairs={{0,1},{1,0},{2,3},{3,2},{4,5},{5,4},{6,7},{7,6},{8,9},{9,8},{10,11... | collective-permute-start | bytes 245768 | tf_op jit(solution)/shard_map/ppermute | solution.py:355
  23.7 8.0 %collective-permute-start.10 = (bf16[32,1792]{1,0:T(8,128)(2,1)S(1)}, bf16[32,1792]{1,0:T(8,128)(2,1)S(1)}, u32[]{:S(2)}, u32[]{:S(2)}) collective-permute-start(bf16[32,1792]{1,0:T(8,128)(2,1)S(1)} %get-tuple-element.32), channel_id=1, source_target_pairs={{0,10},{1,11},{2,8},{3,9},{4,14},{5,15},{6,12},{7,13},{8,2},{9,3},... | collective-permute-start | bytes 344072 | tf_op jit(solution)/shard_map/ppermute | solution.py:355
  25.7 6.7 %collective-permute-start.11 = (bf16[32,1792]{1,0:T(8,128)(2,1)S(1)}, bf16[32,1792]{1,0:T(8,128)(2,1)S(1)}, u32[]{:S(2)}, u32[]{:S(2)}) collective-permute-start(bf16[32,1792]{1,0:T(8,128)(2,1)S(1)} %get-tuple-element.33), channel_id=1, source_target_pairs={{0,8},{1,9},{2,10},{3,11},{4,12},{5,13},{6,14},{7,15},{8,0},{9,1},... | collective-permute-start | bytes 344072 | tf_op jit(solution)/shard_map/ppermute | solution.py:355
  26.9 5.5 %collective-permute-start.12 = (bf16[32,1792]{1,0:T(8,128)(2,1)S(1)}, bf16[32,1792]{1,0:T(8,128)(2,1)S(1)}, u32[]{:S(2)}, u32[]{:S(2)}) collective-permute-start(bf16[32,1792]{1,0:T(8,128)(2,1)S(1)} %get-tuple-element.34), channel_id=1, source_target_pairs={{0,2},{1,3},{2,0},{3,1},{4,6},{5,7},{6,4},{7,5},{8,10},{9,11},{10,... | collective-permute-start | bytes 344072 | tf_op jit(solution)/shard_map/ppermute | solution.py:355
  27.3 4.4 %collective-permute-start.14 = (bf16[40,896]{1,0:T(8,128)(2,1)S(1)}, bf16[40,896]{1,0:T(8,128)(2,1)S(1)}, u32[]{:S(2)}, u32[]{:S(2)}) collective-permute-start(bf16[40,896]{1,0:T(8,128)(2,1)S(1)} %get-tuple-element.39), channel_id=1, source_target_pairs={{0,16},{1,17},{2,18},{3,19},{4,20},{5,21},{6,22},{7,23},{8,24},{9,... | collective-permute-start | bytes 215048 | tf_op jit(solution)/shard_map/ppermute | solution.py:355

commit v5 on v4

--- a/solution.py
+++ b/solution.py
@@ -124,8 +124,9 @@
     row, token = iota((count, tokens), 0), iota((count, tokens), 1)
     piece = quotient(row, cap, count)
     slot = row - cap * piece
-    line, lane = iota(names.shape, 0), iota(names.shape, 1)
-    lane_slot = lane - cap * quotient(lane, cap, names.shape[1])
+    lane = iota(names.shape, 1)
+    lane_group = quotient(lane, cap, names.shape[1])
+    lane_slot = lane - cap * lane_group
     for copy in copies[:3]:
         copy.wait()
     scale = weight[0, 0].astype(F32)
@@ -141,7 +142,8 @@
                 expert == 0, scale[0:1, s : s + 1], scale[1:2, s : s + 1]
             )
             value = jnp.where((slot == s) & (token == name), factor, value)
-            named = jnp.where((line == other) & (lane_slot == s), name, named)
+            here = (lane_group // PIECES == other) & (lane_slot == s)
+            named = jnp.where(here, name, named)
         values.append(value)
     names[...] = named
     for copy in copies[3:]:
@@ -153,7 +155,7 @@
         chosen = jnp.where(piece == j, value, 0.0).astype(BF16)
         total += dot(chosen, rows[0, :, j * piece_cols : (j + 1) * piece_cols])
     near[:, :piece_cols] = total[:count].astype(BF16)
-    far[...] = total[count:].astype(BF16)
+    far[:, :piece_cols] = total[count:].astype(BF16)
     half = hidden.shape[3] // 2
     slots = hidden.shape[2]
     r, c = iota((count, slots), 0), iota((count, slots), 1)
@@ -161,6 +163,7 @@
         hot(r == c + slots), hidden[0, 0, :, half:]
     )
     near[:, piece_cols:] = folded.astype(BF16)
+    far[:, piece_cols:] = folded.astype(BF16)
 
 
 def load_kernel(down_hbm, up_hbm, gate_hbm, after, down, up, gate, sems):
@@ -172,8 +175,8 @@
         copy.wait()
 
 
-def spread_kernel(own, from_x, from_y, from_xy, after, keep, to_1, to_2, to_3):
-    count, piece_cols = from_y.shape
+def spread_kernel(piece_cols, own, from_x, from_y, from_xy, after, keep, to_1, to_2, to_3):
+    count = from_y.shape[0]
     cap = count // PIECES
     slots = 4 * cap
     group, loc, zb, pair, _ = place()
@@ -202,7 +205,7 @@
 def expert_kernel(
     own, from_x, from_y, from_xy, down, gate, up, ret_own, ret_y, ret_x, stack
 ):
-    count, piece_cols = from_y.shape
+    count, piece_cols = ret_y.shape
     cap = count // PIECES
     pad = stack.shape[0] // PIECES
     slots = gate.shape[2]
@@ -228,17 +231,16 @@
     for j in range(PIECES):
         part = dot_nt(grad_up, up[0, j * piece_cols : (j + 1) * piece_cols, :])
         stack[j * pad : (j + 1) * pad, :] = part.astype(BF16)
-    n, m = iota((count, PIECES * pad), 0), iota((count, PIECES * pad), 1)
-    nq = quotient(n, cap, count)
+    n, m = iota((4 * count, PIECES * pad), 0), iota((4 * count, PIECES * pad), 1)
+    nq = quotient(n, cap, 4 * count)
     n_slot = n - cap * nq
     m_piece, m_slot = m // pad, m % pad
-    back = []
-    for k in range(4):
-        match = (m_piece == nq) & (m_slot == (source ^ k) * cap + n_slot)
-        back.append(dot(hot(match), stack[...]))
-    ret_own[...] = back[0].astype(BF16)
-    ret_y[...] = back[2].astype(BF16)
-    ret_x[...] = jnp.concatenate([back[1], back[3]], 0).astype(BF16)
+    back_row = jnp.where(nq < 2 * PIECES, (nq >> 3) * 2, ((nq >> 3) - 2) * 2 + 1)
+    match = (m_piece == nq % PIECES) & (m_slot == (source ^ back_row) * cap + n_slot)
+    back = dot(hot(match), stack[...])
+    ret_own[...] = back[:count].astype(BF16)
+    ret_y[...] = back[count : 2 * count].astype(BF16)
+    ret_x[...] = back[2 * count :].astype(BF16)
 
 
 def merge_kernel(ret_own, ret_y, from_x, near, far):
@@ -269,22 +271,20 @@
     ok = (m_has == m_part) & (m_loc == n_loc) & (m_source * cap + m_slot == n_row)
     place_rows = jnp.where(ok, scale, 0.0).astype(BF16)
     spread = [dot(place_rows, ref[:, piece_cols:]) for ref in refs]
+    picks = []
+    for block in range(4):
+        at = block * count
+        hidden = jnp.concatenate([value[at : at + count] for value in spread], 0).T
+        for k in range(2):
+            first = hidden[2 * k * rows_dev : (2 * k + 1) * rows_dev]
+            second = hidden[(2 * k + 1) * rows_dev : (2 * k + 2) * rows_dev]
+            picks.append(jnp.where(core == 0, first, second).astype(BF16))
+    product = dot(jnp.concatenate(picks, 0), rows).astype(BF16)
     for part in range(2):
-        for side in range(2):
-            at = (2 * part + side) * count
-            hidden = jnp.concatenate([value[at : at + count] for value in spread], 0).T
-            pick = [
-                jnp.where(
-                    core == 0,
-                    hidden[2 * k * rows_dev : (2 * k + 1) * rows_dev],
-                    hidden[(2 * k + 1) * rows_dev : (2 * k + 2) * rows_dev],
-                )
-                for k in range(2)
-            ]
-            product = dot(jnp.concatenate(pick, 0).astype(BF16), rows).astype(BF16)
-            cols = slice(part * piece_cols, (part + 1) * piece_cols)
-            stage[2 * side, :, cols] = product[:rows_dev]
-            stage[2 * side + 1, :, cols] = product[rows_dev:]
+        cols = slice(part * piece_cols, (part + 1) * piece_cols)
+        for k in range(4):
+            at = (4 * part + k) * rows_dev
+            stage[k, :, cols] = product[at : at + rows_dev]
     for k, out in enumerate((keep, to_z, to_x, to_xz)):
         out[...] = stage[(2 * loc + zb) ^ k]
 
@@ -308,14 +308,12 @@
         start = pl.multiple_of(((2 * loc + zb) ^ k) * cols, cols)
         down_out[k] = ref[...].astype(F32)
         send(down_out.at[k], down_hbm.at[0, :, pl.ds(start, cols)])
-    token, lane = iota((tokens, count), 0), iota((tokens, count), 1)
-    piece = quotient(lane, cap, count)
-    match = [token == names[other : other + 1, :count] for other in range(2)]
+    both = jnp.concatenate([near[...].astype(F32), far[...].astype(F32)], 0).astype(BF16)
+    token, lane = iota((tokens, 2 * count), 0), iota((tokens, 2 * count), 1)
+    piece = quotient(lane, cap, 2 * count) % PIECES
+    match = token == names[:1, : 2 * count]
     for j in range(PIECES):
-        total = dot(hot(match[0] & (piece == j)), near[...]) + dot(
-            hot(match[1] & (piece == j)), far[...]
-        )
-        tokens_out[j] = total.astype(BF16)
+        tokens_out[j] = dot(hot(match & (piece == j)), both).astype(BF16)
         send(tokens_out.at[j], tokens_hbm.at[0, :, pl.ds(j * piece_cols, piece_cols)])
     for copy in copies:
         copy.wait()
@@ -371,7 +369,7 @@
         select_kernel,
         [
             ((count, piece_cols + half), BF16),
-            ((count, piece_cols), BF16),
+            ((count, piece_cols + half), BF16),
             ((8, 128), jnp.int32),
         ],
         [hbm(x) for x in inputs],
@@ -388,14 +386,14 @@
     down, up, gate = call(
         load_kernel,
         [(x.shape, x.dtype) for x in held],
-        [hbm(x) for x in held] + [far],
+        [hbm(x) for x in held] + [near],
         [ANY] * 4,
         scratch=[pltpu.SemaphoreType.DMA((3,))],
         nbytes=8 * model * hidden_dev,
     )
     message = ((count, piece_cols + half), BF16)
     mine, to_1, to_2, to_3 = call(
-        spread_kernel, [message] * 4, arrived + (gate,), [VM] * 4 + [ANY], nbytes=count * model
+        functools.partial(spread_kernel, piece_cols), [message] * 4, arrived + (gate,), [VM] * 4 + [ANY], nbytes=count * model
     )
     from_2 = swap(to_2, dp_flip=4)
     from_3 = swap(to_3, dp_flip=6)

time: 34.1 us -> 33.5 us (0.982)
  waiting for transfers between devices: 7.18 us -> 6.16 us
  starting transfers between devices: 15.1 us -> 16 us
  Pallas kernels: 10.9 us -> 10.5 us
    ppermute x15, waiting for transfers between devices: 7.18 us -> 6.16 us  [swap(): return lax.ppermute(value, AXES, pairs)]
    ppermute x15, starting transfers between devices: 15.1 us -> 16 us  [swap(): return lax.ppermute(value, AXES, pairs)]
    pallas_call x7, Pallas kernels: 10.9 us -> 10.5 us  [call(): pl.pallas_call(kernel, out_shape=out_shape, in_specs=specs or [VM] * len(...]
  transfers between devices with their start and end apart: 15 -> 15, of which waited for: 9 -> 8; matrix products, arithmetic and copies ran while one was open for 0% -> 0% of each run, Pallas kernels for 22% -> 21%
where the time goes in v5:
time: 33.5 us; the launch traced here: 33.3 us
  starting transfers between devices  16 us (48%)
  Pallas kernels  10.5 us (31%)
  waiting for transfers between devices  6.16 us (18%)
  between operations  0.7 us (2%)
    ppermute x15, starting transfers between devices, swap(): return lax.ppermute(value, AXES, pairs)  16 us
    pallas_call x7, Pallas kernels, call(): pl.pallas_call(kernel, out_shape=out_shape, in_specs=specs or [VM] * len(...  10.5 us
    ppermute x15, waiting for transfers between devices, swap(): return lax.ppermute(value, AXES, pairs)  6.16 us
  transfers between devices with their start and end apart: 15, of which 8 were waited for; matrix products, arithmetic and copies ran while one was open for 0% of the time, Pallas kernels for 21%

profile of v5, /device:TPU:0, one launch (start us, length us, event | category | flops | bytes accessed | tf_op | source)
XLA Modules:
  0.0 33.3 jit_solution(1255505708161391724)
XLA Ops:
  0.6 1.7 %shard_map.95 = (bf16[40,1024]{1,0:T(8,128)(2,1)S(1)}, bf16[40,1024]{1,0:T(8,128)(2,1)S(1)}, s32[8,128]{1,0:T(8,128)S(1)}) custom-call(s32[1,1,2,5]{3,2,1,0:T(2,128)} %tok_hbm.1, s32[1,1,2]{2,1,0:T(1,128)} %cnt_hbm.1, bf16[1,1,2,5]{3,2,1,0:T(2,128)(2,1)} %weight_hbm.1, bf16[1,64,7168]{2,1,0:T(8,128)(2,1)} %rows_hbm.1, bf16[1,1,20,256]{3,2,1,0:T(8,128)(2,1)} %hidden_hbm.1), custom_call_target="tpu_custom_call" | custom-call | bytes 917504 | tf_op jit(solution)/shard_map/pallas_call | solution.py:328
  2.4 4.0 %collective-permute-start.2 = (bf16[40,1024]{1,0:T(8,128)(2,1)S(1)}, bf16[40,1024]{1,0:T(8,128)(2,1)S(1)}, u32[]{:S(2)}, u32[]{:S(2)}) collective-permute-start(bf16[40,1024]{1,0:T(8,128)(2,1)S(1)} %get-tuple-element.22), channel_id=1, source_target_pairs={{0,24},{1,25},{2,26},{3,27},{4,28},{5,29},{6,30},{7,31},{8,16},{9,... | collective-permute-start | bytes 245768 | tf_op jit(solution)/shard_map/ppermute | solution.py:353
  6.3 0.5 %collective-permute-start.1 = (bf16[40,1024]{1,0:T(8,128)(2,1)S(1)}, bf16[40,1024]{1,0:T(8,128)(2,1)S(1)}, u32[]{:S(2)}, u32[]{:S(2)}) collective-permute-start(bf16[40,1024]{1,0:T(8,128)(2,1)S(1)} %get-tuple-element.22), channel_id=1, source_target_pairs={{0,16},{1,17},{2,18},{3,19},{4,20},{5,21},{6,22},{7,23},{8,24},{9,... | collective-permute-start | bytes 245768 | tf_op jit(solution)/shard_map/ppermute | solution.py:353
  6.9 0.1 collective-permute-start
  7.0 3.2 %shard_map.96 = (bf16[1,256,7168]{2,1,0:T(8,128)(2,1)S(1)}, bf16[1,7168,256]{2,1,0:T(8,128)(2,1)S(1)}, bf16[1,1,20,256]{3,2,1,0:T(8,128)(2,1)S(1)}) custom-call(bf16[1,256,7168]{2,1,0:T(8,128)(2,1)} %down_hbm.1, bf16[1,7168,256]{2,1,0:T(8,128)(2,1)} %up_hbm.1, bf16[1,1,20,256]{3,2,1,0:T(8,128)(2,1)} %gate_hbm.1, bf16[40,1024]{1,0:T(8,128)(2,1)S(1)} %get-tuple-element.21.after.own), custom_call_target="tpu_custom_call" | custom-call | bytes 14680064 | tf_op jit(solution)/shard_map/pallas_call | solution.py:328
  10.2 0.0 collective-permute-done.2.from_xy
  10.2 0.6 %collective-permute-done.1.from_y = bf16[40,1024]{1,0:T(8,128)(2,1)S(1)} collective-permute-done((bf16[40,1024]{1,0:T(8,128)(2,1)S(1)}, bf16[40,1024]{1,0:T(8,128)(2,1)S(1)}, u32[]{:S(2)}, u32[]{:S(2)}) %collective-permute-start.1) | collective-permute-done | bytes 81952 | tf_op jit(solution)/shard_map/ppermute | solution.py:353
  10.8 0.5 %collective-permute-done.from_x = bf16[40,1024]{1,0:T(8,128)(2,1)S(1)} collective-permute-done((bf16[40,1024]{1,0:T(8,128)(2,1)S(1)}, bf16[40,1024]{1,0:T(8,128)(2,1)S(1)}, u32[]{:S(2)}, u32[]{:S(2)}) %collective-permute-start) | collective-permute-done | bytes 81952 | tf_op jit(solution)/shard_map/ppermute | solution.py:353
  11.3 0.3 %shard_map.97 = (bf16[40,1024]{1,0:T(8,128)(2,1)S(1)}, bf16[40,1024]{1,0:T(8,128)(2,1)S(1)}, bf16[40,1024]{1,0:T(8,128)(2,1)S(1)}, bf16[40,1024]{1,0:T(8,128)(2,1)S(1)}) custom-call(bf16[40,1024]{1,0:T(8,128)(2,1)S(1)} %get-tuple-element.21.after.own, bf16[40,1024]{1,0:T(8,128)(2,1)S(1)} %collective-permute-done.from_x, ...), custom_call_target="tpu_custom_call" | custom-call | bytes 286720 | tf_op jit(solution)/shard_map/pallas_call | solution.py:328
  11.6 2.7 %collective-permute-start.3 = (bf16[40,1024]{1,0:T(8,128)(2,1)S(1)}, bf16[40,1024]{1,0:T(8,128)(2,1)S(1)}, u32[]{:S(2)}, u32[]{:S(2)}) collective-permute-start(bf16[40,1024]{1,0:T(8,128)(2,1)S(1)} %get-tuple-element.25), channel_id=1, source_target_pairs={{0,4},{1,5},{2,6},{3,7},{4,0},{5,1},{6,2},{7,3},{8,12},{9,13},{10,... | collective-permute-start | bytes 245768 | tf_op jit(solution)/shard_map/ppermute | solution.py:353
  14.3 1.4 %collective-permute-start.4 = (bf16[40,1024]{1,0:T(8,128)(2,1)S(1)}, bf16[40,1024]{1,0:T(8,128)(2,1)S(1)}, u32[]{:S(2)}, u32[]{:S(2)}) collective-permute-start(bf16[40,1024]{1,0:T(8,128)(2,1)S(1)} %get-tuple-element.26), channel_id=1, source_target_pairs={{0,6},{1,7},{2,4},{3,5},{4,2},{5,3},{6,0},{7,1},{8,14},{9,15},{10,... | collective-permute-start | bytes 245768 | tf_op jit(solution)/shard_map/ppermute | solution.py:353
  15.6 0.2 collective-permute-start.5
  15.9 3.0 %shard_map.98 = (bf16[40,896]{1,0:T(8,128)(2,1)S(1)}, bf16[40,896]{1,0:T(8,128)(2,1)S(1)}, bf16[80,896]{1,0:T(8,128)(2,1)S(1)}) custom-call(bf16[40,1024]{1,0:T(8,128)(2,1)S(1)} %get-tuple-element.21.after.own, bf16[40,1024]{1,0:T(8,128)(2,1)S(1)} %collective-permute-done.from_x, bf16[40,1024]{1,0:T(8,128)(2,1)S(1)} %collective-permute-done.1.from_y, ...), custom_call_target="tpu_custom_call" | custom-call | flops 234881024 | bytes 7340032 | tf_op jit(solution)/shard_map/pallas_call | solution.py:328
  18.9 1.1 %collective-permute-start.13 = (bf16[80,896]{1,0:T(8,128)(2,1)S(1)}, bf16[80,896]{1,0:T(8,128)(2,1)S(1)}, u32[]{:S(2)}, u32[]{:S(2)}) collective-permute-start(bf16[80,896]{1,0:T(8,128)(2,1)S(1)} %get-tuple-element.37), channel_id=1, source_target_pairs={{0,8},{1,9},{2,10},{3,11},{4,12},{5,13},{6,14},{7,15},{8,0},{9,1},... | collective-permute-start | bytes 430088 | tf_op jit(solution)/shard_map/ppermute | solution.py:353
  20.0 0.0 collective-permute-start.6
  20.0 0.0 collective-permute-done.3.from_2
  20.0 0.5 %collective-permute-start.7 = (bf16[40,1024]{1,0:T(8,128)(2,1)S(1)}, bf16[40,1024]{1,0:T(8,128)(2,1)S(1)}, u32[]{:S(2)}, u32[]{:S(2)}) collective-permute-start(bf16[40,1024]{1,0:T(8,128)(2,1)S(1)} %collective-permute-done.3.from_2), channel_id=1, source_target_pairs={{0,1},{1,0},{2,3},{3,2},{4,5},{5,4},{6,7},{7,6},{8,9},{9,8},{10,11... | collective-permute-start | bytes 245768 | tf_op jit(solution)/shard_map/ppermute | solution.py:353
  20.5 0.4 %collective-permute-done.4.from_3 = bf16[40,1024]{1,0:T(8,128)(2,1)S(1)} collective-permute-done((bf16[40,1024]{1,0:T(8,128)(2,1)S(1)}, bf16[40,1024]{1,0:T(8,128)(2,1)S(1)}, u32[]{:S(2)}, u32[]{:S(2)}) %collective-permute-start.4) | collective-permute-done | bytes 81952 | tf_op jit(solution)/shard_map/ppermute | solution.py:353
  20.9 0.0 collective-permute-start.8
  20.9 0.1 collective-permute-done.5.from_1
  21.0 0.4 %collective-permute-start.9 = (bf16[40,1024]{1,0:T(8,128)(2,1)S(1)}, bf16[40,1024]{1,0:T(8,128)(2,1)S(1)}, u32[]{:S(2)}, u32[]{:S(2)}) collective-permute-start(bf16[40,1024]{1,0:T(8,128)(2,1)S(1)} %collective-permute-done.5.from_1), channel_id=1, source_target_pairs={{0,1},{1,0},{2,3},{3,2},{4,5},{5,4},{6,7},{7,6},{8,9},{9,8},{10,11... | collective-permute-start | bytes 245768 | tf_op jit(solution)/shard_map/ppermute | solution.py:353
  21.4 0.0 collective-permute-done.6.swap_own
  21.4 0.0 collective-permute-done.7.swap_2
  21.4 0.8 %collective-permute-done.8.swap_3 = bf16[40,1024]{1,0:T(8,128)(2,1)S(1)} collective-permute-done((bf16[40,1024]{1,0:T(8,128)(2,1)S(1)}, bf16[40,1024]{1,0:T(8,128)(2,1)S(1)}, u32[]{:S(2)}, u32[]{:S(2)}) %collective-permute-start.8) | collective-permute-done | bytes 81952 | tf_op jit(solution)/shard_map/ppermute | solution.py:353
  22.2 0.2 collective-permute-done.9.swap_1
  22.3 0.7 %shard_map.99 = (bf16[32,1792]{1,0:T(8,128)(2,1)S(1)}, bf16[32,1792]{1,0:T(8,128)(2,1)S(1)}, bf16[32,1792]{1,0:T(8,128)(2,1)S(1)}, bf16[32,1792]{1,0:T(8,128)(2,1)S(1)}) custom-call(bf16[40,1024]{1,0:T(8,128)(2,1)S(1)} %get-tuple-element.24.own, bf16[40,1024]{1,0:T(8,128)(2,1)S(1)} %collective-permute-done.3.from_2, ...), custom_call_target="tpu_custom_call" | custom-call | bytes 1048576 | tf_op jit(solution)/shard_map/pallas_call | solution.py:328
  23.1 2.1 %collective-permute-start.10 = (bf16[32,1792]{1,0:T(8,128)(2,1)S(1)}, bf16[32,1792]{1,0:T(8,128)(2,1)S(1)}, u32[]{:S(2)}, u32[]{:S(2)}) collective-permute-start(bf16[32,1792]{1,0:T(8,128)(2,1)S(1)} %get-tuple-element.32), channel_id=1, source_target_pairs={{0,10},{1,11},{2,8},{3,9},{4,14},{5,15},{6,12},{7,13},{8,2},{9,3},... | collective-permute-start | bytes 344072 | tf_op jit(solution)/shard_map/ppermute | solution.py:353
  25.2 0.8 %collective-permute-start.11 = (bf16[32,1792]{1,0:T(8,128)(2,1)S(1)}, bf16[32,1792]{1,0:T(8,128)(2,1)S(1)}, u32[]{:S(2)}, u32[]{:S(2)}) collective-permute-start(bf16[32,1792]{1,0:T(8,128)(2,1)S(1)} %get-tuple-element.33), channel_id=1, source_target_pairs={{0,8},{1,9},{2,10},{3,11},{4,12},{5,13},{6,14},{7,15},{8,0},{9,1},... | collective-permute-start | bytes 344072 | tf_op jit(solution)/shard_map/ppermute | solution.py:353
  26.0 0.6 %collective-permute-start.12 = (bf16[32,1792]{1,0:T(8,128)(2,1)S(1)}, bf16[32,1792]{1,0:T(8,128)(2,1)S(1)}, u32[]{:S(2)}, u32[]{:S(2)}) collective-permute-start(bf16[32,1792]{1,0:T(8,128)(2,1)S(1)} %get-tuple-element.34), channel_id=1, source_target_pairs={{0,2},{1,3},{2,0},{3,1},{4,6},{5,7},{6,4},{7,5},{8,10},{9,11},{10,... | collective-permute-start | bytes 344072 | tf_op jit(solution)/shard_map/ppermute | solution.py:353
  26.6 0.0 collective-permute-done.13.from_x
  26.7 1.6 %collective-permute-start.14 = (bf16[40,896]{1,0:T(8,128)(2,1)S(1)}, bf16[40,896]{1,0:T(8,128)(2,1)S(1)}, u32[]{:S(2)}, u32[]{:S(2)}) collective-permute-start(bf16[40,896]{1,0:T(8,128)(2,1)S(1)} %get-tuple-element.39), channel_id=1, source_target_pairs={{0,16},{1,17},{2,18},{3,19},{4,20},{5,21},{6,22},{7,23},{8,24},{9,... | collective-permute-start | bytes 215048 | tf_op jit(solution)/shard_map/ppermute | solution.py:353
  28.3 2.8 %collective-permute-done.14.far = bf16[40,896]{1,0:T(8,128)(2,1)S(1)} collective-permute-done((bf16[40,896]{1,0:T(8,128)(2,1)S(1)}, bf16[40,896]{1,0:T(8,128)(2,1)S(1)}, u32[]{:S(2)}, u32[]{:S(2)}) %collective-permute-start.14) | collective-permute-done | bytes 71712 | tf_op jit(solution)/shard_map/ppermute | solution.py:353
  31.1 0.0 collective-permute-done.10.from_xz
  31.1 0.8 %collective-permute-done.11.from_x = bf16[32,1792]{1,0:T(8,128)(2,1)S(1)} collective-permute-done((bf16[32,1792]{1,0:T(8,128)(2,1)S(1)}, bf16[32,1792]{1,0:T(8,128)(2,1)S(1)}, u32[]{:S(2)}, u32[]{:S(2)}) %collective-permute-start.11) | collective-permute-done | bytes 114720 | tf_op jit(solution)/shard_map/ppermute | solution.py:353
  31.9 0.0 collective-permute-done.12.from_z
  31.9 1.4 %shard_map.101 = (bf16[1,64,7168]{2,1,0:T(8,128)(2,1)}, f32[1,32,7168]{2,1,0:T(8,128)}) custom-call(bf16[32,1792]{1,0:T(8,128)(2,1)S(1)} %get-tuple-element.31.own, bf16[32,1792]{1,0:T(8,128)(2,1)S(1)} %collective-permute-done.10.from_xz, bf16[32,1792]{1,0:T(8,128)(2,1)S(1)} %collective-permute-done.11.from_x, ...), custom_call_target="tpu_custom_call" | custom-call | bytes 4194304 | tf_op jit(solution)/shard_map/pallas_call | solution.py:328
  (1 shorter events, 0.0 us)
Async XLA Ops:
  2.4 7.8 %collective-permute-start.2 = (bf16[40,1024]{1,0:T(8,128)(2,1)S(1)}, bf16[40,1024]{1,0:T(8,128)(2,1)S(1)}, u32[]{:S(2)}, u32[]{:S(2)}) collective-permute-start(bf16[40,1024]{1,0:T(8,128)(2,1)S(1)} %get-tuple-element.22), channel_id=1, source_target_pairs={{0,24},{1,25},{2,26},{3,27},{4,28},{5,29},{6,30},{7,31},{8,16},{9,... | collective-permute-start | bytes 245768 | tf_op jit(solution)/shard_map/ppermute | solution.py:353
  6.3 4.4 %collective-permute-start.1 = (bf16[40,1024]{1,0:T(8,128)(2,1)S(1)}, bf16[40,1024]{1,0:T(8,128)(2,1)S(1)}, u32[]{:S(2)}, u32[]{:S(2)}) collective-permute-start(bf16[40,1024]{1,0:T(8,128)(2,1)S(1)} %get-tuple-element.22), channel_id=1, source_target_pairs={{0,16},{1,17},{2,18},{3,19},{4,20},{5,21},{6,22},{7,23},{8,24},{9,... | collective-permute-start | bytes 245768 | tf_op jit(solution)/shard_map/ppermute | solution.py:353
  6.9 4.4 %collective-permute-start = (bf16[40,1024]{1,0:T(8,128)(2,1)S(1)}, bf16[40,1024]{1,0:T(8,128)(2,1)S(1)}, u32[]{:S(2)}, u32[]{:S(2)}) collective-permute-start(bf16[40,1024]{1,0:T(8,128)(2,1)S(1)} %get-tuple-element.21.after.own), channel_id=1, source_target_pairs={{0,8},{1,9},{2,10},{3,11},{4,12},{5,13},{6,14},{7,15},{8,0},{9,1},... | collective-permute-start | bytes 245768 | tf_op jit(solution)/shard_map/ppermute | solution.py:353
  11.6 8.3 %collective-permute-start.3 = (bf16[40,1024]{1,0:T(8,128)(2,1)S(1)}, bf16[40,1024]{1,0:T(8,128)(2,1)S(1)}, u32[]{:S(2)}, u32[]{:S(2)}) collective-permute-start(bf16[40,1024]{1,0:T(8,128)(2,1)S(1)} %get-tuple-element.25), channel_id=1, source_target_pairs={{0,4},{1,5},{2,6},{3,7},{4,0},{5,1},{6,2},{7,3},{8,12},{9,13},{10,... | collective-permute-start | bytes 245768 | tf_op jit(solution)/shard_map/ppermute | solution.py:353
  14.3 6.6 %collective-permute-start.4 = (bf16[40,1024]{1,0:T(8,128)(2,1)S(1)}, bf16[40,1024]{1,0:T(8,128)(2,1)S(1)}, u32[]{:S(2)}, u32[]{:S(2)}) collective-permute-start(bf16[40,1024]{1,0:T(8,128)(2,1)S(1)} %get-tuple-element.26), channel_id=1, source_target_pairs={{0,6},{1,7},{2,4},{3,5},{4,2},{5,3},{6,0},{7,1},{8,14},{9,15},{10,... | collective-permute-start | bytes 245768 | tf_op jit(solution)/shard_map/ppermute | solution.py:353
  15.6 5.3 %collective-permute-start.5 = (bf16[40,1024]{1,0:T(8,128)(2,1)S(1)}, bf16[40,1024]{1,0:T(8,128)(2,1)S(1)}, u32[]{:S(2)}, u32[]{:S(2)}) collective-permute-start(bf16[40,1024]{1,0:T(8,128)(2,1)S(1)} %get-tuple-element.27), channel_id=1, source_target_pairs={{0,2},{1,3},{2,0},{3,1},{4,6},{5,7},{6,4},{7,5},{8,10},{9,11},{10,... | collective-permute-start | bytes 245768 | tf_op jit(solution)/shard_map/ppermute | solution.py:353
  18.9 7.7 %collective-permute-start.13 = (bf16[80,896]{1,0:T(8,128)(2,1)S(1)}, bf16[80,896]{1,0:T(8,128)(2,1)S(1)}, u32[]{:S(2)}, u32[]{:S(2)}) collective-permute-start(bf16[80,896]{1,0:T(8,128)(2,1)S(1)} %get-tuple-element.37), channel_id=1, source_target_pairs={{0,8},{1,9},{2,10},{3,11},{4,12},{5,13},{6,14},{7,15},{8,0},{9,1},... | collective-permute-start | bytes 430088 | tf_op jit(solution)/shard_map/ppermute | solution.py:353
  20.0 1.5 %collective-permute-start.6 = (bf16[40,1024]{1,0:T(8,128)(2,1)S(1)}, bf16[40,1024]{1,0:T(8,128)(2,1)S(1)}, u32[]{:S(2)}, u32[]{:S(2)}) collective-permute-start(bf16[40,1024]{1,0:T(8,128)(2,1)S(1)} %get-tuple-element.24.own), channel_id=1, source_target_pairs={{0,1},{1,0},{2,3},{3,2},{4,5},{5,4},{6,7},{7,6},{8,9},{9,8},{10,11... | collective-permute-start | bytes 245768 | tf_op jit(solution)/shard_map/ppermute | solution.py:353
  20.0 1.4 %collective-permute-start.7 = (bf16[40,1024]{1,0:T(8,128)(2,1)S(1)}, bf16[40,1024]{1,0:T(8,128)(2,1)S(1)}, u32[]{:S(2)}, u32[]{:S(2)}) collective-permute-start(bf16[40,1024]{1,0:T(8,128)(2,1)S(1)} %collective-permute-done.3.from_2), channel_id=1, source_target_pairs={{0,1},{1,0},{2,3},{3,2},{4,5},{5,4},{6,7},{7,6},{8,9},{9,8},{10,11... | collective-permute-start | bytes 245768 | tf_op jit(solution)/shard_map/ppermute | solution.py:353
  20.9 1.3 %collective-permute-start.8 = (bf16[40,1024]{1,0:T(8,128)(2,1)S(1)}, bf16[40,1024]{1,0:T(8,128)(2,1)S(1)}, u32[]{:S(2)}, u32[]{:S(2)}) collective-permute-start(bf16[40,1024]{1,0:T(8,128)(2,1)S(1)} %collective-permute-done.4.from_3), channel_id=1, source_target_pairs={{0,1},{1,0},{2,3},{3,2},{4,5},{5,4},{6,7},{7,6},{8,9},{9,8},{10,11... | collective-permute-start | bytes 245768 | tf_op jit(solution)/shard_map/ppermute | solution.py:353
  21.0 1.4 %collective-permute-start.9 = (bf16[40,1024]{1,0:T(8,128)(2,1)S(1)}, bf16[40,1024]{1,0:T(8,128)(2,1)S(1)}, u32[]{:S(2)}, u32[]{:S(2)}) collective-permute-start(bf16[40,1024]{1,0:T(8,128)(2,1)S(1)} %collective-permute-done.5.from_1), channel_id=1, source_target_pairs={{0,1},{1,0},{2,3},{3,2},{4,5},{5,4},{6,7},{7,6},{8,9},{9,8},{10,11... | collective-permute-start | bytes 245768 | tf_op jit(solution)/shard_map/ppermute | solution.py:353
  23.1 8.0 %collective-permute-start.10 = (bf16[32,1792]{1,0:T(8,128)(2,1)S(1)}, bf16[32,1792]{1,0:T(8,128)(2,1)S(1)}, u32[]{:S(2)}, u32[]{:S(2)}) collective-permute-start(bf16[32,1792]{1,0:T(8,128)(2,1)S(1)} %get-tuple-element.32), channel_id=1, source_target_pairs={{0,10},{1,11},{2,8},{3,9},{4,14},{5,15},{6,12},{7,13},{8,2},{9,3},... | collective-permute-start | bytes 344072 | tf_op jit(solution)/shard_map/ppermute | solution.py:353
  25.2 6.7 %collective-permute-start.11 = (bf16[32,1792]{1,0:T(8,128)(2,1)S(1)}, bf16[32,1792]{1,0:T(8,128)(2,1)S(1)}, u32[]{:S(2)}, u32[]{:S(2)}) collective-permute-start(bf16[32,1792]{1,0:T(8,128)(2,1)S(1)} %get-tuple-element.33), channel_id=1, source_target_pairs={{0,8},{1,9},{2,10},{3,11},{4,12},{5,13},{6,14},{7,15},{8,0},{9,1},... | collective-permute-start | bytes 344072 | tf_op jit(solution)/shard_map/ppermute | solution.py:353
  26.0 5.9 %collective-permute-start.12 = (bf16[32,1792]{1,0:T(8,128)(2,1)S(1)}, bf16[32,1792]{1,0:T(8,128)(2,1)S(1)}, u32[]{:S(2)}, u32[]{:S(2)}) collective-permute-start(bf16[32,1792]{1,0:T(8,128)(2,1)S(1)} %get-tuple-element.34), channel_id=1, source_target_pairs={{0,2},{1,3},{2,0},{3,1},{4,6},{5,7},{6,4},{7,5},{8,10},{9,11},{10,... | collective-permute-start | bytes 344072 | tf_op jit(solution)/shard_map/ppermute | solution.py:353
  26.7 4.4 %collective-permute-start.14 = (bf16[40,896]{1,0:T(8,128)(2,1)S(1)}, bf16[40,896]{1,0:T(8,128)(2,1)S(1)}, u32[]{:S(2)}, u32[]{:S(2)}) collective-permute-start(bf16[40,896]{1,0:T(8,128)(2,1)S(1)} %get-tuple-element.39), channel_id=1, source_target_pairs={{0,16},{1,17},{2,18},{3,19},{4,20},{5,21},{6,22},{7,23},{8,24},{9,... | collective-permute-start | bytes 215048 | tf_op jit(solution)/shard_map/ppermute | solution.py:353

commit v6 on v5

--- a/solution.py
+++ b/solution.py
@@ -250,17 +250,11 @@
     far[...] = (ret_y[...].astype(F32) + other[count:]).astype(BF16)
 
 
-def product_kernel(
-    scale, own, from_2, from_3, from_1, swap_own, swap_2, swap_3, swap_1, after, keep, to_xz, to_x,
-    to_z, stage
-):
-    refs = (own, from_2, from_3, from_1, swap_own, swap_2, swap_3, swap_1)
-    count = own.shape[0]
+def products(scale, refs, rows_dev, core):
+    count = refs[0].shape[0]
     cap = count // PIECES
     slots = 4 * cap
-    rows_dev = keep.shape[0]
-    piece_cols = keep.shape[1] // 2
-    _, loc, zb, _, core = place()
+    piece_cols = refs[0].shape[1] - 4 * rows_dev
     rows = jnp.concatenate([ref[:, :piece_cols].astype(F32) for ref in refs], 0).astype(BF16)
     m, n = iota((4 * count, count), 0), iota((4 * count, count), 1)
     mq = quotient(m, cap, 4 * count)
@@ -279,7 +273,20 @@
             first = hidden[2 * k * rows_dev : (2 * k + 1) * rows_dev]
             second = hidden[(2 * k + 1) * rows_dev : (2 * k + 2) * rows_dev]
             picks.append(jnp.where(core == 0, first, second).astype(BF16))
-    product = dot(jnp.concatenate(picks, 0), rows).astype(BF16)
+    return dot(jnp.concatenate(picks, 0), rows)
+
+
+def own_kernel(scale, own, from_2, from_3, from_1, after, total):
+    _, _, _, _, core = place()
+    total[...] = products(scale, (own, from_2, from_3, from_1), total.shape[0] // 8, core)
+
+
+def product_kernel(scale, mine, own, from_2, from_3, from_1, keep, to_xz, to_x, to_z, stage):
+    rows_dev = keep.shape[0]
+    piece_cols = keep.shape[1] // 2
+    _, loc, zb, _, core = place()
+    other = products(scale, (own, from_2, from_3, from_1), rows_dev, core)
+    product = (mine[...] + other).astype(BF16)
     for part in range(2):
         cols = slice(part * piece_cols, (part + 1) * piece_cols)
         for k in range(4):
@@ -289,32 +296,34 @@
         out[...] = stage[(2 * loc + zb) ^ k]
 
 
-def finish_kernel(
-    own, from_xz, from_x, from_z, names, near, far, tokens_hbm, down_hbm, tokens_out, down_out, sems
-):
-    cols = own.shape[1]
+def tokens_kernel(names, near, far, out_hbm, out, sems):
     count, piece_cols = near.shape
     cap = count // PIECES
-    tokens = tokens_out.shape[1]
-    _, loc, zb, _, _ = place()
-    copies = []
-
-    def send(source, target):
-        copy = pltpu.make_async_copy(source, target, sems.at[len(copies)])
-        copy.start()
-        copies.append(copy)
-
-    for k, ref in enumerate((own, from_z, from_x, from_xz)):
-        start = pl.multiple_of(((2 * loc + zb) ^ k) * cols, cols)
-        down_out[k] = ref[...].astype(F32)
-        send(down_out.at[k], down_hbm.at[0, :, pl.ds(start, cols)])
+    tokens = out.shape[1]
     both = jnp.concatenate([near[...].astype(F32), far[...].astype(F32)], 0).astype(BF16)
     token, lane = iota((tokens, 2 * count), 0), iota((tokens, 2 * count), 1)
     piece = quotient(lane, cap, 2 * count) % PIECES
     match = token == names[:1, : 2 * count]
+    copies = []
     for j in range(PIECES):
-        tokens_out[j] = dot(hot(match & (piece == j)), both).astype(BF16)
-        send(tokens_out.at[j], tokens_hbm.at[0, :, pl.ds(j * piece_cols, piece_cols)])
+        out[j] = dot(hot(match & (piece == j)), both).astype(BF16)
+        cols = slice(j * piece_cols, (j + 1) * piece_cols)
+        copies.append(pltpu.make_async_copy(out.at[j], out_hbm.at[0, :, cols], sems.at[j]))
+        copies[-1].start()
+    for copy in copies:
+        copy.wait()
+
+
+def join_kernel(own, from_xz, from_x, from_z, out_hbm, out, sems):
+    cols = own.shape[1]
+    _, loc, zb, _, _ = place()
+    copies = []
+    for k, ref in enumerate((own, from_z, from_x, from_xz)):
+        start = pl.multiple_of(((2 * loc + zb) ^ k) * cols, cols)
+        out[k] = ref[...].astype(F32)
+        copy = pltpu.make_async_copy(out.at[k], out_hbm.at[0, :, pl.ds(start, cols)], sems.at[k])
+        copy.start()
+        copies.append(copy)
     for copy in copies:
         copy.wait()
 
@@ -414,28 +423,44 @@
     parts = (mine, from_2, from_3, from_1)
     swapped = tuple(swap(x, dp_flip=1) for x in parts)
     block = ((rows_dev, 2 * piece_cols), BF16)
+    (half_sum,) = call(
+        functools.partial(own_kernel, 1.0 / replicas),
+        [((8 * rows_dev, piece_cols), F32)],
+        parts + (ret_own,),
+        [VM] * 4 + [ANY],
+        nbytes=1 << 20,
+    )
     own, to_xz, to_x, to_z = call(
         functools.partial(product_kernel, 1.0 / replicas),
         [block] * 4,
-        parts + swapped + (ret_own,),
-        [VM] * 8 + [ANY],
+        (half_sum,) + swapped,
         scratch=[pltpu.VMEM((4, rows_dev, 2 * piece_cols), BF16)],
         nbytes=1 << 20,
     )
     got_xz = swap(to_xz, loc_flip=1, dp_flip=2)
     got_z = swap(to_z, dp_flip=2)
     got_x = swap(to_x, loc_flip=1)
-    input_grad, down_grad = call(
-        finish_kernel,
-        [((1, tokens, model), BF16), ((1, rows_dev, model), F32)],
-        (own, got_xz, got_x, got_z, names, near_sum, back_y),
-        outs_specs=[ANY] * 2,
+    (input_grad,) = call(
+        tokens_kernel,
+        [((1, tokens, model), BF16)],
+        (names, near_sum, back_y),
+        outs_specs=[ANY],
         scratch=[
             pltpu.VMEM((PIECES, tokens, piece_cols), BF16),
+            pltpu.SemaphoreType.DMA((PIECES,)),
+        ],
+        nbytes=2 << 20,
+    )
+    (down_grad,) = call(
+        join_kernel,
+        [((1, rows_dev, model), F32)],
+        (own, got_xz, got_x, got_z),
+        outs_specs=[ANY],
+        scratch=[
             pltpu.VMEM((4, rows_dev, 2 * piece_cols), F32),
-            pltpu.SemaphoreType.DMA((4 + PIECES,)),
+            pltpu.SemaphoreType.DMA((4,)),
         ],
-        nbytes=4 << 20,
+        nbytes=1 << 20,
     )
     return (input_grad, down_grad)
 

time: 33.5 us -> 33.3 us (level)
  waiting for transfers between devices: 6.16 us -> 4.77 us
  Pallas kernels: 10.5 us -> 11.6 us
    ppermute x15, waiting for transfers between devices: 6.16 us -> 4.77 us  [swap(): return lax.ppermute(value, AXES, pairs)]
    pallas_call x7 -> x9, Pallas kernels: 10.5 us -> 11.6 us  [call(): pl.pallas_call(kernel, out_shape=out_shape, in_specs=specs or [VM] * len(...]
  transfers between devices with their start and end apart: 15 -> 15, of which waited for: 8 -> 7; matrix products, arithmetic and copies ran while one was open for 0% -> 0% of each run, Pallas kernels for 21% -> 26%
where the time goes in v6:
time: 33.3 us; the launch traced here: 33.1 us
  starting transfers between devices  16 us (48%)
  Pallas kernels  11.6 us (35%)
  waiting for transfers between devices  4.77 us (14%)
  between operations  0.74 us (2%)
    ppermute x15, starting transfers between devices, swap(): return lax.ppermute(value, AXES, pairs)  16 us
    pallas_call x9, Pallas kernels, call(): pl.pallas_call(kernel, out_shape=out_shape, in_specs=specs or [VM] * len(...  11.6 us
    ppermute x15, waiting for transfers between devices, swap(): return lax.ppermute(value, AXES, pairs)  4.77 us
  transfers between devices with their start and end apart: 15, of which 7 were waited for; matrix products, arithmetic and copies ran while one was open for 0% of the time, Pallas kernels for 26%

profile of v6, /device:TPU:0, one launch (start us, length us, event | category | flops | bytes accessed | tf_op | source)
XLA Modules:
  0.0 33.1 jit_solution(7515118118838017529)
XLA Ops:
  0.6 1.7 %shard_map.95 = (bf16[40,1024]{1,0:T(8,128)(2,1)S(1)}, bf16[40,1024]{1,0:T(8,128)(2,1)S(1)}, s32[8,128]{1,0:T(8,128)S(1)}) custom-call(s32[1,1,2,5]{3,2,1,0:T(2,128)} %tok_hbm.1, s32[1,1,2]{2,1,0:T(1,128)} %cnt_hbm.1, bf16[1,1,2,5]{3,2,1,0:T(2,128)(2,1)} %weight_hbm.1, bf16[1,64,7168]{2,1,0:T(8,128)(2,1)} %rows_hbm.1, bf16[1,1,20,256]{3,2,1,0:T(8,128)(2,1)} %hidden_hbm.1), custom_call_target="tpu_custom_call" | custom-call | bytes 917504 | tf_op jit(solution)/shard_map/pallas_call | solution.py:337
  2.4 4.0 %collective-permute-start.2 = (bf16[40,1024]{1,0:T(8,128)(2,1)S(1)}, bf16[40,1024]{1,0:T(8,128)(2,1)S(1)}, u32[]{:S(2)}, u32[]{:S(2)}) collective-permute-start(bf16[40,1024]{1,0:T(8,128)(2,1)S(1)} %get-tuple-element.23), channel_id=1, source_target_pairs={{0,24},{1,25},{2,26},{3,27},{4,28},{5,29},{6,30},{7,31},{8,16},{9,... | collective-permute-start | bytes 245768 | tf_op jit(solution)/shard_map/ppermute | solution.py:362
  6.3 0.5 %collective-permute-start.1 = (bf16[40,1024]{1,0:T(8,128)(2,1)S(1)}, bf16[40,1024]{1,0:T(8,128)(2,1)S(1)}, u32[]{:S(2)}, u32[]{:S(2)}) collective-permute-start(bf16[40,1024]{1,0:T(8,128)(2,1)S(1)} %get-tuple-element.23), channel_id=1, source_target_pairs={{0,16},{1,17},{2,18},{3,19},{4,20},{5,21},{6,22},{7,23},{8,24},{9,... | collective-permute-start | bytes 245768 | tf_op jit(solution)/shard_map/ppermute | solution.py:362
  6.9 0.1 collective-permute-start
  7.0 3.2 %shard_map.96 = (bf16[1,256,7168]{2,1,0:T(8,128)(2,1)S(1)}, bf16[1,7168,256]{2,1,0:T(8,128)(2,1)S(1)}, bf16[1,1,20,256]{3,2,1,0:T(8,128)(2,1)S(1)}) custom-call(bf16[1,256,7168]{2,1,0:T(8,128)(2,1)} %down_hbm.1, bf16[1,7168,256]{2,1,0:T(8,128)(2,1)} %up_hbm.1, bf16[1,1,20,256]{3,2,1,0:T(8,128)(2,1)} %gate_hbm.1, bf16[40,1024]{1,0:T(8,128)(2,1)S(1)} %get-tuple-element.22.after.own), custom_call_target="tpu_custom_call" | custom-call | bytes 14680064 | tf_op jit(solution)/shard_map/pallas_call | solution.py:337
  10.2 0.0 collective-permute-done.2.from_xy
  10.2 0.6 %collective-permute-done.1.from_y = bf16[40,1024]{1,0:T(8,128)(2,1)S(1)} collective-permute-done((bf16[40,1024]{1,0:T(8,128)(2,1)S(1)}, bf16[40,1024]{1,0:T(8,128)(2,1)S(1)}, u32[]{:S(2)}, u32[]{:S(2)}) %collective-permute-start.1) | collective-permute-done | bytes 81952 | tf_op jit(solution)/shard_map/ppermute | solution.py:362
  10.8 0.5 %collective-permute-done.from_x = bf16[40,1024]{1,0:T(8,128)(2,1)S(1)} collective-permute-done((bf16[40,1024]{1,0:T(8,128)(2,1)S(1)}, bf16[40,1024]{1,0:T(8,128)(2,1)S(1)}, u32[]{:S(2)}, u32[]{:S(2)}) %collective-permute-start) | collective-permute-done | bytes 81952 | tf_op jit(solution)/shard_map/ppermute | solution.py:362
  11.3 0.3 %shard_map.100 = (bf16[40,1024]{1,0:T(8,128)(2,1)S(1)}, bf16[40,1024]{1,0:T(8,128)(2,1)S(1)}, bf16[40,1024]{1,0:T(8,128)(2,1)S(1)}, bf16[40,1024]{1,0:T(8,128)(2,1)S(1)}) custom-call(bf16[40,1024]{1,0:T(8,128)(2,1)S(1)} %get-tuple-element.22.after.own, bf16[40,1024]{1,0:T(8,128)(2,1)S(1)} %collective-permute-done.from_x, ...), custom_call_target="tpu_custom_call" | custom-call | bytes 286720 | tf_op jit(solution)/shard_map/pallas_call | solution.py:337
  11.6 2.7 %collective-permute-start.5 = (bf16[40,1024]{1,0:T(8,128)(2,1)S(1)}, bf16[40,1024]{1,0:T(8,128)(2,1)S(1)}, u32[]{:S(2)}, u32[]{:S(2)}) collective-permute-start(bf16[40,1024]{1,0:T(8,128)(2,1)S(1)} %get-tuple-element.33), channel_id=1, source_target_pairs={{0,4},{1,5},{2,6},{3,7},{4,0},{5,1},{6,2},{7,3},{8,12},{9,13},{10,... | collective-permute-start | bytes 245768 | tf_op jit(solution)/shard_map/ppermute | solution.py:362
  14.3 1.3 %collective-permute-start.6 = (bf16[40,1024]{1,0:T(8,128)(2,1)S(1)}, bf16[40,1024]{1,0:T(8,128)(2,1)S(1)}, u32[]{:S(2)}, u32[]{:S(2)}) collective-permute-start(bf16[40,1024]{1,0:T(8,128)(2,1)S(1)} %get-tuple-element.34), channel_id=1, source_target_pairs={{0,6},{1,7},{2,4},{3,5},{4,2},{5,3},{6,0},{7,1},{8,14},{9,15},{10,... | collective-permute-start | bytes 245768 | tf_op jit(solution)/shard_map/ppermute | solution.py:362
  15.6 0.2 collective-permute-start.7
  15.9 3.0 %shard_map.97 = (bf16[40,896]{1,0:T(8,128)(2,1)S(1)}, bf16[40,896]{1,0:T(8,128)(2,1)S(1)}, bf16[80,896]{1,0:T(8,128)(2,1)S(1)}) custom-call(bf16[40,1024]{1,0:T(8,128)(2,1)S(1)} %get-tuple-element.22.after.own, bf16[40,1024]{1,0:T(8,128)(2,1)S(1)} %collective-permute-done.from_x, bf16[40,1024]{1,0:T(8,128)(2,1)S(1)} %collective-permute-done.1.from_y, ...), custom_call_target="tpu_custom_call" | custom-call | flops 234881024 | bytes 7340032 | tf_op jit(solution)/shard_map/pallas_call | solution.py:337
  18.9 1.1 %collective-permute-start.3 = (bf16[80,896]{1,0:T(8,128)(2,1)S(1)}, bf16[80,896]{1,0:T(8,128)(2,1)S(1)}, u32[]{:S(2)}, u32[]{:S(2)}) collective-permute-start(bf16[80,896]{1,0:T(8,128)(2,1)S(1)} %get-tuple-element.29), channel_id=1, source_target_pairs={{0,8},{1,9},{2,10},{3,11},{4,12},{5,13},{6,14},{7,15},{8,0},{9,1},... | collective-permute-start | bytes 430088 | tf_op jit(solution)/shard_map/ppermute | solution.py:362
  20.0 0.0 collective-permute-start.8
  20.0 0.0 collective-permute-done.5.from_2
  20.0 0.5 %collective-permute-start.9 = (bf16[40,1024]{1,0:T(8,128)(2,1)S(1)}, bf16[40,1024]{1,0:T(8,128)(2,1)S(1)}, u32[]{:S(2)}, u32[]{:S(2)}) collective-permute-start(bf16[40,1024]{1,0:T(8,128)(2,1)S(1)} %collective-permute-done.5.from_2), channel_id=1, source_target_pairs={{0,1},{1,0},{2,3},{3,2},{4,5},{5,4},{6,7},{7,6},{8,9},{9,8},{10,11... | collective-permute-start | bytes 245768 | tf_op jit(solution)/shard_map/ppermute | solution.py:362
  20.5 0.4 %collective-permute-done.6.from_3 = bf16[40,1024]{1,0:T(8,128)(2,1)S(1)} collective-permute-done((bf16[40,1024]{1,0:T(8,128)(2,1)S(1)}, bf16[40,1024]{1,0:T(8,128)(2,1)S(1)}, u32[]{:S(2)}, u32[]{:S(2)}) %collective-permute-start.6) | collective-permute-done | bytes 81952 | tf_op jit(solution)/shard_map/ppermute | solution.py:362
  20.9 0.0 collective-permute-start.10
  20.9 0.1 collective-permute-done.7.from_1
  21.0 0.4 %collective-permute-start.11 = (bf16[40,1024]{1,0:T(8,128)(2,1)S(1)}, bf16[40,1024]{1,0:T(8,128)(2,1)S(1)}, u32[]{:S(2)}, u32[]{:S(2)}) collective-permute-start(bf16[40,1024]{1,0:T(8,128)(2,1)S(1)} %collective-permute-done.7.from_1), channel_id=1, source_target_pairs={{0,1},{1,0},{2,3},{3,2},{4,5},{5,4},{6,7},{7,6},{8,9},{9,8},{10,11... | collective-permute-start | bytes 245768 | tf_op jit(solution)/shard_map/ppermute | solution.py:362
  21.4 0.6 %shard_map.101.mine = f32[256,896]{1,0:T(8,128)S(1)} custom-call(bf16[40,1024]{1,0:T(8,128)(2,1)S(1)} %get-tuple-element.32.own, bf16[40,1024]{1,0:T(8,128)(2,1)S(1)} %collective-permute-done.5.from_2, bf16[40,1024]{1,0:T(8,128)(2,1)S(1)} %collective-permute-done.6.from_3, bf16[40,1024]{1,0:T(8,128)(2,1)S(1)} %collective-permute-done.7.from_1, ...), custom_call_target="tpu_custom_call" | custom-call | bytes 1048576 | tf_op jit(solution)/shard_map/pallas_call | solution.py:337
  22.0 0.0 collective-permute-done.8.own
  22.0 0.0 collective-permute-done.9.from_2
  22.0 0.2 collective-permute-done.10.from_3
  22.2 0.2 collective-permute-done.11.from_1
  22.3 0.6 %shard_map.102 = (bf16[32,1792]{1,0:T(8,128)(2,1)S(1)}, bf16[32,1792]{1,0:T(8,128)(2,1)S(1)}, bf16[32,1792]{1,0:T(8,128)(2,1)S(1)}, bf16[32,1792]{1,0:T(8,128)(2,1)S(1)}) custom-call(f32[256,896]{1,0:T(8,128)S(1)} %shard_map.101.mine, bf16[40,1024]{1,0:T(8,128)(2,1)S(1)} %collective-permute-done.8.own, bf16[40,1024]{1,0:T(8,128)(2,1)S(1)} %collective-permute-done.9.from_2, ...), custom_call_target="tpu_custom_call" | custom-call | bytes 1048576 | tf_op jit(solution)/shard_map/pallas_call | solution.py:337
  22.9 2.1 %collective-permute-start.12 = (bf16[32,1792]{1,0:T(8,128)(2,1)S(1)}, bf16[32,1792]{1,0:T(8,128)(2,1)S(1)}, u32[]{:S(2)}, u32[]{:S(2)}) collective-permute-start(bf16[32,1792]{1,0:T(8,128)(2,1)S(1)} %get-tuple-element.37), channel_id=1, source_target_pairs={{0,10},{1,11},{2,8},{3,9},{4,14},{5,15},{6,12},{7,13},{8,2},{9,3},... | collective-permute-start | bytes 344072 | tf_op jit(solution)/shard_map/ppermute | solution.py:362
  25.1 0.8 %collective-permute-start.13 = (bf16[32,1792]{1,0:T(8,128)(2,1)S(1)}, bf16[32,1792]{1,0:T(8,128)(2,1)S(1)}, u32[]{:S(2)}, u32[]{:S(2)}) collective-permute-start(bf16[32,1792]{1,0:T(8,128)(2,1)S(1)} %get-tuple-element.38), channel_id=1, source_target_pairs={{0,8},{1,9},{2,10},{3,11},{4,12},{5,13},{6,14},{7,15},{8,0},{9,1},... | collective-permute-start | bytes 344072 | tf_op jit(solution)/shard_map/ppermute | solution.py:362
  25.9 0.6 %collective-permute-start.14 = (bf16[32,1792]{1,0:T(8,128)(2,1)S(1)}, bf16[32,1792]{1,0:T(8,128)(2,1)S(1)}, u32[]{:S(2)}, u32[]{:S(2)}) collective-permute-start(bf16[32,1792]{1,0:T(8,128)(2,1)S(1)} %get-tuple-element.39), channel_id=1, source_target_pairs={{0,2},{1,3},{2,0},{3,1},{4,6},{5,7},{6,4},{7,5},{8,10},{9,11},{10,... | collective-permute-start | bytes 344072 | tf_op jit(solution)/shard_map/ppermute | solution.py:362
  26.5 0.0 collective-permute-done.3.from_x
  26.5 1.6 %collective-permute-start.4 = (bf16[40,896]{1,0:T(8,128)(2,1)S(1)}, bf16[40,896]{1,0:T(8,128)(2,1)S(1)}, u32[]{:S(2)}, u32[]{:S(2)}) collective-permute-start(bf16[40,896]{1,0:T(8,128)(2,1)S(1)} %get-tuple-element.31), channel_id=1, source_target_pairs={{0,16},{1,17},{2,18},{3,19},{4,20},{5,21},{6,22},{7,23},{8,24},{9,... | collective-permute-start | bytes 215048 | tf_op jit(solution)/shard_map/ppermute | solution.py:362
  28.1 2.8 %collective-permute-done.4.far = bf16[40,896]{1,0:T(8,128)(2,1)S(1)} collective-permute-done((bf16[40,896]{1,0:T(8,128)(2,1)S(1)}, bf16[40,896]{1,0:T(8,128)(2,1)S(1)}, u32[]{:S(2)}, u32[]{:S(2)}) %collective-permute-start.4) | collective-permute-done | bytes 71712 | tf_op jit(solution)/shard_map/ppermute | solution.py:362
  30.9 1.1 %shard_map.99 = bf16[1,64,7168]{2,1,0:T(8,128)(2,1)} custom-call(s32[8,128]{1,0:T(8,128)S(1)} %get-tuple-element.21.names, bf16[40,896]{1,0:T(8,128)(2,1)S(1)} %get-tuple-element.30.near, bf16[40,896]{1,0:T(8,128)(2,1)S(1)} %collective-permute-done.4.far), custom_call_target="tpu_custom_call" | custom-call | bytes 2097152 | tf_op jit(solution)/shard_map/pallas_call | solution.py:337
  32.1 0.0 collective-permute-done.12.from_xz
  32.1 0.0 collective-permute-done.13.from_x
  32.1 0.0 collective-permute-done.14.from_z
  32.1 1.0 %shard_map.103 = f32[1,32,7168]{2,1,0:T(8,128)} custom-call(bf16[32,1792]{1,0:T(8,128)(2,1)S(1)} %get-tuple-element.36.own, bf16[32,1792]{1,0:T(8,128)(2,1)S(1)} %collective-permute-done.12.from_xz, bf16[32,1792]{1,0:T(8,128)(2,1)S(1)} %collective-permute-done.13.from_x, bf16[32,1792]{1,0:T(8,128)(2,1)S(1)} %collective-permute-done.14.from_z), custom_call_target="tpu_custom_call" | custom-call | bytes 1048576 | tf_op jit(solution)/shard_map/pallas_call | solution.py:337
  (1 shorter events, 0.0 us)
Async XLA Ops:
  2.4 7.8 %collective-permute-start.2 = (bf16[40,1024]{1,0:T(8,128)(2,1)S(1)}, bf16[40,1024]{1,0:T(8,128)(2,1)S(1)}, u32[]{:S(2)}, u32[]{:S(2)}) collective-permute-start(bf16[40,1024]{1,0:T(8,128)(2,1)S(1)} %get-tuple-element.23), channel_id=1, source_target_pairs={{0,24},{1,25},{2,26},{3,27},{4,28},{5,29},{6,30},{7,31},{8,16},{9,... | collective-permute-start | bytes 245768 | tf_op jit(solution)/shard_map/ppermute | solution.py:362
  6.3 4.4 %collective-permute-start.1 = (bf16[40,1024]{1,0:T(8,128)(2,1)S(1)}, bf16[40,1024]{1,0:T(8,128)(2,1)S(1)}, u32[]{:S(2)}, u32[]{:S(2)}) collective-permute-start(bf16[40,1024]{1,0:T(8,128)(2,1)S(1)} %get-tuple-element.23), channel_id=1, source_target_pairs={{0,16},{1,17},{2,18},{3,19},{4,20},{5,21},{6,22},{7,23},{8,24},{9,... | collective-permute-start | bytes 245768 | tf_op jit(solution)/shard_map/ppermute | solution.py:362
  6.9 4.4 %collective-permute-start = (bf16[40,1024]{1,0:T(8,128)(2,1)S(1)}, bf16[40,1024]{1,0:T(8,128)(2,1)S(1)}, u32[]{:S(2)}, u32[]{:S(2)}) collective-permute-start(bf16[40,1024]{1,0:T(8,128)(2,1)S(1)} %get-tuple-element.22.after.own), channel_id=1, source_target_pairs={{0,8},{1,9},{2,10},{3,11},{4,12},{5,13},{6,14},{7,15},{8,0},{9,1},... | collective-permute-start | bytes 245768 | tf_op jit(solution)/shard_map/ppermute | solution.py:362
  11.6 8.3 %collective-permute-start.5 = (bf16[40,1024]{1,0:T(8,128)(2,1)S(1)}, bf16[40,1024]{1,0:T(8,128)(2,1)S(1)}, u32[]{:S(2)}, u32[]{:S(2)}) collective-permute-start(bf16[40,1024]{1,0:T(8,128)(2,1)S(1)} %get-tuple-element.33), channel_id=1, source_target_pairs={{0,4},{1,5},{2,6},{3,7},{4,0},{5,1},{6,2},{7,3},{8,12},{9,13},{10,... | collective-permute-start | bytes 245768 | tf_op jit(solution)/shard_map/ppermute | solution.py:362
  14.3 6.6 %collective-permute-start.6 = (bf16[40,1024]{1,0:T(8,128)(2,1)S(1)}, bf16[40,1024]{1,0:T(8,128)(2,1)S(1)}, u32[]{:S(2)}, u32[]{:S(2)}) collective-permute-start(bf16[40,1024]{1,0:T(8,128)(2,1)S(1)} %get-tuple-element.34), channel_id=1, source_target_pairs={{0,6},{1,7},{2,4},{3,5},{4,2},{5,3},{6,0},{7,1},{8,14},{9,15},{10,... | collective-permute-start | bytes 245768 | tf_op jit(solution)/shard_map/ppermute | solution.py:362
  15.6 5.3 %collective-permute-start.7 = (bf16[40,1024]{1,0:T(8,128)(2,1)S(1)}, bf16[40,1024]{1,0:T(8,128)(2,1)S(1)}, u32[]{:S(2)}, u32[]{:S(2)}) collective-permute-start(bf16[40,1024]{1,0:T(8,128)(2,1)S(1)} %get-tuple-element.35), channel_id=1, source_target_pairs={{0,2},{1,3},{2,0},{3,1},{4,6},{5,7},{6,4},{7,5},{8,10},{9,11},{10,... | collective-permute-start | bytes 245768 | tf_op jit(solution)/shard_map/ppermute | solution.py:362
  18.9 7.6 %collective-permute-start.3 = (bf16[80,896]{1,0:T(8,128)(2,1)S(1)}, bf16[80,896]{1,0:T(8,128)(2,1)S(1)}, u32[]{:S(2)}, u32[]{:S(2)}) collective-permute-start(bf16[80,896]{1,0:T(8,128)(2,1)S(1)} %get-tuple-element.29), channel_id=1, source_target_pairs={{0,8},{1,9},{2,10},{3,11},{4,12},{5,13},{6,14},{7,15},{8,0},{9,1},... | collective-permute-start | bytes 430088 | tf_op jit(solution)/shard_map/ppermute | solution.py:362
  20.0 2.0 %collective-permute-start.8 = (bf16[40,1024]{1,0:T(8,128)(2,1)S(1)}, bf16[40,1024]{1,0:T(8,128)(2,1)S(1)}, u32[]{:S(2)}, u32[]{:S(2)}) collective-permute-start(bf16[40,1024]{1,0:T(8,128)(2,1)S(1)} %get-tuple-element.32.own), channel_id=1, source_target_pairs={{0,1},{1,0},{2,3},{3,2},{4,5},{5,4},{6,7},{7,6},{8,9},{9,8},{10,11... | collective-permute-start | bytes 245768 | tf_op jit(solution)/shard_map/ppermute | solution.py:362
  20.0 2.0 %collective-permute-start.9 = (bf16[40,1024]{1,0:T(8,128)(2,1)S(1)}, bf16[40,1024]{1,0:T(8,128)(2,1)S(1)}, u32[]{:S(2)}, u32[]{:S(2)}) collective-permute-start(bf16[40,1024]{1,0:T(8,128)(2,1)S(1)} %collective-permute-done.5.from_2), channel_id=1, source_target_pairs={{0,1},{1,0},{2,3},{3,2},{4,5},{5,4},{6,7},{7,6},{8,9},{9,8},{10,11... | collective-permute-start | bytes 245768 | tf_op jit(solution)/shard_map/ppermute | solution.py:362
  20.9 1.3 %collective-permute-start.10 = (bf16[40,1024]{1,0:T(8,128)(2,1)S(1)}, bf16[40,1024]{1,0:T(8,128)(2,1)S(1)}, u32[]{:S(2)}, u32[]{:S(2)}) collective-permute-start(bf16[40,1024]{1,0:T(8,128)(2,1)S(1)} %collective-permute-done.6.from_3), channel_id=1, source_target_pairs={{0,1},{1,0},{2,3},{3,2},{4,5},{5,4},{6,7},{7,6},{8,9},{9,8},{10,11... | collective-permute-start | bytes 245768 | tf_op jit(solution)/shard_map/ppermute | solution.py:362
  21.0 1.4 %collective-permute-start.11 = (bf16[40,1024]{1,0:T(8,128)(2,1)S(1)}, bf16[40,1024]{1,0:T(8,128)(2,1)S(1)}, u32[]{:S(2)}, u32[]{:S(2)}) collective-permute-start(bf16[40,1024]{1,0:T(8,128)(2,1)S(1)} %collective-permute-done.7.from_1), channel_id=1, source_target_pairs={{0,1},{1,0},{2,3},{3,2},{4,5},{5,4},{6,7},{7,6},{8,9},{9,8},{10,11... | collective-permute-start | bytes 245768 | tf_op jit(solution)/shard_map/ppermute | solution.py:362
  22.9 9.2 %collective-permute-start.12 = (bf16[32,1792]{1,0:T(8,128)(2,1)S(1)}, bf16[32,1792]{1,0:T(8,128)(2,1)S(1)}, u32[]{:S(2)}, u32[]{:S(2)}) collective-permute-start(bf16[32,1792]{1,0:T(8,128)(2,1)S(1)} %get-tuple-element.37), channel_id=1, source_target_pairs={{0,10},{1,11},{2,8},{3,9},{4,14},{5,15},{6,12},{7,13},{8,2},{9,3},... | collective-permute-start | bytes 344072 | tf_op jit(solution)/shard_map/ppermute | solution.py:362
  25.1 7.1 %collective-permute-start.13 = (bf16[32,1792]{1,0:T(8,128)(2,1)S(1)}, bf16[32,1792]{1,0:T(8,128)(2,1)S(1)}, u32[]{:S(2)}, u32[]{:S(2)}) collective-permute-start(bf16[32,1792]{1,0:T(8,128)(2,1)S(1)} %get-tuple-element.38), channel_id=1, source_target_pairs={{0,8},{1,9},{2,10},{3,11},{4,12},{5,13},{6,14},{7,15},{8,0},{9,1},... | collective-permute-start | bytes 344072 | tf_op jit(solution)/shard_map/ppermute | solution.py:362
  25.9 6.3 %collective-permute-start.14 = (bf16[32,1792]{1,0:T(8,128)(2,1)S(1)}, bf16[32,1792]{1,0:T(8,128)(2,1)S(1)}, u32[]{:S(2)}, u32[]{:S(2)}) collective-permute-start(bf16[32,1792]{1,0:T(8,128)(2,1)S(1)} %get-tuple-element.39), channel_id=1, source_target_pairs={{0,2},{1,3},{2,0},{3,1},{4,6},{5,7},{6,4},{7,5},{8,10},{9,11},{10,... | collective-permute-start | bytes 344072 | tf_op jit(solution)/shard_map/ppermute | solution.py:362
  26.5 4.4 %collective-permute-start.4 = (bf16[40,896]{1,0:T(8,128)(2,1)S(1)}, bf16[40,896]{1,0:T(8,128)(2,1)S(1)}, u32[]{:S(2)}, u32[]{:S(2)}) collective-permute-start(bf16[40,896]{1,0:T(8,128)(2,1)S(1)} %get-tuple-element.31), channel_id=1, source_target_pairs={{0,16},{1,17},{2,18},{3,19},{4,20},{5,21},{6,22},{7,23},{8,24},{9,... | collective-permute-start | bytes 215048 | tf_op jit(solution)/shard_map/ppermute | solution.py:362

commit v7 on v6

--- a/solution.py
+++ b/solution.py
@@ -114,8 +114,8 @@
         (tok_hbm, tok), (cnt_hbm, cnt), (weight_hbm, weight), (rows_hbm, rows), (hidden_hbm, hidden)
     )
     copies = [pltpu.make_async_copy(a, b, sems.at[i]) for i, (a, b) in enumerate(pairs)]
-    for copy in copies:
-        copy.start()
+    for i in (3, 0, 1, 2, 4):
+        copies[i].start()
     cap = tok.shape[3]
     group, _, _, _, _ = place()
     tokens, model = rows.shape[1], rows.shape[2]
@@ -264,7 +264,9 @@
     n_loc, n_row = nq >> 2, n - slots * (nq >> 2)
     ok = (m_has == m_part) & (m_loc == n_loc) & (m_source * cap + m_slot == n_row)
     place_rows = jnp.where(ok, scale, 0.0).astype(BF16)
-    spread = [dot(place_rows, ref[:, piece_cols:]) for ref in refs]
+    wide = 4 * rows_dev
+    every = dot(place_rows, jnp.concatenate([ref[:, piece_cols:] for ref in refs], 1))
+    spread = [every[:, k * wide : (k + 1) * wide] for k in range(len(refs))]
     picks = []
     for block in range(4):
         at = block * count
@@ -276,17 +278,18 @@
     return dot(jnp.concatenate(picks, 0), rows)
 
 
-def own_kernel(scale, own, from_2, from_3, from_1, after, total):
+def early_kernel(scale, own, from_2, from_3, from_1, swap_own, swap_2, after, total):
     _, _, _, _, core = place()
-    total[...] = products(scale, (own, from_2, from_3, from_1), total.shape[0] // 8, core)
-
-
-def product_kernel(scale, mine, own, from_2, from_3, from_1, keep, to_xz, to_x, to_z, stage):
+    refs = (own, from_2, from_3, from_1, swap_own, swap_2)
+    total[...] = products(scale, refs, total.shape[0] // 8, core)
+
+
+def product_kernel(scale, early, swap_3, swap_1, keep, to_xz, to_x, to_z, stage):
     rows_dev = keep.shape[0]
     piece_cols = keep.shape[1] // 2
     _, loc, zb, _, core = place()
-    other = products(scale, (own, from_2, from_3, from_1), rows_dev, core)
-    product = (mine[...] + other).astype(BF16)
+    late = products(scale, (swap_3, swap_1), rows_dev, core)
+    product = (early[...] + late).astype(BF16)
     for part in range(2):
         cols = slice(part * piece_cols, (part + 1) * piece_cols)
         for k in range(4):
@@ -296,7 +299,7 @@
         out[...] = stage[(2 * loc + zb) ^ k]
 
 
-def tokens_kernel(names, near, far, out_hbm, out, sems):
+def tokens_kernel(names, near, far, out):
     count, piece_cols = near.shape
     cap = count // PIECES
     tokens = out.shape[1]
@@ -304,24 +307,20 @@
     token, lane = iota((tokens, 2 * count), 0), iota((tokens, 2 * count), 1)
     piece = quotient(lane, cap, 2 * count) % PIECES
     match = token == names[:1, : 2 * count]
-    copies = []
     for j in range(PIECES):
-        out[j] = dot(hot(match & (piece == j)), both).astype(BF16)
-        cols = slice(j * piece_cols, (j + 1) * piece_cols)
-        copies.append(pltpu.make_async_copy(out.at[j], out_hbm.at[0, :, cols], sems.at[j]))
-        copies[-1].start()
-    for copy in copies:
-        copy.wait()
-
-
-def join_kernel(own, from_xz, from_x, from_z, out_hbm, out, sems):
+        total = dot(hot(match & (piece == j)), both).astype(BF16)
+        out[0, :, j * piece_cols : (j + 1) * piece_cols] = total
+
+
+def join_kernel(own, from_xz, from_x, from_z, summed, tokens_hbm, down_hbm, out, sems):
     cols = own.shape[1]
     _, loc, zb, _, _ = place()
-    copies = []
+    copies = [pltpu.make_async_copy(summed, tokens_hbm, sems.at[4])]
+    copies[0].start()
     for k, ref in enumerate((own, from_z, from_x, from_xz)):
         start = pl.multiple_of(((2 * loc + zb) ^ k) * cols, cols)
         out[k] = ref[...].astype(F32)
-        copy = pltpu.make_async_copy(out.at[k], out_hbm.at[0, :, pl.ds(start, cols)], sems.at[k])
+        copy = pltpu.make_async_copy(out.at[k], down_hbm.at[0, :, pl.ds(start, cols)], sems.at[k])
         copy.start()
         copies.append(copy)
     for copy in copies:
@@ -423,42 +422,37 @@
     parts = (mine, from_2, from_3, from_1)
     swapped = tuple(swap(x, dp_flip=1) for x in parts)
     block = ((rows_dev, 2 * piece_cols), BF16)
-    (half_sum,) = call(
-        functools.partial(own_kernel, 1.0 / replicas),
+    (early_sum,) = call(
+        functools.partial(early_kernel, 1.0 / replicas),
         [((8 * rows_dev, piece_cols), F32)],
-        parts + (ret_own,),
-        [VM] * 4 + [ANY],
+        parts + swapped[:2] + (ret_own,),
+        [VM] * 6 + [ANY],
         nbytes=1 << 20,
     )
     own, to_xz, to_x, to_z = call(
         functools.partial(product_kernel, 1.0 / replicas),
         [block] * 4,
-        (half_sum,) + swapped,
+        (early_sum,) + swapped[2:],
         scratch=[pltpu.VMEM((4, rows_dev, 2 * piece_cols), BF16)],
         nbytes=1 << 20,
     )
     got_xz = swap(to_xz, loc_flip=1, dp_flip=2)
     got_z = swap(to_z, dp_flip=2)
     got_x = swap(to_x, loc_flip=1)
-    (input_grad,) = call(
+    (summed,) = call(
         tokens_kernel,
         [((1, tokens, model), BF16)],
         (names, near_sum, back_y),
-        outs_specs=[ANY],
-        scratch=[
-            pltpu.VMEM((PIECES, tokens, piece_cols), BF16),
-            pltpu.SemaphoreType.DMA((PIECES,)),
-        ],
         nbytes=2 << 20,
     )
-    (down_grad,) = call(
+    input_grad, down_grad = call(
         join_kernel,
-        [((1, rows_dev, model), F32)],
-        (own, got_xz, got_x, got_z),
-        outs_specs=[ANY],
+        [((1, tokens, model), BF16), ((1, rows_dev, model), F32)],
+        (own, got_xz, got_x, got_z, summed),
+        outs_specs=[ANY] * 2,
         scratch=[
             pltpu.VMEM((4, rows_dev, 2 * piece_cols), F32),
-            pltpu.SemaphoreType.DMA((4,)),
+            pltpu.SemaphoreType.DMA((5,)),
         ],
         nbytes=1 << 20,
     )

time: 33.3 us -> 33.1 us (level)
  Pallas kernels: 11.6 us -> 11.1 us
  waiting for transfers between devices: 4.77 us -> 5.2 us
    pallas_call x9, Pallas kernels: 11.6 us -> 11.1 us  [call(): pl.pallas_call(kernel, out_shape=out_shape, in_specs=specs or [VM] * len(...]
    ppermute x15, waiting for transfers between devices: 4.77 us -> 5.2 us  [swap(): return lax.ppermute(value, AXES, pairs)]
  transfers between devices with their start and end apart: 15 -> 15, of which waited for: 7 -> 8; matrix products, arithmetic and copies ran while one was open for 0% -> 0% of each run, Pallas kernels for 26% -> 23%
where the time goes in v7:
time: 33.1 us; the launch traced here: 33 us
  starting transfers between devices  16 us (48%)
  Pallas kernels  11.1 us (34%)
  waiting for transfers between devices  5.2 us (16%)
  between operations  0.71 us (2%)
    ppermute x15, starting transfers between devices, swap(): return lax.ppermute(value, AXES, pairs)  16 us
    pallas_call x9, Pallas kernels, call(): pl.pallas_call(kernel, out_shape=out_shape, in_specs=specs or [VM] * len(...  11.1 us
    ppermute x15, waiting for transfers between devices, swap(): return lax.ppermute(value, AXES, pairs)  5.2 us
  transfers between devices with their start and end apart: 15, of which 8 were waited for; matrix products, arithmetic and copies ran while one was open for 0% of the time, Pallas kernels for 23%

profile of v7, /device:TPU:0, one launch (start us, length us, event | category | flops | bytes accessed | tf_op | source)
XLA Modules:
  0.0 33.0 jit_solution(16055513699332917892)
XLA Ops:
  0.6 1.7 %shard_map.95 = (bf16[40,1024]{1,0:T(8,128)(2,1)S(1)}, bf16[40,1024]{1,0:T(8,128)(2,1)S(1)}, s32[8,128]{1,0:T(8,128)S(1)}) custom-call(s32[1,1,2,5]{3,2,1,0:T(2,128)} %tok_hbm.1, s32[1,1,2]{2,1,0:T(1,128)} %cnt_hbm.1, bf16[1,1,2,5]{3,2,1,0:T(2,128)(2,1)} %weight_hbm.1, bf16[1,64,7168]{2,1,0:T(8,128)(2,1)} %rows_hbm.1, bf16[1,1,20,256]{3,2,1,0:T(8,128)(2,1)} %hidden_hbm.1), custom_call_target="tpu_custom_call" | custom-call | bytes 917504 | tf_op jit(solution)/shard_map/pallas_call | solution.py:336
  2.4 4.0 %collective-permute-start.2 = (bf16[40,1024]{1,0:T(8,128)(2,1)S(1)}, bf16[40,1024]{1,0:T(8,128)(2,1)S(1)}, u32[]{:S(2)}, u32[]{:S(2)}) collective-permute-start(bf16[40,1024]{1,0:T(8,128)(2,1)S(1)} %get-tuple-element.22), channel_id=1, source_target_pairs={{0,24},{1,25},{2,26},{3,27},{4,28},{5,29},{6,30},{7,31},{8,16},{9,... | collective-permute-start | bytes 245768 | tf_op jit(solution)/shard_map/ppermute | solution.py:361
  6.3 0.5 %collective-permute-start.1 = (bf16[40,1024]{1,0:T(8,128)(2,1)S(1)}, bf16[40,1024]{1,0:T(8,128)(2,1)S(1)}, u32[]{:S(2)}, u32[]{:S(2)}) collective-permute-start(bf16[40,1024]{1,0:T(8,128)(2,1)S(1)} %get-tuple-element.22), channel_id=1, source_target_pairs={{0,16},{1,17},{2,18},{3,19},{4,20},{5,21},{6,22},{7,23},{8,24},{9,... | collective-permute-start | bytes 245768 | tf_op jit(solution)/shard_map/ppermute | solution.py:361
  6.8 0.1 collective-permute-start
  7.0 3.2 %shard_map.96 = (bf16[1,256,7168]{2,1,0:T(8,128)(2,1)S(1)}, bf16[1,7168,256]{2,1,0:T(8,128)(2,1)S(1)}, bf16[1,1,20,256]{3,2,1,0:T(8,128)(2,1)S(1)}) custom-call(bf16[1,256,7168]{2,1,0:T(8,128)(2,1)} %down_hbm.1, bf16[1,7168,256]{2,1,0:T(8,128)(2,1)} %up_hbm.1, bf16[1,1,20,256]{3,2,1,0:T(8,128)(2,1)} %gate_hbm.1, bf16[40,1024]{1,0:T(8,128)(2,1)S(1)} %get-tuple-element.21.after.own), custom_call_target="tpu_custom_call" | custom-call | bytes 14680064 | tf_op jit(solution)/shard_map/pallas_call | solution.py:336
  10.2 0.0 collective-permute-done.2.from_xy
  10.2 0.6 %collective-permute-done.1.from_y = bf16[40,1024]{1,0:T(8,128)(2,1)S(1)} collective-permute-done((bf16[40,1024]{1,0:T(8,128)(2,1)S(1)}, bf16[40,1024]{1,0:T(8,128)(2,1)S(1)}, u32[]{:S(2)}, u32[]{:S(2)}) %collective-permute-start.1) | collective-permute-done | bytes 81952 | tf_op jit(solution)/shard_map/ppermute | solution.py:361
  10.8 0.5 %collective-permute-done.from_x = bf16[40,1024]{1,0:T(8,128)(2,1)S(1)} collective-permute-done((bf16[40,1024]{1,0:T(8,128)(2,1)S(1)}, bf16[40,1024]{1,0:T(8,128)(2,1)S(1)}, u32[]{:S(2)}, u32[]{:S(2)}) %collective-permute-start) | collective-permute-done | bytes 81952 | tf_op jit(solution)/shard_map/ppermute | solution.py:361
  11.3 0.3 %shard_map.97 = (bf16[40,1024]{1,0:T(8,128)(2,1)S(1)}, bf16[40,1024]{1,0:T(8,128)(2,1)S(1)}, bf16[40,1024]{1,0:T(8,128)(2,1)S(1)}, bf16[40,1024]{1,0:T(8,128)(2,1)S(1)}) custom-call(bf16[40,1024]{1,0:T(8,128)(2,1)S(1)} %get-tuple-element.21.after.own, bf16[40,1024]{1,0:T(8,128)(2,1)S(1)} %collective-permute-done.from_x, ...), custom_call_target="tpu_custom_call" | custom-call | bytes 286720 | tf_op jit(solution)/shard_map/pallas_call | solution.py:336
  11.6 2.6 %collective-permute-start.3 = (bf16[40,1024]{1,0:T(8,128)(2,1)S(1)}, bf16[40,1024]{1,0:T(8,128)(2,1)S(1)}, u32[]{:S(2)}, u32[]{:S(2)}) collective-permute-start(bf16[40,1024]{1,0:T(8,128)(2,1)S(1)} %get-tuple-element.25), channel_id=1, source_target_pairs={{0,4},{1,5},{2,6},{3,7},{4,0},{5,1},{6,2},{7,3},{8,12},{9,13},{10,... | collective-permute-start | bytes 245768 | tf_op jit(solution)/shard_map/ppermute | solution.py:361
  14.3 1.4 %collective-permute-start.4 = (bf16[40,1024]{1,0:T(8,128)(2,1)S(1)}, bf16[40,1024]{1,0:T(8,128)(2,1)S(1)}, u32[]{:S(2)}, u32[]{:S(2)}) collective-permute-start(bf16[40,1024]{1,0:T(8,128)(2,1)S(1)} %get-tuple-element.26), channel_id=1, source_target_pairs={{0,6},{1,7},{2,4},{3,5},{4,2},{5,3},{6,0},{7,1},{8,14},{9,15},{10,... | collective-permute-start | bytes 245768 | tf_op jit(solution)/shard_map/ppermute | solution.py:361
  15.6 0.2 collective-permute-start.5
  15.9 3.0 %shard_map.98 = (bf16[40,896]{1,0:T(8,128)(2,1)S(1)}, bf16[40,896]{1,0:T(8,128)(2,1)S(1)}, bf16[80,896]{1,0:T(8,128)(2,1)S(1)}) custom-call(bf16[40,1024]{1,0:T(8,128)(2,1)S(1)} %get-tuple-element.21.after.own, bf16[40,1024]{1,0:T(8,128)(2,1)S(1)} %collective-permute-done.from_x, bf16[40,1024]{1,0:T(8,128)(2,1)S(1)} %collective-permute-done.1.from_y, ...), custom_call_target="tpu_custom_call" | custom-call | flops 234881024 | bytes 7340032 | tf_op jit(solution)/shard_map/pallas_call | solution.py:336
  18.9 1.1 %collective-permute-start.13 = (bf16[80,896]{1,0:T(8,128)(2,1)S(1)}, bf16[80,896]{1,0:T(8,128)(2,1)S(1)}, u32[]{:S(2)}, u32[]{:S(2)}) collective-permute-start(bf16[80,896]{1,0:T(8,128)(2,1)S(1)} %get-tuple-element.37), channel_id=1, source_target_pairs={{0,8},{1,9},{2,10},{3,11},{4,12},{5,13},{6,14},{7,15},{8,0},{9,1},... | collective-permute-start | bytes 430088 | tf_op jit(solution)/shard_map/ppermute | solution.py:361
  20.0 0.0 collective-permute-start.6
  20.0 0.0 collective-permute-done.3.from_2
  20.0 0.5 %collective-permute-start.7 = (bf16[40,1024]{1,0:T(8,128)(2,1)S(1)}, bf16[40,1024]{1,0:T(8,128)(2,1)S(1)}, u32[]{:S(2)}, u32[]{:S(2)}) collective-permute-start(bf16[40,1024]{1,0:T(8,128)(2,1)S(1)} %collective-permute-done.3.from_2), channel_id=1, source_target_pairs={{0,1},{1,0},{2,3},{3,2},{4,5},{5,4},{6,7},{7,6},{8,9},{9,8},{10,11... | collective-permute-start | bytes 245768 | tf_op jit(solution)/shard_map/ppermute | solution.py:361
  20.5 0.4 %collective-permute-done.4.from_3 = bf16[40,1024]{1,0:T(8,128)(2,1)S(1)} collective-permute-done((bf16[40,1024]{1,0:T(8,128)(2,1)S(1)}, bf16[40,1024]{1,0:T(8,128)(2,1)S(1)}, u32[]{:S(2)}, u32[]{:S(2)}) %collective-permute-start.4) | collective-permute-done | bytes 81952 | tf_op jit(solution)/shard_map/ppermute | solution.py:361
  20.9 0.0 collective-permute-start.8
  20.9 0.1 collective-permute-done.5.from_1
  21.0 0.4 %collective-permute-start.9 = (bf16[40,1024]{1,0:T(8,128)(2,1)S(1)}, bf16[40,1024]{1,0:T(8,128)(2,1)S(1)}, u32[]{:S(2)}, u32[]{:S(2)}) collective-permute-start(bf16[40,1024]{1,0:T(8,128)(2,1)S(1)} %collective-permute-done.5.from_1), channel_id=1, source_target_pairs={{0,1},{1,0},{2,3},{3,2},{4,5},{5,4},{6,7},{7,6},{8,9},{9,8},{10,11... | collective-permute-start | bytes 245768 | tf_op jit(solution)/shard_map/ppermute | solution.py:361
  21.4 0.0 collective-permute-done.6.swap_own
  21.4 0.0 collective-permute-done.7.swap_2
  21.4 0.6 %shard_map.99.early = f32[256,896]{1,0:T(8,128)S(1)} custom-call(bf16[40,1024]{1,0:T(8,128)(2,1)S(1)} %get-tuple-element.24.own, bf16[40,1024]{1,0:T(8,128)(2,1)S(1)} %collective-permute-done.3.from_2, bf16[40,1024]{1,0:T(8,128)(2,1)S(1)} %collective-permute-done.4.from_3, bf16[40,1024]{1,0:T(8,128)(2,1)S(1)} %collective-permute-done.5.from_1, ...), custom_call_target="tpu_custom_call" | custom-call | bytes 1048576 | tf_op jit(solution)/shard_map/pallas_call | solution.py:336
  22.0 0.2 collective-permute-done.8.swap_3
  22.2 0.2 collective-permute-done.9.swap_1
  22.3 0.5 %shard_map.100 = (bf16[32,1792]{1,0:T(8,128)(2,1)S(1)}, bf16[32,1792]{1,0:T(8,128)(2,1)S(1)}, bf16[32,1792]{1,0:T(8,128)(2,1)S(1)}, bf16[32,1792]{1,0:T(8,128)(2,1)S(1)}) custom-call(f32[256,896]{1,0:T(8,128)S(1)} %shard_map.99.early, bf16[40,1024]{1,0:T(8,128)(2,1)S(1)} %collective-permute-done.8.swap_3, bf16[40,1024]{1,0:T(8,128)(2,1)S(1)} %collective-permute-done.9.swap_1), custom_call_target="tpu_custom_call" | custom-call | bytes 1048576 | tf_op jit(solution)/shard_map/pallas_call | solution.py:336
  22.9 2.1 %collective-permute-start.10 = (bf16[32,1792]{1,0:T(8,128)(2,1)S(1)}, bf16[32,1792]{1,0:T(8,128)(2,1)S(1)}, u32[]{:S(2)}, u32[]{:S(2)}) collective-permute-start(bf16[32,1792]{1,0:T(8,128)(2,1)S(1)} %get-tuple-element.32), channel_id=1, source_target_pairs={{0,10},{1,11},{2,8},{3,9},{4,14},{5,15},{6,12},{7,13},{8,2},{9,3},... | collective-permute-start | bytes 344072 | tf_op jit(solution)/shard_map/ppermute | solution.py:361
  25.0 0.9 %collective-permute-start.11 = (bf16[32,1792]{1,0:T(8,128)(2,1)S(1)}, bf16[32,1792]{1,0:T(8,128)(2,1)S(1)}, u32[]{:S(2)}, u32[]{:S(2)}) collective-permute-start(bf16[32,1792]{1,0:T(8,128)(2,1)S(1)} %get-tuple-element.33), channel_id=1, source_target_pairs={{0,8},{1,9},{2,10},{3,11},{4,12},{5,13},{6,14},{7,15},{8,0},{9,1},... | collective-permute-start | bytes 344072 | tf_op jit(solution)/shard_map/ppermute | solution.py:361
  25.8 0.6 %collective-permute-start.12 = (bf16[32,1792]{1,0:T(8,128)(2,1)S(1)}, bf16[32,1792]{1,0:T(8,128)(2,1)S(1)}, u32[]{:S(2)}, u32[]{:S(2)}) collective-permute-start(bf16[32,1792]{1,0:T(8,128)(2,1)S(1)} %get-tuple-element.34), channel_id=1, source_target_pairs={{0,2},{1,3},{2,0},{3,1},{4,6},{5,7},{6,4},{7,5},{8,10},{9,11},{10,... | collective-permute-start | bytes 344072 | tf_op jit(solution)/shard_map/ppermute | solution.py:361
  26.4 0.0 collective-permute-done.13.from_x
  26.5 1.6 %collective-permute-start.14 = (bf16[40,896]{1,0:T(8,128)(2,1)S(1)}, bf16[40,896]{1,0:T(8,128)(2,1)S(1)}, u32[]{:S(2)}, u32[]{:S(2)}) collective-permute-start(bf16[40,896]{1,0:T(8,128)(2,1)S(1)} %get-tuple-element.39), channel_id=1, source_target_pairs={{0,16},{1,17},{2,18},{3,19},{4,20},{5,21},{6,22},{7,23},{8,24},{9,... | collective-permute-start | bytes 215048 | tf_op jit(solution)/shard_map/ppermute | solution.py:361
  28.0 2.8 %collective-permute-done.14.far = bf16[40,896]{1,0:T(8,128)(2,1)S(1)} collective-permute-done((bf16[40,896]{1,0:T(8,128)(2,1)S(1)}, bf16[40,896]{1,0:T(8,128)(2,1)S(1)}, u32[]{:S(2)}, u32[]{:S(2)}) %collective-permute-start.14) | collective-permute-done | bytes 71712 | tf_op jit(solution)/shard_map/ppermute | solution.py:361
  30.9 0.4 %shard_map.102.summed = bf16[1,64,7168]{2,1,0:T(8,128)(2,1)S(1)} custom-call(s32[8,128]{1,0:T(8,128)S(1)} %get-tuple-element.35.names, bf16[40,896]{1,0:T(8,128)(2,1)S(1)} %get-tuple-element.38.near, bf16[40,896]{1,0:T(8,128)(2,1)S(1)} %collective-permute-done.14.far), custom_call_target="tpu_custom_call" | custom-call | bytes 2097152 | tf_op jit(solution)/shard_map/pallas_call | solution.py:336
  31.2 0.0 collective-permute-done.10.from_xz
  31.3 0.4 %collective-permute-done.11.from_x = bf16[32,1792]{1,0:T(8,128)(2,1)S(1)} collective-permute-done((bf16[32,1792]{1,0:T(8,128)(2,1)S(1)}, bf16[32,1792]{1,0:T(8,128)(2,1)S(1)}, u32[]{:S(2)}, u32[]{:S(2)}) %collective-permute-start.11) | collective-permute-done | bytes 114720 | tf_op jit(solution)/shard_map/ppermute | solution.py:361
  31.7 0.0 collective-permute-done.12.from_z
  31.7 1.3 %shard_map.103 = (bf16[1,64,7168]{2,1,0:T(8,128)(2,1)}, f32[1,32,7168]{2,1,0:T(8,128)}) custom-call(bf16[32,1792]{1,0:T(8,128)(2,1)S(1)} %get-tuple-element.31.own, bf16[32,1792]{1,0:T(8,128)(2,1)S(1)} %collective-permute-done.10.from_xz, bf16[32,1792]{1,0:T(8,128)(2,1)S(1)} %collective-permute-done.11.from_x, ...), custom_call_target="tpu_custom_call" | custom-call | bytes 1048576 | tf_op jit(solution)/shard_map/pallas_call | solution.py:336
  (1 shorter events, 0.0 us)
Async XLA Ops:
  2.4 7.8 %collective-permute-start.2 = (bf16[40,1024]{1,0:T(8,128)(2,1)S(1)}, bf16[40,1024]{1,0:T(8,128)(2,1)S(1)}, u32[]{:S(2)}, u32[]{:S(2)}) collective-permute-start(bf16[40,1024]{1,0:T(8,128)(2,1)S(1)} %get-tuple-element.22), channel_id=1, source_target_pairs={{0,24},{1,25},{2,26},{3,27},{4,28},{5,29},{6,30},{7,31},{8,16},{9,... | collective-permute-start | bytes 245768 | tf_op jit(solution)/shard_map/ppermute | solution.py:361
  6.3 4.4 %collective-permute-start.1 = (bf16[40,1024]{1,0:T(8,128)(2,1)S(1)}, bf16[40,1024]{1,0:T(8,128)(2,1)S(1)}, u32[]{:S(2)}, u32[]{:S(2)}) collective-permute-start(bf16[40,1024]{1,0:T(8,128)(2,1)S(1)} %get-tuple-element.22), channel_id=1, source_target_pairs={{0,16},{1,17},{2,18},{3,19},{4,20},{5,21},{6,22},{7,23},{8,24},{9,... | collective-permute-start | bytes 245768 | tf_op jit(solution)/shard_map/ppermute | solution.py:361
  6.8 4.4 %collective-permute-start = (bf16[40,1024]{1,0:T(8,128)(2,1)S(1)}, bf16[40,1024]{1,0:T(8,128)(2,1)S(1)}, u32[]{:S(2)}, u32[]{:S(2)}) collective-permute-start(bf16[40,1024]{1,0:T(8,128)(2,1)S(1)} %get-tuple-element.21.after.own), channel_id=1, source_target_pairs={{0,8},{1,9},{2,10},{3,11},{4,12},{5,13},{6,14},{7,15},{8,0},{9,1},... | collective-permute-start | bytes 245768 | tf_op jit(solution)/shard_map/ppermute | solution.py:361
  11.6 8.3 %collective-permute-start.3 = (bf16[40,1024]{1,0:T(8,128)(2,1)S(1)}, bf16[40,1024]{1,0:T(8,128)(2,1)S(1)}, u32[]{:S(2)}, u32[]{:S(2)}) collective-permute-start(bf16[40,1024]{1,0:T(8,128)(2,1)S(1)} %get-tuple-element.25), channel_id=1, source_target_pairs={{0,4},{1,5},{2,6},{3,7},{4,0},{5,1},{6,2},{7,3},{8,12},{9,13},{10,... | collective-permute-start | bytes 245768 | tf_op jit(solution)/shard_map/ppermute | solution.py:361
  14.3 6.6 %collective-permute-start.4 = (bf16[40,1024]{1,0:T(8,128)(2,1)S(1)}, bf16[40,1024]{1,0:T(8,128)(2,1)S(1)}, u32[]{:S(2)}, u32[]{:S(2)}) collective-permute-start(bf16[40,1024]{1,0:T(8,128)(2,1)S(1)} %get-tuple-element.26), channel_id=1, source_target_pairs={{0,6},{1,7},{2,4},{3,5},{4,2},{5,3},{6,0},{7,1},{8,14},{9,15},{10,... | collective-permute-start | bytes 245768 | tf_op jit(solution)/shard_map/ppermute | solution.py:361
  15.6 5.3 %collective-permute-start.5 = (bf16[40,1024]{1,0:T(8,128)(2,1)S(1)}, bf16[40,1024]{1,0:T(8,128)(2,1)S(1)}, u32[]{:S(2)}, u32[]{:S(2)}) collective-permute-start(bf16[40,1024]{1,0:T(8,128)(2,1)S(1)} %get-tuple-element.27), channel_id=1, source_target_pairs={{0,2},{1,3},{2,0},{3,1},{4,6},{5,7},{6,4},{7,5},{8,10},{9,11},{10,... | collective-permute-start | bytes 245768 | tf_op jit(solution)/shard_map/ppermute | solution.py:361
  18.9 7.5 %collective-permute-start.13 = (bf16[80,896]{1,0:T(8,128)(2,1)S(1)}, bf16[80,896]{1,0:T(8,128)(2,1)S(1)}, u32[]{:S(2)}, u32[]{:S(2)}) collective-permute-start(bf16[80,896]{1,0:T(8,128)(2,1)S(1)} %get-tuple-element.37), channel_id=1, source_target_pairs={{0,8},{1,9},{2,10},{3,11},{4,12},{5,13},{6,14},{7,15},{8,0},{9,1},... | collective-permute-start | bytes 430088 | tf_op jit(solution)/shard_map/ppermute | solution.py:361
  20.0 1.5 %collective-permute-start.6 = (bf16[40,1024]{1,0:T(8,128)(2,1)S(1)}, bf16[40,1024]{1,0:T(8,128)(2,1)S(1)}, u32[]{:S(2)}, u32[]{:S(2)}) collective-permute-start(bf16[40,1024]{1,0:T(8,128)(2,1)S(1)} %get-tuple-element.24.own), channel_id=1, source_target_pairs={{0,1},{1,0},{2,3},{3,2},{4,5},{5,4},{6,7},{7,6},{8,9},{9,8},{10,11... | collective-permute-start | bytes 245768 | tf_op jit(solution)/shard_map/ppermute | solution.py:361
  20.0 1.4 %collective-permute-start.7 = (bf16[40,1024]{1,0:T(8,128)(2,1)S(1)}, bf16[40,1024]{1,0:T(8,128)(2,1)S(1)}, u32[]{:S(2)}, u32[]{:S(2)}) collective-permute-start(bf16[40,1024]{1,0:T(8,128)(2,1)S(1)} %collective-permute-done.3.from_2), channel_id=1, source_target_pairs={{0,1},{1,0},{2,3},{3,2},{4,5},{5,4},{6,7},{7,6},{8,9},{9,8},{10,11... | collective-permute-start | bytes 245768 | tf_op jit(solution)/shard_map/ppermute | solution.py:361
  20.9 1.3 %collective-permute-start.8 = (bf16[40,1024]{1,0:T(8,128)(2,1)S(1)}, bf16[40,1024]{1,0:T(8,128)(2,1)S(1)}, u32[]{:S(2)}, u32[]{:S(2)}) collective-permute-start(bf16[40,1024]{1,0:T(8,128)(2,1)S(1)} %collective-permute-done.4.from_3), channel_id=1, source_target_pairs={{0,1},{1,0},{2,3},{3,2},{4,5},{5,4},{6,7},{7,6},{8,9},{9,8},{10,11... | collective-permute-start | bytes 245768 | tf_op jit(solution)/shard_map/ppermute | solution.py:361
  21.0 1.4 %collective-permute-start.9 = (bf16[40,1024]{1,0:T(8,128)(2,1)S(1)}, bf16[40,1024]{1,0:T(8,128)(2,1)S(1)}, u32[]{:S(2)}, u32[]{:S(2)}) collective-permute-start(bf16[40,1024]{1,0:T(8,128)(2,1)S(1)} %collective-permute-done.5.from_1), channel_id=1, source_target_pairs={{0,1},{1,0},{2,3},{3,2},{4,5},{5,4},{6,7},{7,6},{8,9},{9,8},{10,11... | collective-permute-start | bytes 245768 | tf_op jit(solution)/shard_map/ppermute | solution.py:361
  22.9 8.4 %collective-permute-start.10 = (bf16[32,1792]{1,0:T(8,128)(2,1)S(1)}, bf16[32,1792]{1,0:T(8,128)(2,1)S(1)}, u32[]{:S(2)}, u32[]{:S(2)}) collective-permute-start(bf16[32,1792]{1,0:T(8,128)(2,1)S(1)} %get-tuple-element.32), channel_id=1, source_target_pairs={{0,10},{1,11},{2,8},{3,9},{4,14},{5,15},{6,12},{7,13},{8,2},{9,3},... | collective-permute-start | bytes 344072 | tf_op jit(solution)/shard_map/ppermute | solution.py:361
  25.0 6.7 %collective-permute-start.11 = (bf16[32,1792]{1,0:T(8,128)(2,1)S(1)}, bf16[32,1792]{1,0:T(8,128)(2,1)S(1)}, u32[]{:S(2)}, u32[]{:S(2)}) collective-permute-start(bf16[32,1792]{1,0:T(8,128)(2,1)S(1)} %get-tuple-element.33), channel_id=1, source_target_pairs={{0,8},{1,9},{2,10},{3,11},{4,12},{5,13},{6,14},{7,15},{8,0},{9,1},... | collective-permute-start | bytes 344072 | tf_op jit(solution)/shard_map/ppermute | solution.py:361
  25.8 5.8 %collective-permute-start.12 = (bf16[32,1792]{1,0:T(8,128)(2,1)S(1)}, bf16[32,1792]{1,0:T(8,128)(2,1)S(1)}, u32[]{:S(2)}, u32[]{:S(2)}) collective-permute-start(bf16[32,1792]{1,0:T(8,128)(2,1)S(1)} %get-tuple-element.34), channel_id=1, source_target_pairs={{0,2},{1,3},{2,0},{3,1},{4,6},{5,7},{6,4},{7,5},{8,10},{9,11},{10,... | collective-permute-start | bytes 344072 | tf_op jit(solution)/shard_map/ppermute | solution.py:361
  26.5 4.4 %collective-permute-start.14 = (bf16[40,896]{1,0:T(8,128)(2,1)S(1)}, bf16[40,896]{1,0:T(8,128)(2,1)S(1)}, u32[]{:S(2)}, u32[]{:S(2)}) collective-permute-start(bf16[40,896]{1,0:T(8,128)(2,1)S(1)} %get-tuple-element.39), channel_id=1, source_target_pairs={{0,16},{1,17},{2,18},{3,19},{4,20},{5,21},{6,22},{7,23},{8,24},{9,... | collective-permute-start | bytes 215048 | tf_op jit(solution)/shard_map/ppermute | solution.py:361

commit v8 on v7

--- a/solution.py
+++ b/solution.py
@@ -312,7 +312,7 @@
         out[0, :, j * piece_cols : (j + 1) * piece_cols] = total
 
 
-def join_kernel(own, from_xz, from_x, from_z, summed, tokens_hbm, down_hbm, out, sems):
+def join_kernel(own, from_xz, from_z, from_x, summed, tokens_hbm, down_hbm, out, sems):
     cols = own.shape[1]
     _, loc, zb, _, _ = place()
     copies = [pltpu.make_async_copy(summed, tokens_hbm, sems.at[4])]
@@ -448,7 +448,7 @@
     input_grad, down_grad = call(
         join_kernel,
         [((1, tokens, model), BF16), ((1, rows_dev, model), F32)],
-        (own, got_xz, got_x, got_z, summed),
+        (own, got_xz, got_z, got_x, summed),
         outs_specs=[ANY] * 2,
         scratch=[
             pltpu.VMEM((4, rows_dev, 2 * piece_cols), F32),

time: 33.1 us -> 33.1 us (level)
  no operation moved by 1% of the time
where the time goes in v8:
time: 33.1 us; the launch traced here: 32.9 us
  starting transfers between devices  16 us (48%)
  Pallas kernels  11.1 us (34%)
  waiting for transfers between devices  5.19 us (16%)
  between operations  0.72 us (2%)
    ppermute x15, starting transfers between devices, swap(): return lax.ppermute(value, AXES, pairs)  16 us
    pallas_call x9, Pallas kernels, call(): pl.pallas_call(kernel, out_shape=out_shape, in_specs=specs or [VM] * len(...  11.1 us
    ppermute x15, waiting for transfers between devices, swap(): return lax.ppermute(value, AXES, pairs)  5.19 us
  transfers between devices with their start and end apart: 15, of which 8 were waited for; matrix products, arithmetic and copies ran while one was open for 0% of the time, Pallas kernels for 23%

profile of v8, /device:TPU:0, one launch (start us, length us, event | category | flops | bytes accessed | tf_op | source)
XLA Modules:
  0.0 32.9 jit_solution(6490516611691086201)
XLA Ops:
  0.6 1.7 %shard_map.95 = (bf16[40,1024]{1,0:T(8,128)(2,1)S(1)}, bf16[40,1024]{1,0:T(8,128)(2,1)S(1)}, s32[8,128]{1,0:T(8,128)S(1)}) custom-call(s32[1,1,2,5]{3,2,1,0:T(2,128)} %tok_hbm.1, s32[1,1,2]{2,1,0:T(1,128)} %cnt_hbm.1, bf16[1,1,2,5]{3,2,1,0:T(2,128)(2,1)} %weight_hbm.1, bf16[1,64,7168]{2,1,0:T(8,128)(2,1)} %rows_hbm.1, bf16[1,1,20,256]{3,2,1,0:T(8,128)(2,1)} %hidden_hbm.1), custom_call_target="tpu_custom_call" | custom-call | bytes 917504 | tf_op jit(solution)/shard_map/pallas_call | solution.py:336
  2.4 4.0 %collective-permute-start.2 = (bf16[40,1024]{1,0:T(8,128)(2,1)S(1)}, bf16[40,1024]{1,0:T(8,128)(2,1)S(1)}, u32[]{:S(2)}, u32[]{:S(2)}) collective-permute-start(bf16[40,1024]{1,0:T(8,128)(2,1)S(1)} %get-tuple-element.22), channel_id=1, source_target_pairs={{0,24},{1,25},{2,26},{3,27},{4,28},{5,29},{6,30},{7,31},{8,16},{9,... | collective-permute-start | bytes 245768 | tf_op jit(solution)/shard_map/ppermute | solution.py:361
  6.3 0.5 %collective-permute-start.1 = (bf16[40,1024]{1,0:T(8,128)(2,1)S(1)}, bf16[40,1024]{1,0:T(8,128)(2,1)S(1)}, u32[]{:S(2)}, u32[]{:S(2)}) collective-permute-start(bf16[40,1024]{1,0:T(8,128)(2,1)S(1)} %get-tuple-element.22), channel_id=1, source_target_pairs={{0,16},{1,17},{2,18},{3,19},{4,20},{5,21},{6,22},{7,23},{8,24},{9,... | collective-permute-start | bytes 245768 | tf_op jit(solution)/shard_map/ppermute | solution.py:361
  6.8 0.1 collective-permute-start
  7.0 3.2 %shard_map.96 = (bf16[1,256,7168]{2,1,0:T(8,128)(2,1)S(1)}, bf16[1,7168,256]{2,1,0:T(8,128)(2,1)S(1)}, bf16[1,1,20,256]{3,2,1,0:T(8,128)(2,1)S(1)}) custom-call(bf16[1,256,7168]{2,1,0:T(8,128)(2,1)} %down_hbm.1, bf16[1,7168,256]{2,1,0:T(8,128)(2,1)} %up_hbm.1, bf16[1,1,20,256]{3,2,1,0:T(8,128)(2,1)} %gate_hbm.1, bf16[40,1024]{1,0:T(8,128)(2,1)S(1)} %get-tuple-element.21.after.own), custom_call_target="tpu_custom_call" | custom-call | bytes 14680064 | tf_op jit(solution)/shard_map/pallas_call | solution.py:336
  10.2 0.0 collective-permute-done.2.from_xy
  10.2 0.6 %collective-permute-done.1.from_y = bf16[40,1024]{1,0:T(8,128)(2,1)S(1)} collective-permute-done((bf16[40,1024]{1,0:T(8,128)(2,1)S(1)}, bf16[40,1024]{1,0:T(8,128)(2,1)S(1)}, u32[]{:S(2)}, u32[]{:S(2)}) %collective-permute-start.1) | collective-permute-done | bytes 81952 | tf_op jit(solution)/shard_map/ppermute | solution.py:361
  10.8 0.5 %collective-permute-done.from_x = bf16[40,1024]{1,0:T(8,128)(2,1)S(1)} collective-permute-done((bf16[40,1024]{1,0:T(8,128)(2,1)S(1)}, bf16[40,1024]{1,0:T(8,128)(2,1)S(1)}, u32[]{:S(2)}, u32[]{:S(2)}) %collective-permute-start) | collective-permute-done | bytes 81952 | tf_op jit(solution)/shard_map/ppermute | solution.py:361
  11.3 0.3 %shard_map.97 = (bf16[40,1024]{1,0:T(8,128)(2,1)S(1)}, bf16[40,1024]{1,0:T(8,128)(2,1)S(1)}, bf16[40,1024]{1,0:T(8,128)(2,1)S(1)}, bf16[40,1024]{1,0:T(8,128)(2,1)S(1)}) custom-call(bf16[40,1024]{1,0:T(8,128)(2,1)S(1)} %get-tuple-element.21.after.own, bf16[40,1024]{1,0:T(8,128)(2,1)S(1)} %collective-permute-done.from_x, ...), custom_call_target="tpu_custom_call" | custom-call | bytes 286720 | tf_op jit(solution)/shard_map/pallas_call | solution.py:336
  11.6 2.6 %collective-permute-start.3 = (bf16[40,1024]{1,0:T(8,128)(2,1)S(1)}, bf16[40,1024]{1,0:T(8,128)(2,1)S(1)}, u32[]{:S(2)}, u32[]{:S(2)}) collective-permute-start(bf16[40,1024]{1,0:T(8,128)(2,1)S(1)} %get-tuple-element.25), channel_id=1, source_target_pairs={{0,4},{1,5},{2,6},{3,7},{4,0},{5,1},{6,2},{7,3},{8,12},{9,13},{10,... | collective-permute-start | bytes 245768 | tf_op jit(solution)/shard_map/ppermute | solution.py:361
  14.3 1.4 %collective-permute-start.4 = (bf16[40,1024]{1,0:T(8,128)(2,1)S(1)}, bf16[40,1024]{1,0:T(8,128)(2,1)S(1)}, u32[]{:S(2)}, u32[]{:S(2)}) collective-permute-start(bf16[40,1024]{1,0:T(8,128)(2,1)S(1)} %get-tuple-element.26), channel_id=1, source_target_pairs={{0,6},{1,7},{2,4},{3,5},{4,2},{5,3},{6,0},{7,1},{8,14},{9,15},{10,... | collective-permute-start | bytes 245768 | tf_op jit(solution)/shard_map/ppermute | solution.py:361
  15.6 0.2 collective-permute-start.5
  15.9 3.0 %shard_map.98 = (bf16[40,896]{1,0:T(8,128)(2,1)S(1)}, bf16[40,896]{1,0:T(8,128)(2,1)S(1)}, bf16[80,896]{1,0:T(8,128)(2,1)S(1)}) custom-call(bf16[40,1024]{1,0:T(8,128)(2,1)S(1)} %get-tuple-element.21.after.own, bf16[40,1024]{1,0:T(8,128)(2,1)S(1)} %collective-permute-done.from_x, bf16[40,1024]{1,0:T(8,128)(2,1)S(1)} %collective-permute-done.1.from_y, ...), custom_call_target="tpu_custom_call" | custom-call | flops 234881024 | bytes 7340032 | tf_op jit(solution)/shard_map/pallas_call | solution.py:336
  18.9 1.1 %collective-permute-start.13 = (bf16[80,896]{1,0:T(8,128)(2,1)S(1)}, bf16[80,896]{1,0:T(8,128)(2,1)S(1)}, u32[]{:S(2)}, u32[]{:S(2)}) collective-permute-start(bf16[80,896]{1,0:T(8,128)(2,1)S(1)} %get-tuple-element.37), channel_id=1, source_target_pairs={{0,8},{1,9},{2,10},{3,11},{4,12},{5,13},{6,14},{7,15},{8,0},{9,1},... | collective-permute-start | bytes 430088 | tf_op jit(solution)/shard_map/ppermute | solution.py:361
  20.0 0.0 collective-permute-start.6
  20.0 0.0 collective-permute-done.3.from_2
  20.0 0.5 %collective-permute-start.7 = (bf16[40,1024]{1,0:T(8,128)(2,1)S(1)}, bf16[40,1024]{1,0:T(8,128)(2,1)S(1)}, u32[]{:S(2)}, u32[]{:S(2)}) collective-permute-start(bf16[40,1024]{1,0:T(8,128)(2,1)S(1)} %collective-permute-done.3.from_2), channel_id=1, source_target_pairs={{0,1},{1,0},{2,3},{3,2},{4,5},{5,4},{6,7},{7,6},{8,9},{9,8},{10,11... | collective-permute-start | bytes 245768 | tf_op jit(solution)/shard_map/ppermute | solution.py:361
  20.5 0.4 %collective-permute-done.4.from_3 = bf16[40,1024]{1,0:T(8,128)(2,1)S(1)} collective-permute-done((bf16[40,1024]{1,0:T(8,128)(2,1)S(1)}, bf16[40,1024]{1,0:T(8,128)(2,1)S(1)}, u32[]{:S(2)}, u32[]{:S(2)}) %collective-permute-start.4) | collective-permute-done | bytes 81952 | tf_op jit(solution)/shard_map/ppermute | solution.py:361
  20.9 0.0 collective-permute-start.8
  20.9 0.1 collective-permute-done.5.from_1
  21.0 0.4 %collective-permute-start.9 = (bf16[40,1024]{1,0:T(8,128)(2,1)S(1)}, bf16[40,1024]{1,0:T(8,128)(2,1)S(1)}, u32[]{:S(2)}, u32[]{:S(2)}) collective-permute-start(bf16[40,1024]{1,0:T(8,128)(2,1)S(1)} %collective-permute-done.5.from_1), channel_id=1, source_target_pairs={{0,1},{1,0},{2,3},{3,2},{4,5},{5,4},{6,7},{7,6},{8,9},{9,8},{10,11... | collective-permute-start | bytes 245768 | tf_op jit(solution)/shard_map/ppermute | solution.py:361
  21.4 0.0 collective-permute-done.6.swap_own
  21.4 0.0 collective-permute-done.7.swap_2
  21.4 0.6 %shard_map.99.early = f32[256,896]{1,0:T(8,128)S(1)} custom-call(bf16[40,1024]{1,0:T(8,128)(2,1)S(1)} %get-tuple-element.24.own, bf16[40,1024]{1,0:T(8,128)(2,1)S(1)} %collective-permute-done.3.from_2, bf16[40,1024]{1,0:T(8,128)(2,1)S(1)} %collective-permute-done.4.from_3, bf16[40,1024]{1,0:T(8,128)(2,1)S(1)} %collective-permute-done.5.from_1, ...), custom_call_target="tpu_custom_call" | custom-call | bytes 1048576 | tf_op jit(solution)/shard_map/pallas_call | solution.py:336
  22.0 0.2 collective-permute-done.8.swap_3
  22.2 0.2 collective-permute-done.9.swap_1
  22.3 0.5 %shard_map.100 = (bf16[32,1792]{1,0:T(8,128)(2,1)S(1)}, bf16[32,1792]{1,0:T(8,128)(2,1)S(1)}, bf16[32,1792]{1,0:T(8,128)(2,1)S(1)}, bf16[32,1792]{1,0:T(8,128)(2,1)S(1)}) custom-call(f32[256,896]{1,0:T(8,128)S(1)} %shard_map.99.early, bf16[40,1024]{1,0:T(8,128)(2,1)S(1)} %collective-permute-done.8.swap_3, bf16[40,1024]{1,0:T(8,128)(2,1)S(1)} %collective-permute-done.9.swap_1), custom_call_target="tpu_custom_call" | custom-call | bytes 1048576 | tf_op jit(solution)/shard_map/pallas_call | solution.py:336
  22.9 2.1 %collective-permute-start.10 = (bf16[32,1792]{1,0:T(8,128)(2,1)S(1)}, bf16[32,1792]{1,0:T(8,128)(2,1)S(1)}, u32[]{:S(2)}, u32[]{:S(2)}) collective-permute-start(bf16[32,1792]{1,0:T(8,128)(2,1)S(1)} %get-tuple-element.32), channel_id=1, source_target_pairs={{0,10},{1,11},{2,8},{3,9},{4,14},{5,15},{6,12},{7,13},{8,2},{9,3},... | collective-permute-start | bytes 344072 | tf_op jit(solution)/shard_map/ppermute | solution.py:361
  25.0 0.5 %collective-permute-start.11 = (bf16[32,1792]{1,0:T(8,128)(2,1)S(1)}, bf16[32,1792]{1,0:T(8,128)(2,1)S(1)}, u32[]{:S(2)}, u32[]{:S(2)}) collective-permute-start(bf16[32,1792]{1,0:T(8,128)(2,1)S(1)} %get-tuple-element.33), channel_id=1, source_target_pairs={{0,2},{1,3},{2,0},{3,1},{4,6},{5,7},{6,4},{7,5},{8,10},{9,11},{10,... | collective-permute-start | bytes 344072 | tf_op jit(solution)/shard_map/ppermute | solution.py:361
  25.5 0.9 %collective-permute-start.12 = (bf16[32,1792]{1,0:T(8,128)(2,1)S(1)}, bf16[32,1792]{1,0:T(8,128)(2,1)S(1)}, u32[]{:S(2)}, u32[]{:S(2)}) collective-permute-start(bf16[32,1792]{1,0:T(8,128)(2,1)S(1)} %get-tuple-element.34), channel_id=1, source_target_pairs={{0,8},{1,9},{2,10},{3,11},{4,12},{5,13},{6,14},{7,15},{8,0},{9,1},... | collective-permute-start | bytes 344072 | tf_op jit(solution)/shard_map/ppermute | solution.py:361
  26.4 0.0 collective-permute-done.13.from_x
  26.5 1.6 %collective-permute-start.14 = (bf16[40,896]{1,0:T(8,128)(2,1)S(1)}, bf16[40,896]{1,0:T(8,128)(2,1)S(1)}, u32[]{:S(2)}, u32[]{:S(2)}) collective-permute-start(bf16[40,896]{1,0:T(8,128)(2,1)S(1)} %get-tuple-element.39), channel_id=1, source_target_pairs={{0,16},{1,17},{2,18},{3,19},{4,20},{5,21},{6,22},{7,23},{8,24},{9,... | collective-permute-start | bytes 215048 | tf_op jit(solution)/shard_map/ppermute | solution.py:361
  28.0 2.8 %collective-permute-done.14.far = bf16[40,896]{1,0:T(8,128)(2,1)S(1)} collective-permute-done((bf16[40,896]{1,0:T(8,128)(2,1)S(1)}, bf16[40,896]{1,0:T(8,128)(2,1)S(1)}, u32[]{:S(2)}, u32[]{:S(2)}) %collective-permute-start.14) | collective-permute-done | bytes 71712 | tf_op jit(solution)/shard_map/ppermute | solution.py:361
  30.9 0.4 %shard_map.102.summed = bf16[1,64,7168]{2,1,0:T(8,128)(2,1)S(1)} custom-call(s32[8,128]{1,0:T(8,128)S(1)} %get-tuple-element.35.names, bf16[40,896]{1,0:T(8,128)(2,1)S(1)} %get-tuple-element.38.near, bf16[40,896]{1,0:T(8,128)(2,1)S(1)} %collective-permute-done.14.far), custom_call_target="tpu_custom_call" | custom-call | bytes 2097152 | tf_op jit(solution)/shard_map/pallas_call | solution.py:336
  31.2 0.0 collective-permute-done.10.from_xz
  31.3 0.0 collective-permute-done.11.from_z
  31.3 0.4 %collective-permute-done.12.from_x = bf16[32,1792]{1,0:T(8,128)(2,1)S(1)} collective-permute-done((bf16[32,1792]{1,0:T(8,128)(2,1)S(1)}, bf16[32,1792]{1,0:T(8,128)(2,1)S(1)}, u32[]{:S(2)}, u32[]{:S(2)}) %collective-permute-start.12) | collective-permute-done | bytes 114720 | tf_op jit(solution)/shard_map/ppermute | solution.py:361
  31.7 1.3 %shard_map.103 = (bf16[1,64,7168]{2,1,0:T(8,128)(2,1)}, f32[1,32,7168]{2,1,0:T(8,128)}) custom-call(bf16[32,1792]{1,0:T(8,128)(2,1)S(1)} %get-tuple-element.31.own, bf16[32,1792]{1,0:T(8,128)(2,1)S(1)} %collective-permute-done.10.from_xz, bf16[32,1792]{1,0:T(8,128)(2,1)S(1)} %collective-permute-done.11.from_z, ...), custom_call_target="tpu_custom_call" | custom-call | bytes 1048576 | tf_op jit(solution)/shard_map/pallas_call | solution.py:336
  (1 shorter events, 0.0 us)
Async XLA Ops:
  2.4 7.8 %collective-permute-start.2 = (bf16[40,1024]{1,0:T(8,128)(2,1)S(1)}, bf16[40,1024]{1,0:T(8,128)(2,1)S(1)}, u32[]{:S(2)}, u32[]{:S(2)}) collective-permute-start(bf16[40,1024]{1,0:T(8,128)(2,1)S(1)} %get-tuple-element.22), channel_id=1, source_target_pairs={{0,24},{1,25},{2,26},{3,27},{4,28},{5,29},{6,30},{7,31},{8,16},{9,... | collective-permute-start | bytes 245768 | tf_op jit(solution)/shard_map/ppermute | solution.py:361
  6.3 4.4 %collective-permute-start.1 = (bf16[40,1024]{1,0:T(8,128)(2,1)S(1)}, bf16[40,1024]{1,0:T(8,128)(2,1)S(1)}, u32[]{:S(2)}, u32[]{:S(2)}) collective-permute-start(bf16[40,1024]{1,0:T(8,128)(2,1)S(1)} %get-tuple-element.22), channel_id=1, source_target_pairs={{0,16},{1,17},{2,18},{3,19},{4,20},{5,21},{6,22},{7,23},{8,24},{9,... | collective-permute-start | bytes 245768 | tf_op jit(solution)/shard_map/ppermute | solution.py:361
  6.8 4.4 %collective-permute-start = (bf16[40,1024]{1,0:T(8,128)(2,1)S(1)}, bf16[40,1024]{1,0:T(8,128)(2,1)S(1)}, u32[]{:S(2)}, u32[]{:S(2)}) collective-permute-start(bf16[40,1024]{1,0:T(8,128)(2,1)S(1)} %get-tuple-element.21.after.own), channel_id=1, source_target_pairs={{0,8},{1,9},{2,10},{3,11},{4,12},{5,13},{6,14},{7,15},{8,0},{9,1},... | collective-permute-start | bytes 245768 | tf_op jit(solution)/shard_map/ppermute | solution.py:361
  11.6 8.3 %collective-permute-start.3 = (bf16[40,1024]{1,0:T(8,128)(2,1)S(1)}, bf16[40,1024]{1,0:T(8,128)(2,1)S(1)}, u32[]{:S(2)}, u32[]{:S(2)}) collective-permute-start(bf16[40,1024]{1,0:T(8,128)(2,1)S(1)} %get-tuple-element.25), channel_id=1, source_target_pairs={{0,4},{1,5},{2,6},{3,7},{4,0},{5,1},{6,2},{7,3},{8,12},{9,13},{10,... | collective-permute-start | bytes 245768 | tf_op jit(solution)/shard_map/ppermute | solution.py:361
  14.3 6.6 %collective-permute-start.4 = (bf16[40,1024]{1,0:T(8,128)(2,1)S(1)}, bf16[40,1024]{1,0:T(8,128)(2,1)S(1)}, u32[]{:S(2)}, u32[]{:S(2)}) collective-permute-start(bf16[40,1024]{1,0:T(8,128)(2,1)S(1)} %get-tuple-element.26), channel_id=1, source_target_pairs={{0,6},{1,7},{2,4},{3,5},{4,2},{5,3},{6,0},{7,1},{8,14},{9,15},{10,... | collective-permute-start | bytes 245768 | tf_op jit(solution)/shard_map/ppermute | solution.py:361
  15.6 5.3 %collective-permute-start.5 = (bf16[40,1024]{1,0:T(8,128)(2,1)S(1)}, bf16[40,1024]{1,0:T(8,128)(2,1)S(1)}, u32[]{:S(2)}, u32[]{:S(2)}) collective-permute-start(bf16[40,1024]{1,0:T(8,128)(2,1)S(1)} %get-tuple-element.27), channel_id=1, source_target_pairs={{0,2},{1,3},{2,0},{3,1},{4,6},{5,7},{6,4},{7,5},{8,10},{9,11},{10,... | collective-permute-start | bytes 245768 | tf_op jit(solution)/shard_map/ppermute | solution.py:361
  18.9 7.5 %collective-permute-start.13 = (bf16[80,896]{1,0:T(8,128)(2,1)S(1)}, bf16[80,896]{1,0:T(8,128)(2,1)S(1)}, u32[]{:S(2)}, u32[]{:S(2)}) collective-permute-start(bf16[80,896]{1,0:T(8,128)(2,1)S(1)} %get-tuple-element.37), channel_id=1, source_target_pairs={{0,8},{1,9},{2,10},{3,11},{4,12},{5,13},{6,14},{7,15},{8,0},{9,1},... | collective-permute-start | bytes 430088 | tf_op jit(solution)/shard_map/ppermute | solution.py:361
  20.0 1.5 %collective-permute-start.6 = (bf16[40,1024]{1,0:T(8,128)(2,1)S(1)}, bf16[40,1024]{1,0:T(8,128)(2,1)S(1)}, u32[]{:S(2)}, u32[]{:S(2)}) collective-permute-start(bf16[40,1024]{1,0:T(8,128)(2,1)S(1)} %get-tuple-element.24.own), channel_id=1, source_target_pairs={{0,1},{1,0},{2,3},{3,2},{4,5},{5,4},{6,7},{7,6},{8,9},{9,8},{10,11... | collective-permute-start | bytes 245768 | tf_op jit(solution)/shard_map/ppermute | solution.py:361
  20.0 1.4 %collective-permute-start.7 = (bf16[40,1024]{1,0:T(8,128)(2,1)S(1)}, bf16[40,1024]{1,0:T(8,128)(2,1)S(1)}, u32[]{:S(2)}, u32[]{:S(2)}) collective-permute-start(bf16[40,1024]{1,0:T(8,128)(2,1)S(1)} %collective-permute-done.3.from_2), channel_id=1, source_target_pairs={{0,1},{1,0},{2,3},{3,2},{4,5},{5,4},{6,7},{7,6},{8,9},{9,8},{10,11... | collective-permute-start | bytes 245768 | tf_op jit(solution)/shard_map/ppermute | solution.py:361
  20.9 1.3 %collective-permute-start.8 = (bf16[40,1024]{1,0:T(8,128)(2,1)S(1)}, bf16[40,1024]{1,0:T(8,128)(2,1)S(1)}, u32[]{:S(2)}, u32[]{:S(2)}) collective-permute-start(bf16[40,1024]{1,0:T(8,128)(2,1)S(1)} %collective-permute-done.4.from_3), channel_id=1, source_target_pairs={{0,1},{1,0},{2,3},{3,2},{4,5},{5,4},{6,7},{7,6},{8,9},{9,8},{10,11... | collective-permute-start | bytes 245768 | tf_op jit(solution)/shard_map/ppermute | solution.py:361
  21.0 1.4 %collective-permute-start.9 = (bf16[40,1024]{1,0:T(8,128)(2,1)S(1)}, bf16[40,1024]{1,0:T(8,128)(2,1)S(1)}, u32[]{:S(2)}, u32[]{:S(2)}) collective-permute-start(bf16[40,1024]{1,0:T(8,128)(2,1)S(1)} %collective-permute-done.5.from_1), channel_id=1, source_target_pairs={{0,1},{1,0},{2,3},{3,2},{4,5},{5,4},{6,7},{7,6},{8,9},{9,8},{10,11... | collective-permute-start | bytes 245768 | tf_op jit(solution)/shard_map/ppermute | solution.py:361
  22.9 8.4 %collective-permute-start.10 = (bf16[32,1792]{1,0:T(8,128)(2,1)S(1)}, bf16[32,1792]{1,0:T(8,128)(2,1)S(1)}, u32[]{:S(2)}, u32[]{:S(2)}) collective-permute-start(bf16[32,1792]{1,0:T(8,128)(2,1)S(1)} %get-tuple-element.32), channel_id=1, source_target_pairs={{0,10},{1,11},{2,8},{3,9},{4,14},{5,15},{6,12},{7,13},{8,2},{9,3},... | collective-permute-start | bytes 344072 | tf_op jit(solution)/shard_map/ppermute | solution.py:361
  25.0 6.3 %collective-permute-start.11 = (bf16[32,1792]{1,0:T(8,128)(2,1)S(1)}, bf16[32,1792]{1,0:T(8,128)(2,1)S(1)}, u32[]{:S(2)}, u32[]{:S(2)}) collective-permute-start(bf16[32,1792]{1,0:T(8,128)(2,1)S(1)} %get-tuple-element.33), channel_id=1, source_target_pairs={{0,2},{1,3},{2,0},{3,1},{4,6},{5,7},{6,4},{7,5},{8,10},{9,11},{10,... | collective-permute-start | bytes 344072 | tf_op jit(solution)/shard_map/ppermute | solution.py:361
  25.5 6.2 %collective-permute-start.12 = (bf16[32,1792]{1,0:T(8,128)(2,1)S(1)}, bf16[32,1792]{1,0:T(8,128)(2,1)S(1)}, u32[]{:S(2)}, u32[]{:S(2)}) collective-permute-start(bf16[32,1792]{1,0:T(8,128)(2,1)S(1)} %get-tuple-element.34), channel_id=1, source_target_pairs={{0,8},{1,9},{2,10},{3,11},{4,12},{5,13},{6,14},{7,15},{8,0},{9,1},... | collective-permute-start | bytes 344072 | tf_op jit(solution)/shard_map/ppermute | solution.py:361
  26.5 4.4 %collective-permute-start.14 = (bf16[40,896]{1,0:T(8,128)(2,1)S(1)}, bf16[40,896]{1,0:T(8,128)(2,1)S(1)}, u32[]{:S(2)}, u32[]{:S(2)}) collective-permute-start(bf16[40,896]{1,0:T(8,128)(2,1)S(1)} %get-tuple-element.39), channel_id=1, source_target_pairs={{0,16},{1,17},{2,18},{3,19},{4,20},{5,21},{6,22},{7,23},{8,24},{9,... | collective-permute-start | bytes 215048 | tf_op jit(solution)/shard_map/ppermute | solution.py:361
